TPU v7x, 32 devices: a whole 2x2x4 slice. The times are simulated.
32 devices in a mesh: fsdp: 2 (over x), dp: 16 (over z, y, core).
Axes of the slice: x: 2, y: 2, z: 4, core: 2. Of those that a mesh axis runs over, the one named last changes fastest.
Arguments:
- tokens: bfloat16 [2, 16, 1024, 768], P('fsdp', 'dp'), may hold values from -6 to 6
- live: int32 [2, 16], P('fsdp', 'dp'), may hold values from 0 to 1, as said below
- norm_gain: bfloat16 [768], P('fsdp'), may hold values from 0.5 to 1.5
- w_in: bfloat16 [768, 3352], P('fsdp'), may hold values from -0.21875 to 0.21875
- conv_weight: bfloat16 [1792, 4], P('fsdp'), may hold values from -3 to 3
- conv_bias: bfloat16 [1792], P('fsdp'), may hold values from -3 to 3
- dt_bias: bfloat16 [24], P('fsdp'), may hold values from -4 to 0
- a_log: bfloat16 [24], P('fsdp'), may hold values from -3 to 1
- d_skip: bfloat16 [24], P('fsdp'), may hold values from 0.5 to 1.5
- inner_gain: bfloat16 [1536], P('fsdp'), may hold values from 0.5 to 1.5
- w_out: bfloat16 [1536, 768], P('fsdp'), may hold values from -0.15625 to 0.15625
- cotangent: bfloat16 [2, 16, 1024, 768], P('fsdp', 'dp'), may hold values from -6 to 6
Outputs:
- block_out: bfloat16 [2, 16, 1024, 768], P('fsdp', 'dp')
- input_grad: float32 [2, 16, 1024, 768], P('fsdp', 'dp')
- norm_gain_grad: float32 [768], P('fsdp')
- w_in_grad: float32 [768, 3352], P('fsdp')
- conv_weight_grad: float32 [1792, 4], P('fsdp')
- conv_bias_grad: float32 [1792], P('fsdp')
- dt_bias_grad: float32 [24], P('fsdp')
- a_log_grad: float32 [24], P('fsdp')
- d_skip_grad: float32 [24], P('fsdp')
- inner_gain_grad: float32 [1536], P('fsdp')
- w_out_grad: float32 [1536, 768], P('fsdp')
Inputs may be any that keep to these rules, and one draw needn't show every extreme that they name: `live`: 1 marks a device that holds a sequence; some devices hold none.
All inputs are finite; a program needn't handle non-finite values.
Results may differ from a plain program's by a relative error of at most 0.0097.
Values may be sent and summed in bfloat16 or wider, within the bound.
No kernel may reach another device: no remote copies, remote signals or barrier semaphores. Data moves between devices by JAX's collectives and lax.ppermute only.
A program may use at most 192 MiB of HBM per device.

v0:
```python
import functools
import math

import jax
import jax.numpy as jnp
from jax import lax
from jax.experimental import pallas as pl
from jax.experimental.pallas import tpu as pltpu
from jax.sharding import PartitionSpec as P

EPSILON = 1e-05
LOG2E = math.log2(math.e)
SPAN = 256
STRETCH = 128
GROUP = 8
TILE = 256
LANES = 128
SPARE = 256
TILES_ABREAST = 7
HEADS_ABREAST = 2
HEAD_RANGES = ((0, 16), (16, 8))
VMEM_LIMIT = 60 * 1024 * 1024

F32 = jnp.float32
BF16 = jnp.bfloat16


def mul_nn(a, b):
    return lax.dot_general(a, b, (((1,), (0,)), ((), ())), preferred_element_type=F32)


def mul_nt(a, b):
    return lax.dot_general(a, b, (((1,), (1,)), ((), ())), preferred_element_type=F32)


def mul_tn(a, b):
    return lax.dot_general(a, b, (((0,), (0,)), ((), ())), preferred_element_type=F32)


def triangle(size, keep):
    rows = lax.broadcasted_iota(jnp.int32, (size, size), 0)
    cols = lax.broadcasted_iota(jnp.int32, (size, size), 1)
    return keep(rows, cols)


def lane_sums(values, matrix):
    high = values.astype(BF16)
    rest = values - high.astype(F32)
    middle = rest.astype(BF16)
    low = (rest - middle.astype(F32)).astype(BF16)
    return mul_nn(high, matrix) + mul_nn(middle, matrix) + mul_nn(low, matrix)


def as_columns(rows):
    heads, span = rows.shape
    return jnp.concatenate([rows, jnp.zeros((LANES - heads, span), F32)], axis=0).T


def fold(block):
    total = block[:, :LANES]
    for first in range(LANES, block.shape[1], LANES):
        total = total + block[:, first : first + LANES]
    return total


def eighths(block):
    return block.reshape(block.shape[0] // 8, 8, block.shape[1]).sum(axis=0)


def softplus(v):
    return jnp.maximum(v, 0.0) + jnp.log1p(jnp.exp(-jnp.abs(v)))


def sigmoid(v):
    return 0.5 * jnp.tanh(0.5 * v) + 0.5


def decays(step, rate2):
    span = step.shape[1]
    upper = triangle(span, lambda r, c: r <= c).astype(BF16)
    cum = lane_sums(step * rate2, upper)
    total = cum[:, span - 1 : span]
    return cum, jnp.exp2(total - cum), jnp.exp2(cum), jnp.exp2(total)


def piece_copies(places_ref, lengths, pieces, whole_ref, sems):
    copies = []
    for k, piece in enumerate(pieces):
        rows, columns = lengths[k], piece.shape[1]
        target = whole_ref.at[
            pl.ds(pl.multiple_of(places_ref[2 * k], 16), rows),
            pl.ds(pl.multiple_of(places_ref[2 * k + 1], LANES), columns),
        ]
        copies.append(pltpu.make_async_copy(piece.at[pl.ds(0, rows), :], target, sems.at[k]))
    return copies


def forward_body(sizes, lengths, places_ref, tokens_ref, gain_ref, raw_weight_ref, taps_ref, heads_ref, *refs):
    n_pieces = len(lengths)
    pieces, refs = refs[:n_pieces], refs[n_pieces:]
    (
        normed_ref,
        mixed_ref,
        active_ref,
        raw_ref,
        states_ref,
        gate_ref,
        scanned_ref,
        weight_ref,
        weight,
        state,
        extended,
        carried,
        scaled,
        update,
        cum_s,
        step_s,
        factor_s,
        ec_s,
        total_s,
        sems,
    ) = refs
    inner, conv, heads, state_dim = sizes
    width = inner // heads
    span = tokens_ref.shape[0]
    stretch = min(STRETCH, span)
    copies = piece_copies(places_ref, lengths, pieces, weight, sems)
    kept = pltpu.make_async_copy(weight, weight_ref, sems.at[n_pieces])

    @pl.when(pl.program_id(0) == 0)
    def _():
        for copy in copies:
            copy.start()
        state[...] = jnp.zeros_like(state)
        extended[:, span:, :] = jnp.zeros((conv // LANES, 8, LANES), F32)

    u = tokens_ref[...].astype(F32)
    normed = u * lax.rsqrt(jnp.mean(u * u, axis=1, keepdims=True) + EPSILON) * gain_ref[...]
    normed = normed.astype(BF16)
    normed_ref[...] = normed

    @pl.when(pl.program_id(0) == 0)
    def _():
        for copy in copies:
            copy.wait()
        steps = raw_weight_ref.shape[0]
        weight[inner + conv : inner + conv + steps, :] = raw_weight_ref[...]
        weight[inner + conv + steps :, :] = jnp.zeros((SPARE - steps, weight.shape[1]), BF16)
        kept.start()

    @pl.loop(0, inner // TILE, unroll=6)
    def _(i):
        rows = pl.ds(pl.multiple_of(i * TILE, TILE), TILE)
        gate_ref[rows, :] = mul_nt(weight[rows, :], normed)

    @pl.loop(0, conv // TILE, unroll=TILES_ABREAST)
    def _(i):
        first = pl.multiple_of(i * TILE, TILE)
        wide = mul_nt(normed, weight[pl.ds(pl.multiple_of(inner + first, TILE), TILE), :])
        for k in range(TILE // LANES):
            index = i * (TILE // LANES) + k
            block = wide[:, k * LANES : (k + 1) * LANES]
            extended[index, :8, :] = extended[index, span:, :]
            extended[index, 8:, :] = block
            taps = taps_ref[index]
            summed = taps[4:5] + block * taps[3:4]
            for shift in range(1, 4):
                summed = summed + extended[index, 8 - shift : 8 - shift + span, :] * taps[3 - shift : 4 - shift]
            lanes = pl.ds(pl.multiple_of(first + k * LANES, LANES), LANES)
            mixed_ref[:, lanes] = block.astype(BF16)
            active_ref[lanes, :] = (summed * sigmoid(summed)).T.astype(BF16)

    raw = mul_nt(raw_weight_ref[...], normed)[:heads] + heads_ref[:, 0:1]
    raw_ref[...] = raw
    step_all = softplus(raw)
    rate2 = -jnp.exp(heads_ref[:, 1:2]) * LOG2E
    causal = triangle(stretch, lambda r, c: r <= c)
    for part in range(span // stretch):
        lanes = slice(part * stretch, (part + 1) * stretch)
        step = step_all[:, lanes]
        cum, factor, ec, total = decays(step, rate2)
        cum_s[...] = cum
        step_s[...] = step
        factor_s[...] = factor * step
        ec_s[...] = ec
        total_s[...] = jnp.broadcast_to(total, (heads, LANES))
        b_in = active_ref[inner : inner + state_dim, lanes]
        c_in = active_ref[inner + state_dim : inner + 2 * state_dim, lanes]
        scores = jnp.where(causal, mul_tn(b_in, c_in), 0.0)
        low_state = state[...].astype(BF16)
        states_ref[part] = low_state
        carried[...] = mul_nn(low_state, c_in)

        @pl.loop(0, heads // GROUP, unroll=HEADS_ABREAST)
        def _(group):
            eight = pl.ds(pl.multiple_of(group * GROUP, GROUP), GROUP)
            cum_g, step_g, factor_g, ec_g = cum_s[eight, :], step_s[eight, :], factor_s[eight, :], ec_s[eight, :]
            cum_c = as_columns(cum_g)
            for j in range(GROUP):
                rows = pl.ds(pl.multiple_of((group * GROUP + j) * width, width), width)
                row = slice(j, j + 1)
                values = active_ref[rows, lanes].astype(F32)
                stepped = (values * step_g[row]).astype(BF16)
                decay = jnp.exp2(jnp.minimum(cum_g[row] - cum_c[:, row], 0.0))
                weights = (scores * decay).astype(BF16)
                scanned_ref[rows, lanes] = mul_nn(stepped, weights) + ec_g[row] * carried[rows, :]
                scaled[rows, :] = (values * factor_g[row]).astype(BF16)

        update[...] = mul_nt(scaled[...], b_in)

        @pl.loop(0, heads // GROUP, unroll=HEADS_ABREAST)
        def _(group):
            eight = pl.ds(pl.multiple_of(group * GROUP, GROUP), GROUP)
            total_g = total_s[eight, :]
            for j in range(GROUP):
                rows = pl.ds(pl.multiple_of((group * GROUP + j) * width, width), width)
                state[rows, :] = total_g[j : j + 1] * state[rows, :] + update[rows, :]

    @pl.when(pl.program_id(0) == pl.num_programs(0) - 1)
    def _():
        kept.wait()


def gated_body(sizes, lengths, places_ref, skip_ref, alive_ref, cotangent_ref, inner_gain_ref, *refs):
    n_pieces = len(lengths)
    gate, scanned, values_ref = refs[:3]
    pieces, refs = refs[3 : 3 + n_pieces], refs[3 + n_pieces :]
    (
        low_mixed_ref,
        d_gate_ref,
        d_scan_ref,
        row_part_ref,
        skip_part_ref,
        gain_part_ref,
        out_weight_ref,
        out_weight,
        gated,
        d_normed,
        sems,
    ) = refs
    inner, conv, heads, state_dim = sizes
    width = inner // heads
    span = cotangent_ref.shape[0]
    copies = piece_copies(places_ref, lengths, pieces, out_weight, sems)
    kept = pltpu.make_async_copy(out_weight, out_weight_ref, sems.at[n_pieces])

    @pl.when(pl.program_id(0) == 0)
    def _():
        for copy in copies:
            copy.start()
        gain_part_ref[...] = jnp.zeros_like(gain_part_ref)

    def gated_head(h, squares):
        rows = pl.ds(pl.multiple_of(h * width, width), width)
        z = gate[rows, :]
        y = scanned[rows, :] + skip_ref[h] * values_ref[rows, :].astype(F32)
        v = y * (z * sigmoid(z))
        gated[rows, :] = v
        return squares + eighths(v * v)

    squares = lax.fori_loop(0, heads, gated_head, jnp.zeros((8, span), F32), unroll=4)
    scale = lax.rsqrt(jnp.sum(squares, axis=0, keepdims=True) / inner + EPSILON)

    @pl.when(pl.program_id(0) == 0)
    def _():
        for copy in copies:
            copy.wait()
        kept.start()

    incoming = (cotangent_ref[...].astype(F32) * alive_ref[0]).astype(BF16)

    def norm_tile(i, dots):
        rows = pl.ds(pl.multiple_of(i * TILE, TILE), TILE)
        gain = inner_gain_ref[rows, :]
        unit = gated[rows, :] * scale
        low_mixed_ref[rows, :] = (unit * gain).astype(BF16)
        d_mixed = mul_nt(out_weight[rows, :], incoming)
        gain_part_ref[rows, :] += fold(d_mixed * unit)
        d_unit = d_mixed * gain
        d_normed[rows, :] = d_unit
        return dots + eighths(d_unit * unit)

    dots = lax.fori_loop(0, inner // TILE, norm_tile, jnp.zeros((8, span), F32), unroll=3)
    mean_dot = jnp.sum(dots, axis=0, keepdims=True) / inner

    @pl.loop(0, heads // GROUP, unroll=HEADS_ABREAST)
    def _(group):
        eight = pl.ds(pl.multiple_of(group * GROUP, GROUP), GROUP)
        row_parts, skip_parts, d_gates = [], [], []
        for j in range(GROUP):
            h = group * GROUP + j
            rows = pl.ds(pl.multiple_of(h * width, width), width)
            z = gate[rows, :]
            sig = sigmoid(z)
            values = values_ref[rows, :].astype(F32)
            pure = scanned[rows, :]
            y = pure + skip_ref[h] * values
            d_gated = scale * (d_normed[rows, :] - gated[rows, :] * (scale * mean_dot))
            d_scan = (d_gated * (z * sig)).astype(BF16)
            d_scan_ref[rows, :] = d_scan
            d_gates.append(d_gated * y * (sig * (1.0 + z * (1.0 - sig))))
            if len(d_gates) * width == LANES:
                lanes = pl.ds(pl.multiple_of((h + 1) * width - LANES, LANES), LANES)
                d_gate_ref[:, lanes] = jnp.concatenate(d_gates, axis=0).T.astype(BF16)
                d_gates = []
            d_scan = d_scan.astype(F32)
            row_parts.append(jnp.sum(d_scan * pure, axis=0, keepdims=True))
            skip_parts.append(jnp.sum(d_scan * values, axis=0, keepdims=True))
        row_part_ref[eight, :] = jnp.concatenate(row_parts, axis=0)
        skip_part_ref[eight, :] = jnp.concatenate(skip_parts, axis=0)

    @pl.when(pl.program_id(0) == pl.num_programs(0) - 1)
    def _():
        kept.wait()


def backward_body(sizes, first_head, last, *refs):
    refs = list(refs)
    take = lambda n: [refs.pop(0) for _ in range(n)]
    skip_ref, active_ref, low_bc_ref = take(3)
    mixed_refs = take(2 if last else 1)
    before_refs = take(2 if last else 1)
    d_scan_ref, raw_ref, row_part_ref, states_ref, taps_ref, heads_ref = take(6)
    bc_part_ref, d_raw_before_ref, _ = take(3) if last else (None, None, None)
    d_rest_ref = take(1)[0]
    d_raw_ref, rate_part_ref, conv_part_ref = take(3)
    bc_out_ref = None if last else take(1)[0]
    (
        d_state,
        extended,
        d_extended,
        d_active,
        sums,
        from_state,
        scaled,
        d_scaled,
        d_scores,
        state_dots,
        cum_s,
        step_s,
        factor_s,
        ec_s,
        total_s,
        pair_s,
        direct_s,
        ending_s,
    ) = refs
    all_inner, conv, all_heads, state_dim = sizes
    inner, span = active_ref.shape
    width = all_inner // all_heads
    heads = inner // width
    tiles = [(ref, before, t) for ref, before in zip(mixed_refs, before_refs) for t in range(ref.shape[1] // LANES)]
    first_tiles = [first_head * width // LANES, all_inner // LANES]
    stretch = min(STRETCH, span)
    first_block = pl.program_id(0) == pl.num_programs(0) - 1

    @pl.when(pl.program_id(0) == 0)
    def _():
        d_state[...] = jnp.zeros_like(d_state)
        d_extended[:, :8, :] = jnp.zeros((len(tiles), 8, LANES), F32)
        sums[...] = jnp.zeros_like(sums)

    raw = raw_ref[...]
    step_all = softplus(raw)
    slope = sigmoid(raw)
    rate = -jnp.exp(heads_ref[first_head : first_head + heads, 1:2])
    rate2 = rate * LOG2E
    causal = triangle(stretch, lambda r, c: r <= c)
    ending = triangle(stretch, lambda r, c: r >= c).astype(BF16)
    before_it = triangle(stretch, lambda r, c: r < c).astype(BF16)
    for part in reversed(range(span // stretch)):
        lanes = slice(part * stretch, (part + 1) * stretch)
        step = step_all[:, lanes]
        cum, factor, ec, total = decays(step, rate2)
        cum_s[...] = cum
        step_s[...] = step
        factor_s[...] = factor
        ec_s[...] = ec
        total_s[...] = jnp.broadcast_to(total, (heads, LANES))
        b_in = low_bc_ref[:state_dim, lanes]
        c_in = low_bc_ref[state_dim:, lanes]
        scores = jnp.where(causal, mul_tn(b_in, c_in), 0.0)
        low_d_state = d_state[...].astype(BF16)
        from_state[...] = mul_nn(low_d_state, b_in)
        d_scores[...] = jnp.zeros_like(d_scores)

        @pl.loop(0, heads // GROUP, unroll=HEADS_ABREAST)
        def _(group):
            eight = pl.ds(pl.multiple_of(group * GROUP, GROUP), GROUP)
            cum_g, step_g, factor_g, ec_g = cum_s[eight, :], step_s[eight, :], factor_s[eight, :], ec_s[eight, :]
            cum_c = as_columns(cum_g)
            pairs, directs, endings, dots = [], [], [], []
            d_scores_g = d_scores[...]
            for j in range(GROUP):
                h = group * GROUP + j
                rows = pl.ds(pl.multiple_of(h * width, width), width)
                row = slice(j, j + 1)
                values = active_ref[rows, lanes].astype(F32)
                stepped = (values * step_g[row]).astype(BF16)
                low_d = d_scan_ref[rows, lanes]
                d_scan = low_d.astype(F32)
                decay = jnp.exp2(jnp.minimum(cum_g[row] - cum_c[:, row], 0.0))
                weights = (scores * decay).astype(BF16)
                inside = mul_nt(low_d, weights)
                d_scores_g = d_scores_g + mul_tn(stepped, low_d) * decay
                across = from_state[rows, :] * factor_g[row]
                both = inside + across
                d_active[rows, lanes] = step_g[row] * both + skip_ref[first_head + h] * d_scan
                pairs.append(jnp.sum(stepped.astype(F32) * inside, axis=0, keepdims=True))
                directs.append(jnp.sum(values * both, axis=0, keepdims=True))
                endings.append(jnp.sum(values * across, axis=0, keepdims=True))
                scaled[rows, :] = (values * (step_g[row] * factor_g[row])).astype(BF16)
                d_scaled[rows, :] = (d_scan * ec_g[row]).astype(BF16)
                dots.append(jnp.sum(d_state[rows, :] * states_ref[part, rows, :].astype(F32), axis=0, keepdims=True))
            d_scores[...] = d_scores_g
            pair_s[eight, :] = jnp.concatenate(pairs, axis=0)
            direct_s[eight, :] = jnp.concatenate(directs, axis=0)
            ending_s[eight, :] = jnp.concatenate(endings, axis=0)
            state_dots[eight, :] = jnp.concatenate(dots, axis=0)

        low_d_scores = jnp.where(causal, d_scores[...], 0.0).astype(BF16)
        low_state = states_ref[part]
        d_b = mul_tn(low_d_state, scaled[...]) + mul_nt(c_in, low_d_scores)
        d_c = mul_tn(low_state, d_scaled[...]) + mul_nn(b_in, low_d_scores)
        if last:
            d_active[inner : inner + state_dim, lanes] = d_b + bc_part_ref[:state_dim, lanes]
            d_active[inner + state_dim :, lanes] = d_c + bc_part_ref[state_dim:, lanes]
        else:
            bc_out_ref[:state_dim, lanes] = d_b
            bc_out_ref[state_dim:, lanes] = d_c
        from_state[...] = mul_nt(d_scaled[...], c_in)

        @pl.loop(0, heads // GROUP, unroll=HEADS_ABREAST)
        def _(group):
            eight = pl.ds(pl.multiple_of(group * GROUP, GROUP), GROUP)
            total_g = total_s[eight, :]
            for j in range(GROUP):
                rows = pl.ds(pl.multiple_of((group * GROUP + j) * width, width), width)
                d_state[rows, :] = total_g[j : j + 1] * d_state[rows, :] + from_state[rows, :]

        d_log = (
            lane_sums(row_part_ref[:, lanes] - pair_s[...], ending)
            + lane_sums(step * ending_s[...], before_it)
            + total * jnp.sum(state_dots[...], axis=1, keepdims=True)
        )
        rate_part_ref[:, lanes] = d_log * step * rate
        d_raw_ref[:, lanes] = (direct_s[...] + d_log * rate) * slope[:, lanes]

    for index, (mixed_ref, before_ref, tile) in enumerate(tiles):
        lanes = slice(tile * LANES, (tile + 1) * LANES)
        active_rows = slice(index * LANES, (index + 1) * LANES)
        before = before_ref[:, lanes].astype(F32)[8:]
        extended[index, :8, :] = jnp.where(first_block, 0.0, before)
        extended[index, 8:, :] = mixed_ref[:, lanes].astype(F32)
        taps = taps_ref[first_tiles[0] + index if mixed_ref is mixed_refs[0] else first_tiles[1] + tile]
        moved = [extended[index, 8 - shift : 8 - shift + span, :] for shift in range(4)]
        summed = taps[4:5] + moved[0] * taps[3:4]
        for shift in range(1, 4):
            summed = summed + moved[shift] * taps[3 - shift : 4 - shift]
        sig = sigmoid(summed)
        d_summed = d_active[active_rows, :].T * (sig * (1.0 + summed * (1.0 - sig)))
        d_extended[index, span:, :] = d_extended[index, :8, :]
        d_extended[index, :span, :] = d_summed
        d_block = d_summed * taps[3:4]
        for shift in range(1, 4):
            d_block = d_block + d_extended[index, shift : shift + span, :] * taps[3 - shift : 4 - shift]
        d_rest_ref[:, active_rows] = d_block.astype(BF16)
        for shift in range(4):
            sums[3 - shift, index] += eighths(d_summed * moved[shift])
        sums[4, index] += eighths(d_summed)

    if last:
        d_raw = jnp.concatenate([d_raw_before_ref[...], d_raw_ref[...]], axis=0)
        done = len(tiles) * LANES
        d_rest_ref[:, done : done + LANES] = as_columns(d_raw).astype(BF16)
        d_rest_ref[:, done + LANES :] = jnp.zeros((span, d_rest_ref.shape[1] - done - LANES), BF16)

    @pl.when(first_block)
    def _():
        for k in range(5):
            conv_part_ref[k] = jnp.sum(sums[k], axis=1)


def whole(shape):
    return pl.BlockSpec(shape, lambda c: (0,) * len(shape), pipeline_mode=pl.Buffered(1))


ANYWHERE = pl.BlockSpec(memory_space=pl.ANY)
SCALARS = pl.BlockSpec(memory_space=pltpu.SMEM)


def kernel_options(microseconds):
    return dict(
        compiler_params=pltpu.CompilerParams(
            dimension_semantics=("arbitrary",), vmem_limit_bytes=VMEM_LIMIT
        ),
        cost_estimate=pl.CostEstimate(
            flops=microseconds * 10**9, bytes_accessed=microseconds * 10**6, transcendentals=0
        ),
    )


def forward(sizes, places, tokens, gain, raw_weight, taps, heads_in, pieces, lengths):
    inner, conv, heads, state_dim = sizes
    length, model = tokens.shape
    span = min(SPAN, length)
    stretch = min(STRETCH, span)
    parts = span // stretch
    along = lambda rows: pl.BlockSpec((rows, span), lambda c: (0, c))
    down = lambda columns: pl.BlockSpec((span, columns), lambda c: (c, 0))
    shape = jax.ShapeDtypeStruct
    return pl.pallas_call(
        functools.partial(forward_body, sizes, tuple(lengths)),
        grid=(length // span,),
        in_specs=[
            SCALARS,
            down(model),
            whole(gain.shape),
            whole(raw_weight.shape),
            whole(taps.shape),
            whole(heads_in.shape),
        ]
        + [ANYWHERE] * len(pieces),
        out_specs=[
            down(model),
            down(conv),
            along(conv),
            along(heads),
            pl.BlockSpec((parts, inner, state_dim), lambda c: (c, 0, 0)),
            along(inner),
            along(inner),
            ANYWHERE,
        ],
        out_shape=[
            shape((length, model), BF16),
            shape((length, conv), BF16),
            shape((conv, length), BF16),
            shape((heads, length), F32),
            shape((length // stretch, inner, state_dim), BF16),
            shape((inner, length), F32),
            shape((inner, length), F32),
            shape((inner + conv + SPARE, model), BF16),
        ],
        scratch_shapes=[
            pltpu.VMEM((inner + conv + SPARE, model), BF16),
            pltpu.VMEM((inner, state_dim), F32),
            pltpu.VMEM((conv // LANES, span + 8, LANES), F32),
            pltpu.VMEM((inner, stretch), F32),
            pltpu.VMEM((inner, stretch), BF16),
            pltpu.VMEM((inner, state_dim), F32),
            pltpu.VMEM((heads, stretch), F32),
            pltpu.VMEM((heads, stretch), F32),
            pltpu.VMEM((heads, stretch), F32),
            pltpu.VMEM((heads, stretch), F32),
            pltpu.VMEM((heads, LANES), F32),
            pltpu.SemaphoreType.DMA((len(pieces) + 1,)),
        ],
        name="block_forward",
        **kernel_options(30),
    )(places, tokens, gain, raw_weight, taps, heads_in, *pieces)


def gated(sizes, places, skip, alive, cotangent, inner_gain, gate, scanned, active, pieces, lengths):
    inner, conv, heads, state_dim = sizes
    length, model = cotangent.shape
    span = min(SPAN, length)
    along = lambda rows: pl.BlockSpec((rows, span), lambda c: (0, c))
    shape = jax.ShapeDtypeStruct
    return pl.pallas_call(
        functools.partial(gated_body, sizes, tuple(lengths)),
        grid=(length // span,),
        in_specs=[
            SCALARS,
            SCALARS,
            SCALARS,
            pl.BlockSpec((span, model), lambda c: (c, 0)),
            whole(inner_gain.shape),
            along(inner),
            along(inner),
            along(inner),
        ]
        + [ANYWHERE] * len(pieces),
        out_specs=[
            along(inner),
            pl.BlockSpec((span, inner), lambda c: (c, 0)),
            along(inner),
            along(heads),
            along(heads),
            pl.BlockSpec((inner, LANES), lambda c: (0, 0)),
            ANYWHERE,
        ],
        out_shape=[
            shape((inner, length), BF16),
            shape((length, inner), BF16),
            shape((inner, length), BF16),
            shape((heads, length), F32),
            shape((heads, length), F32),
            shape((inner, LANES), F32),
            shape((inner, model), BF16),
        ],
        scratch_shapes=[
            pltpu.VMEM((inner, model), BF16),
            pltpu.VMEM((inner, span), F32),
            pltpu.VMEM((inner, span), F32),
            pltpu.SemaphoreType.DMA((len(pieces) + 1,)),
        ],
        name="block_gated",
        **kernel_options(15),
    )(places, skip, alive, cotangent, inner_gain, gate, scanned, active, *pieces)


def input_body(alive_ref, tokens_ref, cotangent_ref, gain_ref, d_gate_ref, d_rest_ref, weight_ref, grad_ref, gain_part_ref):
    @pl.when(pl.program_id(0) == 0)
    def _():
        gain_part_ref[...] = jnp.zeros_like(gain_part_ref)

    inner = d_gate_ref.shape[1]
    d_normed = mul_nn(d_gate_ref[...], weight_ref[:inner, :]) + mul_nn(d_rest_ref[...], weight_ref[inner:, :])
    u = tokens_ref[...].astype(F32)
    scale = lax.rsqrt(jnp.mean(u * u, axis=1, keepdims=True) + EPSILON)
    unit = u * scale
    gain_part_ref[...] += eighths(d_normed * unit)
    d_unit = d_normed * gain_ref[...]
    slope = scale * (d_unit - unit * jnp.mean(d_unit * unit, axis=1, keepdims=True))
    grad_ref[...] = cotangent_ref[...].astype(F32) * alive_ref[0] + slope


def input_backward(alive, tokens, cotangent, gain, d_gate, d_rest, weight):
    length, model = tokens.shape
    span = min(SPAN, length)
    down = lambda columns: pl.BlockSpec((span, columns), lambda c: (c, 0))
    shape = jax.ShapeDtypeStruct
    return pl.pallas_call(
        input_body,
        grid=(length // span,),
        in_specs=[
            SCALARS,
            down(model),
            down(model),
            whole(gain.shape),
            down(d_gate.shape[1]),
            down(d_rest.shape[1]),
            whole(weight.shape),
        ],
        out_specs=[down(model), pl.BlockSpec((8, model), lambda c: (0, 0))],
        out_shape=[shape((length, model), F32), shape((8, model), F32)],
        name="input_backward",
        **kernel_options(8),
    )(alive, tokens, cotangent, gain, d_gate, d_rest, weight)


def backward(sizes, first_head, heads, skip, active, mixed, d_scan, raw, row_part, states, taps, heads_in, earlier):
    all_inner, conv, all_heads, state_dim = sizes
    width = all_inner // all_heads
    inner = heads * width
    last = first_head + heads == all_heads
    length = active.shape[1]
    span = min(SPAN, length)
    stretch = min(STRETCH, span)
    parts = span // stretch
    blocks = length // span
    per = span // 16
    at = first_head // heads
    bc = conv - all_inner
    bc_at = all_inner // bc
    along = lambda rows, index: pl.BlockSpec((rows, span), lambda c: (index, blocks - 1 - c))
    down = lambda columns, index: pl.BlockSpec((span, columns), lambda c: (blocks - 1 - c, index))
    ahead = lambda columns, index: pl.BlockSpec(
        (16, columns), lambda c: (jnp.maximum((blocks - 1 - c) * per - 1, 0), index)
    )
    shape = jax.ShapeDtypeStruct
    tiles = (inner + (bc if last else 0)) // LANES
    share = first_head * width if last else inner
    results = pl.pallas_call(
        functools.partial(backward_body, sizes, first_head, last),
        grid=(blocks,),
        in_specs=[SCALARS, along(inner, at), along(bc, bc_at), down(inner, at)]
        + [down(bc, bc_at)] * last
        + [ahead(inner, at)]
        + [ahead(bc, bc_at)] * last
        + [
            along(inner, at),
            along(heads, at),
            along(heads, at),
            pl.BlockSpec((parts, inner, state_dim), lambda c: (blocks - 1 - c, at, 0)),
            whole(taps.shape),
            whole(heads_in.shape),
        ]
        + [along(bc, 0), along(first_head, 0), ANYWHERE] * last,
        out_specs=[down(share, 1 if last else 0)]
        + [along(heads, 0), along(heads, 0), pl.BlockSpec((5, tiles, LANES), lambda c: (0, 0, 0))]
        + [along(bc, 0)] * (not last),
        out_shape=[shape((length, 2 * share), BF16)]
        + [shape((heads, length), F32), shape((heads, length), F32), shape((5, tiles, LANES), F32)]
        + [shape((bc, length), F32)] * (not last),
        scratch_shapes=[
            pltpu.VMEM((inner, state_dim), F32),
            pltpu.VMEM((tiles, span + 8, LANES), F32),
            pltpu.VMEM((tiles, span + 8, LANES), F32),
            pltpu.VMEM((tiles * LANES, span), F32),
            pltpu.VMEM((5, tiles, 8, LANES), F32),
            pltpu.VMEM((inner, stretch), F32),
            pltpu.VMEM((inner, stretch), BF16),
            pltpu.VMEM((inner, stretch), BF16),
            pltpu.VMEM((stretch, stretch), F32),
            pltpu.VMEM((heads, state_dim), F32),
            pltpu.VMEM((heads, stretch), F32),
            pltpu.VMEM((heads, stretch), F32),
            pltpu.VMEM((heads, stretch), F32),
            pltpu.VMEM((heads, stretch), F32),
            pltpu.VMEM((heads, LANES), F32),
            pltpu.VMEM((heads, stretch), F32),
            pltpu.VMEM((heads, stretch), F32),
            pltpu.VMEM((heads, stretch), F32),
        ],
        input_output_aliases={3 + 2 * 2 + 6 + 2: 0} if last else {},
        name="block_backward",
        **kernel_options(4 + heads),
    )(
        skip,
        active,
        active,
        *[mixed] * (2 + 2 * last),
        d_scan,
        raw,
        row_part,
        states,
        taps,
        heads_in,
        *((earlier[-1], earlier[1], earlier[0]) if last else ()),
    )
    return results


def powers_of_two(size):
    bits, bit = [], 1
    while bit < size:
        bits.append(bit)
        bit *= 2
    return bits if bit == size else None


def swap(block, axis, bit):
    pairs = [(k, k ^ bit) for k in range(lax.axis_size(axis))]
    return lax.ppermute(block, axis, pairs)


def cut(block, index, pieces, axis=0):
    size = block.shape[axis] // pieces
    return lax.dynamic_slice_in_dim(block, index * size, size, axis)


def halve(block, axis, bit):
    side = (lax.axis_index(axis) // bit) % 2
    got = swap(cut(block, 1 - side, 2), axis, bit)
    return (cut(block, side, 2).astype(F32) + got.astype(F32)).astype(block.dtype)


def double(block, axis, bit):
    side = (lax.axis_index(axis) // bit) % 2
    other = swap(block, axis, bit)
    return jnp.where(
        side == 0, jnp.concatenate([block, other], axis=0), jnp.concatenate([other, block], axis=0)
    )


def pair_sum(product, core):
    return added(product(core), swap(product(1 - core).astype(BF16), "dp", 1))


def after(value, *earlier):
    return lax.optimization_barrier((value, *earlier))[0]


def added(keep, got):
    return (keep.astype(F32) + got.astype(F32)).astype(BF16)


def together(*arrays):
    return lax.optimization_barrier(arrays)


def sides(block, axis, bit):
    side = (lax.axis_index(axis) // bit) % 2
    return cut(block, side, 2), cut(block, 1 - side, 2)


def joined(block, other, side, axis=0):
    return jnp.where(
        side == 0, jnp.concatenate([block, other], axis), jnp.concatenate([other, block], axis)
    )


def pair_sum(product, core):
    return added(product(core), swap(product(1 - core).astype(BF16), "dp", 1))


def after(value, *earlier):
    return lax.optimization_barrier((value, *earlier))[0]


def added(keep, got):
    return (keep.astype(F32) + got.astype(F32)).astype(BF16)


class Chain:
    def __init__(self, keep, give, axis, bit):
        self.keep, self.give, self.axis, self.bit = keep, give, axis, bit

    def start(self):
        self.got = swap(self.give, self.axis, self.bit)
        return self.give

    def finish(self, *beside):
        return added(self.keep, after(self.got, *beside) if beside else self.got)


def halving(block, axis, bit):
    side = (lax.axis_index(axis) // bit) % 2
    return Chain(cut(block, side, 2), cut(block, 1 - side, 2), axis, bit)


def spread(block, bits):
    for bit in reversed(bits):
        block = double(block, "dp", bit)
    return block


class Plain:
    def __init__(self):
        self.groups = lax.axis_size("fsdp")
        self.mine = lax.axis_index("fsdp")

    def gather(self, w_in, packed, w_out, main, prepare):
        by_group = lax.all_gather(w_in.T, "fsdp")
        weight = by_group.transpose(1, 0, 2).reshape(by_group.shape[1], -1)
        out_weight = lax.all_gather(w_out, "fsdp", tiled=True)
        here = jnp.zeros((2,), jnp.int32)
        sizes = [main], [out_weight.shape[0]]
        return (
            ([weight], here, sizes[0]),
            weight[main:],
            prepare(lax.all_gather(packed, "fsdp")),
            ([out_weight], here, sizes[1]),
        )

    def late(self, pieces, places, lengths, earlier):
        return pieces, places, lengths

    def own(self, total, axis):
        return cut(total, self.mine, self.groups, axis).astype(F32)

    def sums(self, low_mixed, incoming, d_gate, normed, kernels, columns, fillers):
        everywhere = lambda term, axis: self.own(lax.psum(term.astype(BF16), ("fsdp", "dp")), axis)
        g_out = everywhere(mul_nn(low_mixed, incoming), 0)
        g_rows, results = [everywhere(mul_tn(d_gate, normed), 1)], []
        for kernel in kernels:
            results.append(kernel(results))
        rest = results[-1][0]
        g_rows.append(everywhere(mul_tn(rest[:, :columns], normed), 1))
        block_out = fillers[0](d_gate)
        input_grad, small = fillers[1](results, rest, d_gate)
        total = cut(lax.psum(small, ("fsdp", "dp")), self.mine, self.groups)[0]
        return g_out, g_rows, fillers[2](total), input_grad, block_out


class Paired:
    def __init__(self):
        self.mine = lax.axis_index("fsdp")
        self.core = lax.axis_index("dp") % 2
        self.bits = powers_of_two(lax.axis_size("dp"))

    def gather(self, w_in, packed, w_out, main, prepare):
        mine, core = self.mine, self.core
        rows = w_in.T
        columns = rows.shape[1]
        last = jnp.pad(rows[main:], ((0, 32 - (rows.shape[0] - main)), (0, 0)))
        half = main // 2
        outer = half // 48 * 16
        middle = half - 2 * outer
        near = self.bits[1]
        side = (lax.axis_index("dp") // near) % 2
        first_row = core * half
        row = lambda where: first_row + jnp.where(side == where, 0, outer + middle)
        part = lambda start, count: lax.dynamic_slice_in_dim(rows, start, count, 0)
        other_packed = swap(packed, "fsdp", 1)
        mine_outer = swap(jnp.concatenate([part(row(0), outer), last], axis=0), "fsdp", 1)
        mine_middle = swap(after(part(first_row + outer, middle), mine_outer), "fsdp", 1)
        near_outer = swap(mine_outer, "dp", near)
        in_order = lambda a, b, axis: jnp.where(
            mine == 0, jnp.concatenate([a, b], axis), jnp.concatenate([b, a], axis)
        )
        raw_weight = in_order(last, mine_outer[outer:], 1)
        prepared = prepare(in_order(packed[None], other_packed[None], 0))
        raw_weight, *prepared = together(raw_weight, *prepared, mine_middle)[:-1]
        core_outer = swap(after(mine_outer, near_outer, mine_middle, raw_weight, *prepared), "dp", 1)
        core_middle = swap(mine_middle, "dp", 1)
        core_near = swap(near_outer, "dp", 1)
        there = (1 - mine) * columns
        across = half - 2 * first_row
        places = [0, mine * columns]
        for start in (row(0), first_row + outer, row(1)):
            places += [start, there, start + across, there]
        places = jnp.stack(places).astype(jnp.int32)
        pieces = [rows, mine_outer, core_outer, mine_middle, core_middle, near_outer, core_near]
        lengths = [main, outer, outer, middle, middle, outer, outer]
        relayed = core_near

        each = w_out.shape[0]
        direct_out = swap(after(cut(w_out, core, 2), relayed), "fsdp", 1)
        other = (1 - mine) * each
        places_out = jnp.stack(
            [mine * each, 0, other + core * (each // 2), 0, other + (1 - core) * (each // 2), 0]
        ).astype(jnp.int32)
        return (
            (pieces, places, lengths),
            raw_weight,
            prepared,
            ([w_out, direct_out], places_out, [each, each // 2, each // 2]),
        )

    def late(self, pieces, places, lengths, earlier):
        own, direct = pieces
        direct = after(direct, earlier)
        return [own, direct, swap(direct, "dp", 1)], places, lengths

    def sums(self, low_mixed, incoming, d_gate, normed, kernels, columns, fillers):
        mine, core, (near, *far) = self.mine, self.core, self.bits[1:]
        near_side = (lax.axis_index("dp") // near) % 2
        owned = lambda block: (cut(block, mine, 2, 1), cut(block, 1 - mine, 2, 1))
        across = lambda give: swap(give, "fsdp", 1)
        over = lambda give, bit: swap(give, "dp", bit)

        def by_cores(term, axis):
            return cut(term, core, 2, axis), swap(cut(term, 1 - core, 2, axis), "dp", 1)

        out_keep, out_got = by_cores(mul_nn(low_mixed, incoming).astype(BF16), 1)
        gate_term = mul_tn(d_gate, normed).astype(BF16)
        out_got, gate_term = together(out_got, gate_term)
        out_block = added(out_keep, out_got)
        out_give = cut(out_block, 1 - mine, 2)
        got_out = across(out_give)
        gate_keep, gate_got = by_cores(after(gate_term, out_give), 0)
        gate_keep, gate_give = owned(added(gate_keep, gate_got))
        got_gate = across(gate_give)
        first = kernels[0]([], gate_give)
        got_out, got_gate, _ = together(got_out, got_gate, first[-1])
        keep_a = jnp.concatenate([cut(out_block, mine, 2), gate_keep], axis=0)
        got_a = jnp.concatenate([got_out, got_gate], axis=0)
        keep_a, give_a = sides(added(keep_a, got_a), "dp", near)
        got_a = over(give_a, near)
        second = kernels[1]([first], give_a)
        got_a, rest = together(got_a, second[0])
        keep_b, got_b = by_cores(mul_tn(rest[:, :columns], normed).astype(BF16), 0)
        block_b = added(keep_b, got_b)
        keep_b, give_b = owned(block_b)
        got_b = across(give_b)
        side = lambda bit: (lax.axis_index("dp") // bit) % 2
        results = [first, second]
        turn, wide = far[0], far[1:]

        keep_a, give_a = sides(added(keep_a, after(got_a, give_b)), "dp", turn)
        got_a = over(give_a, turn)
        block_out = fillers[0](after(give_b, give_a))
        got_a, block_out = together(got_a, block_out)
        block_a = added(keep_a, got_a)
        sent_a = [over(block_a, bit) for bit in wide[:1]]
        input_grad, small = fillers[1](results, rest, block_a)
        for bit in wide[1:]:
            block_a = added(block_a, sent_a.pop())
            sent_a = [over(block_a, bit)]
        *sent_a, got_b, small = together(*sent_a, got_b, small)
        if sent_a:
            block_a = added(block_a, sent_a[0])
        block_b = added(keep_b, got_b)

        keep_b, give_b = sides(block_b, "dp", near)
        got_b, got_a, got_s = together(over(give_b, near), over(block_a, turn), over(small, 1))
        block_a, small = joined(block_a, got_a, side(turn)), small + got_s
        spread_a = over(block_a, near)
        keep_b, give_b = sides(added(keep_b, got_b), "dp", turn)
        got_b, got_s = together(over(give_b, turn), over(small, near))
        block_b, small = added(keep_b, got_b), small + got_s
        for bit in wide:
            got_b, got_s = together(over(block_b, bit), over(small, bit))
            block_b, small = added(block_b, got_b), small + got_s
        got_b, got_s, spread_a = together(over(block_b, turn), over(small, turn), spread_a)
        block_b, small = joined(block_b, got_b, side(turn)), small + got_s
        block_a = joined(block_a, spread_a, side(near))
        got_b, got_s = together(over(block_b, near), across(cut(small, 1 - mine, 2)[0]))
        block_b, total = joined(block_b, got_b, side(near)), cut(small, mine, 2)[0] + got_s
        size = out_block.shape[0] // 2
        swapped_a, swapped_b, *g_small = together(swap(block_a, "dp", 1), swap(block_b, "dp", 1), *fillers[2](total))
        g_out = joined(block_a[:size], swapped_a[:size], core, 1).astype(F32)
        g_rows = [joined(block_a[size:], swapped_a[size:], core), joined(block_b, swapped_b, core)]
        return g_out, [rows.astype(F32) for rows in g_rows], g_small, input_grad, block_out


def shards(
    tokens,
    live,
    norm_gain,
    w_in,
    conv_weight,
    conv_bias,
    dt_bias,
    a_log,
    d_skip,
    inner_gain,
    w_out,
    cotangent,
):
    groups, copies = lax.axis_size("fsdp"), lax.axis_size("dp")
    taps = conv_weight.shape[1]
    heads = dt_bias.shape[0] * groups
    inner, conv = inner_gain.shape[0] * groups, conv_bias.shape[0] * groups
    model = tokens.shape[-1]
    proj = w_in.shape[1]
    main = inner + conv
    sizes = (inner, conv, heads, (conv - inner) // 2)
    paired = groups == 2 and powers_of_two(copies) and copies > 2 and main % 32 == 0
    links = Paired() if paired else Plain()

    rest = jnp.concatenate([norm_gain, dt_bias, a_log, d_skip])
    line = max(conv_bias.shape[0], inner_gain.shape[0], rest.shape[0])
    lined = lambda table: jnp.pad(table, ((0, 0), (0, line - table.shape[1])))
    packed = jnp.concatenate([lined(conv_weight.T), lined(conv_bias[None]), lined(inner_gain[None]), lined(rest[None])])

    def prepare(packed):
        packed = packed.astype(F32)
        pick = lambda row, first, each: packed[:, row, first : first + each].reshape(-1)
        model_each, heads_each = norm_gain.shape[0], dt_bias.shape[0]
        table = packed[:, : taps + 1, : conv // groups].transpose(1, 0, 2).reshape(taps + 1, conv)
        table = jnp.concatenate([table, jnp.zeros((7 - taps, conv), F32)], axis=0)
        taps_in = table.reshape(8, conv // LANES, LANES).transpose(1, 0, 2)
        inner_all = pick(taps + 1, 0, inner // groups)[:, None]
        gain_all = pick(taps + 2, 0, model_each)[None]
        by_head = [pick(taps + 2, model_each + k * heads_each, heads_each) for k in range(3)]
        return [taps_in, inner_all, gain_all, jnp.stack(by_head[:2], axis=1), by_head[2]]

    in_pieces, raw_weight, prepared, out_pieces = links.gather(w_in, packed, w_out, main, prepare)
    raw_weight = jnp.pad(raw_weight, ((0, 32 - raw_weight.shape[0]), (0, 0)))
    taps_in, inner_all, gain_all, heads_in, skip = prepared

    alive = live.astype(F32).reshape(1)
    low_tokens, low_cotangent = tokens[0, 0], cotangent[0, 0]
    normed, mixed, active, raw, states, gate, scanned, weight = forward(
        sizes, in_pieces[1], low_tokens, gain_all, raw_weight, taps_in, heads_in, in_pieces[0], in_pieces[2]
    )
    out_pieces = links.late(*out_pieces, normed)
    low_mixed, d_gate, d_scan, row_part, skip_part, gain_part, out_weight = gated(
        sizes, out_pieces[1], skip, alive, low_cotangent, inner_all, gate, scanned, active, out_pieces[0], out_pieces[2]
    )
    u = low_tokens.astype(F32)
    incoming = low_cotangent.astype(F32) * alive[0]

    def backward_step(first, count):
        def step(earlier, *sent):
            scan = after(d_scan, *sent) if sent else d_scan
            return backward(
                sizes,
                first,
                count,
                skip,
                active,
                mixed,
                scan,
                raw,
                row_part,
                states,
                taps_in,
                heads_in,
                earlier[-1] if earlier else None,
            )

        return step

    kernels = [backward_step(first, count) for first, count in HEAD_RANGES]

    step = 64
    rest_columns = -(-(proj - inner) // step) * step

    def input_part(results, rest, tie):
        d_raw, rate_part = [jnp.concatenate([result[k] for result in results], axis=0) for k in (1, 2)]
        conv_part = jnp.concatenate([result[3] for result in results], axis=1).reshape(taps + 1, conv)
        input_grad, gain_part_in = input_backward(
            alive, low_tokens, low_cotangent, gain_all, d_gate, after(rest, tie), weight
        )
        terms = [
            conv_part,
            jnp.sum(gain_part, axis=1)[None],
            jnp.sum(gain_part_in, axis=0)[None],
            jnp.sum(d_raw, axis=1)[None],
            jnp.sum(rate_part, axis=1)[None],
            jnp.sum(skip_part, axis=1)[None],
        ]
        by_owner = [
            jnp.moveaxis(term.reshape(term.shape[0], groups, -1), 1, 0).reshape(groups, -1) for term in terms
        ]
        count = sum(term.shape[1] for term in by_owner)
        by_owner.append(jnp.zeros((groups, -count % (8 * LANES)), F32))
        return input_grad, jnp.concatenate(by_owner, axis=1).reshape(groups, -1, LANES)

    def out_part(tie):
        branch = mul_tn(after(low_mixed, tie), out_weight)
        return (alive[0] * (u + branch)).astype(BF16)

    def small_grads(total):
        total = total.reshape(-1)
        shapes = [(taps + 1, conv), (1, inner), (1, model), (1, heads), (1, heads), (1, heads)]
        first, parts = 0, []
        for lines, line in shapes:
            size = lines * line // groups
            parts.append(total[first : first + size].reshape(lines, -1))
            first += size
        g_conv, g_inner, g_gain, g_bias, g_rate, g_skip = parts
        return [g_gain[0], g_conv[:taps].T, g_conv[taps], g_bias[0], g_rate[0], g_skip[0], g_inner[0]]

    g_out, g_rows, g_small, input_grad, block_out = links.sums(
        low_mixed,
        incoming.astype(BF16),
        d_gate,
        normed,
        kernels,
        rest_columns,
        [out_part, input_part, small_grads],
    )
    g_proj = jnp.concatenate([g_rows[0], g_rows[1][: proj - inner]], axis=0).T
    return (
        block_out.reshape(tokens.shape),
        input_grad.reshape(cotangent.shape),
        g_small[0],
        g_proj,
        *g_small[1:],
        g_out,
    )


def solution(mesh):
    by_device = P("fsdp", "dp", None, None)
    lines, tables = P("fsdp"), P("fsdp", None)
    return jax.shard_map(
        shards,
        mesh=mesh,
        in_specs=(
            by_device,
            P("fsdp", "dp"),
            lines,
            tables,
            tables,
            lines,
            lines,
            lines,
            lines,
            lines,
            tables,
            by_device,
        ),
        out_specs=(by_device, by_device, lines, tables, tables, lines, lines, lines, lines, lines, tables),
        check_vma=False,
    )
```

profile of v0, /device:TPU:1, one launch (start us, length us, event | category | flops | bytes accessed | tf_op | source)
XLA Modules:
  0.0 236.0 jit_solution(15494778117588343985)
XLA Ops:
  0.7 1.1 dynamic-slice_bitcast_fusion.1
  1.9 0.7 slice.102
  2.6 2.1 collective-permute-start
  4.7 0.7 broadcast_in_dim.19
  6.1 0.8 pad_maximum_fusion.4
  6.9 0.7 fusion.13
  7.7 1.1 dynamic-slice_bitcast_fusion
  8.9 6.1 %collective-permute-done.1 = bf16[7,896]{1,0:T(8,128)(2,1)S(1)} collective-permute-done((bf16[7,896]{1,0:T(8,128)(2,1)S(1)}, bf16[7,896]{1,0:T(8,128)(2,1)S(1)}, u32[]{:S(2)}, u32[]{:S(2)}) %collective-permute-start.1) | collective-permute-done | bytes 12576 | tf_op jit(solution)/shard_map/ppermute | solution.py:745
  15.6 1.1 collective-permute-start.2
  16.7 1.2 collective-permute-start.3
  20.1 5.9 %collective-permute-done.2.refs_3_ = bf16[576,384]{1,0:T(8,128)(2,1)S(1)} collective-permute-done((bf16[576,384]{1,0:T(8,128)(2,1)S(1)}, bf16[576,384]{1,0:T(8,128)(2,1)S(1)}, u32[]{:S(2)}, u32[]{:S(2)}) %collective-permute-start.2) | collective-permute-done | bytes 442400 | tf_op jit(solution)/shard_map/ppermute | solution.py:745
  26.6 2.7 %collective-permute-start.6 = (bf16[576,384]{1,0:T(8,128)(2,1)S(1)}, bf16[576,384]{1,0:T(8,128)(2,1)}, u32[]{:S(2)}, u32[]{:S(2)}) collective-permute-start(bf16[576,384]{1,0:T(8,128)(2,1)S(1)} %collective-permute-done.3.refs_5_), channel_id=1, source_target_pairs={{0,1},{1,0},{2,3},{3,2},{4,5},{5,4},{6,7},{7,6},{8,9},{9,8},{10,11... | collective-permute-start | bytes 1327112 | tf_op jit(solution)/shard_map/ppermute | solution.py:745
  32.1 24.0 %block_forward.1 = (bf16[1024,768]{1,0:T(8,128)(2,1)}, bf16[1024,1792]{1,0:T(8,128)(2,1)}, bf16[1792,1024]{1,0:T(8,128)(2,1)}, f32[24,1024]{1,0:T(8,128)}, bf16[...) custom-call(s32[14]{0:T(128)} %stack.60.places_ref, ...), custom_call_target="tpu_custom_call" | custom-call | flops 30000001024 | bytes 30000000 | tf_op jit(solution)/shard_map/block_forward/pallas_call | solution.py:512
  57.9 1.2 copy.30.inner_gain_ref
  59.1 0.8 copy-done.14
  59.9 19.9 %block_gated.1 = (bf16[1536,1024]{1,0:T(8,128)(2,1)}, bf16[1024,1536]{1,0:T(8,128)(2,1)}, bf16[1536,1024]{1,0:T(8,128)(2,1)}, f32[24,1024]{1,0:T(8,128)}, f32[24...) custom-call(s32[6]{0:T(128)} %stack.50.places_ref, f32[24]{0:T(128)} %reshape_squeeze.3.skip_ref.refs_0_, ...), custom_call_target="tpu_custom_call" | custom-call | flops 15000000512 | bytes 15000000 | tf_op jit(solution)/shard_map/block_gated/pallas_call | solution.py:569
  79.9 4.5 %convolution_convert_fusion.1 = bf16[1536,768]{1,0:T(8,128)(2,1)S(1)} fusion(bf16[1536,1024]{1,0:T(8,128)(2,1)} %get-tuple-element.98, f32[]{:T(128)} %bitcast.26, bf16[1,1,1024,768]{3,2,1,0:T(8,128)(2,1)S(1)} %copy-done.11), kind=kOutput, calls=%fused_computation.4 | convolution fusion | flops 2419458048 | bytes 7077892 | tf_op jit(solution)/shard_map/dot_general | solution.py:29
  84.4 1.4 copy-done.1
  86.2 5.2 %convolution_convert_fusion = bf16[1536,768]{1,0:T(8,128)(2,1)S(1)} fusion(bf16[1024,1536]{1,0:T(8,128)(2,1)} %get-tuple-element.99.d_gate_ref, bf16[1024,768]{1,0:T(8,128)(2,1)} %get-tuple-element.96), kind=kOutput, calls=%fused_computation.3 | convolution fusion | flops 2417098752 | bytes 7077888 | tf_op jit(solution)/shard_map/dot_general | solution.py:37
  91.4 1.6 add_convert_fusion.3
  93.0 1.0 constant_dynamic-slice_fusion.10
  93.9 1.1 constant_dynamic-slice_fusion.8
  95.9 2.3 collective-permute-done.10
  98.2 1.6 add_convert_fusion.2
  100.5 21.0 %block_backward.2 = (bf16[1024,2048]{1,0:T(8,128)(2,1)}, f32[16,1024]{1,0:T(8,128)}, f32[16,1024]{1,0:T(8,128)}, f32[5,8,128]{2,1,0:T(8,128)}, f32[256,1024]{1,0:T(8,128)}) custom-call(f32[24]{0:T(128)} %reshape_squeeze.3.skip_ref.refs_0_, bf16[1792,1024]{1,0:T(8,128)(2,1)} %get-tuple-element.94.refs_2_.refs_1_, ...), custom_call_target="tpu_custom_call" | custom-call | flops 20000000000 | bytes 20000000 | tf_op jit(solution)/shard_map/block_backward/pallas_call | solution.py:674
  121.6 1.5 collective-permute-done.12
  123.4 1.3 collective-permute-start.13
  124.7 15.0 %block_backward.3 = (bf16[1024,2048]{1,0:T(8,128)(2,1)}, f32[8,1024]{1,0:T(8,128)}, f32[8,1024]{1,0:T(8,128)}, f32[5,6,128]{2,1,0:T(8,128)}) custom-call(f32[24]{0:T(128)} %reshape_squeeze.3.skip_ref.refs_0_, bf16[1792,1024]{1,0:T(8,128)(2,1)} %get-tuple-element.94.refs_2_.refs_1_, ...), custom_call_target="tpu_custom_call", output_to_operand_aliasing={{0}: (15, {})} | custom-call | flops 12000000000 | bytes 12000000 | tf_op jit(solution)/shard_map/block_backward/pallas_call | solution.py:674
  139.8 0.8 copy-done.4
  140.6 5.8 %fusion.2 = bf16[1856,768]{1,0:T(8,128)(2,1)S(1)} fusion(bf16[1024,768]{1,0:T(8,128)(2,1)} %get-tuple-element.96, bf16[1024,2048]{1,0:T(8,128)(2,1)} %get-tuple-element.122.d_rest_ref), kind=kOutput, calls=%fused_computation.5 | convolution fusion | flops 2920660992 | bytes 8355840 | tf_op jit(solution)/shard_map/dot_general | solution.py:37
  146.4 1.6 copy-done
  148.0 1.3 collective-permute-start.14
  149.3 3.0 %collective-permute-done.14 = bf16[928,768]{1,0:T(8,128)(2,1)} collective-permute-done((bf16[928,768]{1,0:T(8,128)(2,1)S(1)}, bf16[928,768]{1,0:T(8,128)(2,1)}, u32[]{:S(2)}, u32[]{:S(2)}) %collective-permute-start.14) | collective-permute-done | bytes 1425440 | tf_op jit(solution)/shard_map/ppermute | solution.py:745
  152.3 2.3 add_convert_fusion
  154.6 0.9 constant_dynamic-slice_fusion.3
  155.7 1.4 collective-permute-start.15
  157.1 3.9 %multiply_convert_fusion = bf16[1024,768]{1,0:T(8,128)(2,1)} fusion(bf16[1536,1024]{1,0:T(8,128)(2,1)S(1)} %copy-done.17, bf16[1536,768]{1,0:T(8,128)(2,1)S(1)} %copy-done.18, f32[]{:T(128)} %bitcast.26, bf16[1,1,1024,768]{3,2,1,0:T(8,128)(2,1)S(1)} %copy-done.12), kind=kOutput, calls=%fused_computation.6 | convolution fusion | flops 2419064832 | bytes 8650756 | tf_op jit(solution)/shard_map/dot_general | solution.py:37
  161.0 0.9 reduce_sum.45
  161.9 0.7 reshape_transpose_reshape_broadcast_in_dim.15
  162.8 1.0 maximum_reduce_fusion
  164.0 0.8 pad_maximum_fusion.3
  165.4 2.4 %collective-permute-start.16 = (bf16[384,384]{1,0:T(8,128)(2,1)S(1)}, bf16[384,384]{1,0:T(8,128)(2,1)S(1)}, u32[]{:S(2)}, u32[]{:S(2)}) collective-permute-start(bf16[384,384]{1,0:T(8,128)(2,1)S(1)} %add_convert_fusion.8), channel_id=1, source_target_pairs={{0,8},{1,9},{2,10},{3,11},{4,12},{5,13},{6,14},{7,15},{8,0},{9,1},... | collective-permute-start | bytes 884744 | tf_op jit(solution)/shard_map/ppermute | solution.py:745
  167.8 11.9 %input_backward.1 = (f32[1024,768]{1,0:T(8,128)}, f32[8,768]{1,0:T(8,128)}) custom-call(f32[1]{0:T(128)} %bitcast.15.alive_ref, bf16[1024,768]{1,0:T(8,128)(2,1)} %bitcast.86, bf16[1024,768]{1,0:T(8,128)(2,1)} %bitcast.84, f32[1,768]{1,0:T(1,128)} %bitcast.82, bf16[1024,1536]{1,0:T(8,128)(2,1)} %get-tuple-element.99.d_gate_ref, ...), custom_call_target="tpu_custom_call" | custom-call | flops 8000000000 | bytes 8000000 | tf_op jit(solution)/shard_map/input_backward/pallas_call | solution.py:633
  179.8 0.7 reduce_sum.46
  181.0 1.0 collective-permute-done.17
  182.0 1.3 add_convert_fusion.4
  183.7 1.2 collective-permute-start.19
  184.9 1.8 collective-permute-start.20
  186.7 0.9 collective-permute-done.20
  187.6 2.9 %collective-permute-done.19 = bf16[384,384]{1,0:T(8,128)(2,1)S(1)} collective-permute-done((bf16[384,384]{1,0:T(8,128)(2,1)S(1)}, bf16[384,384]{1,0:T(8,128)(2,1)S(1)}, u32[]{:S(2)}, u32[]{:S(2)}) %collective-permute-start.19) | collective-permute-done | bytes 294944 | tf_op jit(solution)/shard_map/ppermute | solution.py:745
  190.5 1.3 collective-permute-done.18
  191.8 1.6 collective-permute-start.21
  193.6 2.8 %collective-permute-done.22 = f32[2,48,128]{2,1,0:T(8,128)S(1)} collective-permute-done((f32[2,48,128]{2,1,0:T(8,128)S(1)}, f32[2,48,128]{2,1,0:T(8,128)S(1)}, u32[]{:S(2)}, u32[]{:S(2)}) %collective-permute-start.22) | collective-permute-done | bytes 49184 | tf_op jit(solution)/shard_map/ppermute | solution.py:745
  196.4 2.4 %collective-permute-start.23 = (bf16[232,384]{1,0:T(8,128)(2,1)S(1)}, bf16[232,384]{1,0:T(8,128)(2,1)S(1)}, u32[]{:S(2)}, u32[]{:S(2)}) collective-permute-start(bf16[232,384]{1,0:T(8,128)(2,1)S(1)} %add_convert_fusion.10), channel_id=1, source_target_pairs={{0,8},{1,9},{2,10},{3,11},{4,12},{5,13},{6,14},{7,15},{8,0},{9,1},... | collective-permute-start | bytes 534536 | tf_op jit(solution)/shard_map/ppermute | solution.py:745
  199.3 7.9 %collective-permute-done.24 = f32[2,48,128]{2,1,0:T(8,128)S(1)} collective-permute-done((f32[2,48,128]{2,1,0:T(8,128)S(1)}, f32[2,48,128]{2,1,0:T(8,128)S(1)}, u32[]{:S(2)}, u32[]{:S(2)}) %collective-permute-start.24) | collective-permute-done | bytes 49184 | tf_op jit(solution)/shard_map/ppermute | solution.py:745
  207.2 1.5 collective-permute-start.25
  208.9 3.6 %collective-permute-done.26 = f32[2,48,128]{2,1,0:T(8,128)S(1)} collective-permute-done((f32[2,48,128]{2,1,0:T(8,128)S(1)}, f32[2,48,128]{2,1,0:T(8,128)S(1)}, u32[]{:S(2)}, u32[]{:S(2)}) %collective-permute-start.26) | collective-permute-done | bytes 49184 | tf_op jit(solution)/shard_map/ppermute | solution.py:745
  213.8 4.1 %collective-permute-start.28 = (bf16[1536,384]{1,0:T(8,128)(2,1)S(1)}, bf16[1536,384]{1,0:T(8,128)(2,1)}, u32[]{:S(2)}, u32[]{:S(2)}) collective-permute-start(bf16[1536,384]{1,0:T(8,128)(2,1)S(1)} %maximum_select_fusion), channel_id=1, source_target_pairs={{0,1},{1,0},{2,3},{3,2},{4,5},{5,4},{6,7},{7,6},{8,9},{9,8},{10,11... | collective-permute-start | bytes 3538952 | tf_op jit(solution)/shard_map/ppermute | solution.py:745
  218.1 1.7 collective-permute-done.29
  220.1 5.1 %collective-permute-start.31 = (bf16[928,384]{1,0:T(8,128)(2,1)S(1)}, bf16[928,384]{1,0:T(8,128)(2,1)}, u32[]{:S(2)}, u32[]{:S(2)}) collective-permute-start(bf16[928,384]{1,0:T(8,128)(2,1)S(1)} %maximum_select_fusion.3), channel_id=1, source_target_pairs={{0,1},{1,0},{2,3},{3,2},{4,5},{5,4},{6,7},{7,6},{8,9},{9,8},{10,11... | collective-permute-start | bytes 2138120 | tf_op jit(solution)/shard_map/ppermute | solution.py:745
  228.2 1.4 fusion.16
  229.5 1.6 fusion.6
  231.2 1.7 fusion.7
  233.3 2.7 %convert_bitcast_fusion = f32[384,3352]{0,1:T(8,128)} fusion(bf16[1816,384]{1,0:T(8,128)(2,1)S(1)} %fusion.6, bf16[1536,384]{1,0:T(8,128)(2,1)S(1)} %maximum_select_fusion.1), kind=kLoop, calls=%fused_computation | loop fusion | flops 5148672 | bytes 7723008 | tf_op jit(solution)/shard_map/transpose | solution.py:1128
  (131 shorter events, 18.8 us)
Async XLA Ops:
  0.6 8.2 %copy-start.9 = (bf16[896,4]{0,1:T(4,128)(2,1)S(1)}, bf16[896,4]{0,1:T(4,128)(2,1)}, u32[]{:S(2)}) copy-start(bf16[896,4]{0,1:T(4,128)(2,1)} %param.16) | copy-start | bytes 21508
  0.7 29.8 %copy-start.6 = (bf16[768,768]{1,0:T(8,128)(2,1)S(1)}, bf16[768,768]{1,0:T(8,128)(2,1)}, u32[]{:S(2)}) copy-start(bf16[768,768]{1,0:T(8,128)(2,1)} %refs_3_.1) | copy-start | bytes 3538948
  2.6 12.9 %collective-permute-start = (bf16[576,384]{1,0:T(8,128)(2,1)S(1)}, bf16[576,384]{1,0:T(8,128)(2,1)S(1)}, u32[]{:S(2)}, u32[]{:S(2)}) collective-permute-start(bf16[576,384]{1,0:T(8,128)(2,1)S(1)} %pad_maximum_fusion.2), channel_id=1, source_target_pairs={{0,16},{16,0},{1,17},{17,1},{2,18},{18,2},{3,19},{19,3},{4,20},{20... | collective-permute-start | bytes 1327112 | tf_op jit(solution)/shard_map/ppermute | solution.py:745
  7.6 7.3 %collective-permute-start.1 = (bf16[7,896]{1,0:T(8,128)(2,1)S(1)}, bf16[7,896]{1,0:T(8,128)(2,1)S(1)}, u32[]{:S(2)}, u32[]{:S(2)}) collective-permute-start(bf16[7,896]{1,0:T(8,128)(2,1)S(1)} %fusion.13), channel_id=1, source_target_pairs={{0,16},{16,0},{1,17},{17,1},{2,18},{18,2},{3,19},{19,3},{4,20},{20... | collective-permute-start | bytes 37640 | tf_op jit(solution)/shard_map/ppermute | solution.py:745
  15.6 16.6 %copy-start.10 = (bf16[576,384]{1,0:T(8,128)(2,1)}, bf16[576,384]{1,0:T(8,128)(2,1)S(1)}, u32[]{:S(2)}) copy-start(bf16[576,384]{1,0:T(8,128)(2,1)S(1)} %collective-permute-done.refs_1_) | copy-start | bytes 1327108
  15.6 10.4 %collective-permute-start.2 = (bf16[576,384]{1,0:T(8,128)(2,1)S(1)}, bf16[576,384]{1,0:T(8,128)(2,1)S(1)}, u32[]{:S(2)}, u32[]{:S(2)}) collective-permute-start(bf16[576,384]{1,0:T(8,128)(2,1)S(1)} %dynamic-slice_bitcast_fusion), channel_id=1, source_target_pairs={{0,16},{16,0},{1,17},{17,1},{2,18},{18,2},{3,19},{19,3},{4,20},{20... | collective-permute-start | bytes 1327112 | tf_op jit(solution)/shard_map/ppermute | solution.py:745
  16.7 9.8 %collective-permute-start.3 = (bf16[576,384]{1,0:T(8,128)(2,1)S(1)}, bf16[576,384]{1,0:T(8,128)(2,1)S(1)}, u32[]{:S(2)}, u32[]{:S(2)}) collective-permute-start(bf16[576,384]{1,0:T(8,128)(2,1)S(1)} %collective-permute-done.refs_1_), channel_id=1, source_target_pairs={{0,2},{1,3},{2,0},{3,1},{4,6},{5,7},{6,4},{7,5},{8,10},{9,11},{10,... | collective-permute-start | bytes 1327112 | tf_op jit(solution)/shard_map/ppermute | solution.py:745
  26.0 6.1 %copy-start.15 = (bf16[576,384]{1,0:T(8,128)(2,1)}, bf16[576,384]{1,0:T(8,128)(2,1)S(1)}, u32[]{:S(2)}) copy-start(bf16[576,384]{1,0:T(8,128)(2,1)S(1)} %collective-permute-done.2.refs_3_) | copy-start | bytes 1327108
  26.6 5.6 %copy-start.16 = (bf16[576,384]{1,0:T(8,128)(2,1)}, bf16[576,384]{1,0:T(8,128)(2,1)S(1)}, u32[]{:S(2)}) copy-start(bf16[576,384]{1,0:T(8,128)(2,1)S(1)} %collective-permute-done.3.refs_5_) | copy-start | bytes 1327108
  26.6 4.7 %collective-permute-start.6 = (bf16[576,384]{1,0:T(8,128)(2,1)S(1)}, bf16[576,384]{1,0:T(8,128)(2,1)}, u32[]{:S(2)}, u32[]{:S(2)}) collective-permute-start(bf16[576,384]{1,0:T(8,128)(2,1)S(1)} %collective-permute-done.3.refs_5_), channel_id=1, source_target_pairs={{0,1},{1,0},{2,3},{3,2},{4,5},{5,4},{6,7},{7,6},{8,9},{9,8},{10,11... | collective-permute-start | bytes 1327112 | tf_op jit(solution)/shard_map/ppermute | solution.py:745
  29.3 2.2 collective-permute-start.4
  29.3 2.8 %collective-permute-start.5 = (bf16[576,384]{1,0:T(8,128)(2,1)S(1)}, bf16[576,384]{1,0:T(8,128)(2,1)}, u32[]{:S(2)}, u32[]{:S(2)}) collective-permute-start(bf16[576,384]{1,0:T(8,128)(2,1)S(1)} %collective-permute-done.2.refs_3_), channel_id=1, source_target_pairs={{0,1},{1,0},{2,3},{3,2},{4,5},{5,4},{6,7},{7,6},{8,9},{9,8},{10,11... | collective-permute-start | bytes 1327112 | tf_op jit(solution)/shard_map/ppermute | solution.py:745
  31.2 24.9 %collective-permute-start.7 = (bf16[384,768]{1,0:T(8,128)(2,1)S(1)}, bf16[384,768]{1,0:T(8,128)(2,1)S(1)}, u32[]{:S(2)}, u32[]{:S(2)}) collective-permute-start(bf16[384,768]{1,0:T(8,128)(2,1)S(1)} %constant_dynamic-slice_fusion.12), channel_id=1, source_target_pairs={{0,16},{16,0},{1,17},{17,1},{2,18},{18,2},{3,19},{19,3},{4,20},{20... | collective-permute-start | bytes 1769480 | tf_op jit(solution)/shard_map/ppermute | solution.py:745
  56.2 2.9 %copy-start.13 = (bf16[384,768]{1,0:T(8,128)(2,1)}, bf16[384,768]{1,0:T(8,128)(2,1)S(1)}, u32[]{:S(2)}) copy-start(bf16[384,768]{1,0:T(8,128)(2,1)S(1)} %collective-permute-done.7.refs_4_) | copy-start | bytes 1769476
  56.2 2.9 %collective-permute-start.8 = (bf16[384,768]{1,0:T(8,128)(2,1)S(1)}, bf16[384,768]{1,0:T(8,128)(2,1)S(1)}, u32[]{:S(2)}, u32[]{:S(2)}) collective-permute-start(bf16[384,768]{1,0:T(8,128)(2,1)S(1)} %collective-permute-done.7.refs_4_), channel_id=1, source_target_pairs={{0,1},{1,0},{2,3},{3,2},{4,5},{5,4},{6,7},{7,6},{8,9},{9,8},{10,11... | collective-permute-start | bytes 1769480 | tf_op jit(solution)/shard_map/ppermute | solution.py:745
  59.1 0.8 copy-start.14
  59.9 19.9 %copy-start.11 = (bf16[1,1,1024,768]{3,2,1,0:T(8,128)(2,1)S(1)}, bf16[1,1,1024,768]{3,2,1,0:T(8,128)(2,1)}, u32[]{:S(2)}) copy-start(bf16[1,1,1024,768]{3,2,1,0:T(8,128)(2,1)} %param.23) | copy-start | bytes 4718596
  84.4 1.4 copy-start.1
  85.9 5.4 %collective-permute-start.9 = (bf16[1536,384]{1,0:T(8,128)(2,1)S(1)}, bf16[1536,384]{1,0:T(8,128)(2,1)}, u32[]{:S(2)}, u32[]{:S(2)}) collective-permute-start(bf16[1536,384]{1,0:T(8,128)(2,1)S(1)} %constant_dynamic-slice_fusion.11), channel_id=1, source_target_pairs={{0,1},{1,0},{2,3},{3,2},{4,5},{5,4},{6,7},{7,6},{8,9},{9,8},{10,11... | collective-permute-start | bytes 3538952 | tf_op jit(solution)/shard_map/ppermute | solution.py:745
  86.2 5.2 %copy-start.2 = (bf16[1536,768]{1,0:T(8,128)(2,1)S(1)}, bf16[1536,768]{1,0:T(8,128)(2,1)}, u32[]{:S(2)}) copy-start(bf16[1536,768]{1,0:T(8,128)(2,1)} %copy-done.1) | copy-start | bytes 7077892
  95.0 3.2 %collective-permute-start.10 = (bf16[768,768]{1,0:T(8,128)(2,1)}, bf16[768,768]{1,0:T(8,128)(2,1)}, u32[]{:S(2)}, u32[]{:S(2)}) collective-permute-start(bf16[768,768]{1,0:T(8,128)(2,1)} %constant_dynamic-slice_fusion.8), channel_id=1, source_target_pairs={{0,1},{1,0},{2,3},{3,2},{4,5},{5,4},{6,7},{7,6},{8,9},{9,8},{10,11... | collective-permute-start | bytes 3538952 | tf_op jit(solution)/shard_map/ppermute | solution.py:745
  95.4 26.2 %collective-permute-start.11 = (bf16[768,384]{1,0:T(8,128)(2,1)}, bf16[768,384]{1,0:T(8,128)(2,1)S(1)}, u32[]{:S(2)}, u32[]{:S(2)}) collective-permute-start(bf16[768,384]{1,0:T(8,128)(2,1)} %get-tuple-element.167), channel_id=1, source_target_pairs={{0,16},{16,0},{1,17},{17,1},{2,18},{18,2},{3,19},{19,3},{4,20},{20... | collective-permute-start | bytes 1769480 | tf_op jit(solution)/shard_map/ppermute | solution.py:745
  100.0 23.1 %collective-permute-start.12 = (bf16[768,384]{1,0:T(8,128)(2,1)S(1)}, bf16[768,384]{1,0:T(8,128)(2,1)S(1)}, u32[]{:S(2)}, u32[]{:S(2)}) collective-permute-start(bf16[768,384]{1,0:T(8,128)(2,1)S(1)} %get-tuple-element.164), channel_id=1, source_target_pairs={{0,16},{16,0},{1,17},{17,1},{2,18},{18,2},{3,19},{19,3},{4,20},{20... | collective-permute-start | bytes 1769480 | tf_op jit(solution)/shard_map/ppermute | solution.py:745
  123.4 16.3 %collective-permute-start.13 = (bf16[768,384]{1,0:T(8,128)(2,1)S(1)}, bf16[768,384]{1,0:T(8,128)(2,1)S(1)}, u32[]{:S(2)}, u32[]{:S(2)}) collective-permute-start(bf16[768,384]{1,0:T(8,128)(2,1)S(1)} %constant_dynamic-slice_fusion.5), channel_id=1, source_target_pairs={{0,2},{1,3},{2,0},{3,1},{4,6},{5,7},{6,4},{7,5},{8,10},{9,11},{10,... | collective-permute-start | bytes 1769480 | tf_op jit(solution)/shard_map/ppermute | solution.py:745
  139.8 0.8 copy-start.4
  146.4 1.6 copy-start
  148.0 4.3 %collective-permute-start.14 = (bf16[928,768]{1,0:T(8,128)(2,1)S(1)}, bf16[928,768]{1,0:T(8,128)(2,1)}, u32[]{:S(2)}, u32[]{:S(2)}) collective-permute-start(bf16[928,768]{1,0:T(8,128)(2,1)S(1)} %constant_dynamic-slice_fusion.4), channel_id=1, source_target_pairs={{0,1},{1,0},{2,3},{3,2},{4,5},{5,4},{6,7},{7,6},{8,9},{9,8},{10,11... | collective-permute-start | bytes 4276232 | tf_op jit(solution)/shard_map/ppermute | solution.py:745
  149.3 6.2 %copy-start.5 = (bf16[768,384]{1,0:T(8,128)(2,1)S(1)}, bf16[768,384]{1,0:T(8,128)(2,1)}, u32[]{:S(2)}) copy-start(bf16[768,384]{1,0:T(8,128)(2,1)} %copy-done.4) | copy-start | bytes 1769476
  152.3 4.8 %copy-start.17 = (bf16[1536,1024]{1,0:T(8,128)(2,1)S(1)}, bf16[1536,1024]{1,0:T(8,128)(2,1)}, u32[]{:S(2)}) copy-start(bf16[1536,1024]{1,0:T(8,128)(2,1)} %get-tuple-element.98) | copy-start | bytes 9437188
  152.3 4.8 %copy-start.18 = (bf16[1536,768]{1,0:T(8,128)(2,1)S(1)}, bf16[1536,768]{1,0:T(8,128)(2,1)}, u32[]{:S(2)}) copy-start(bf16[1536,768]{1,0:T(8,128)(2,1)} %get-tuple-element.119) | copy-start | bytes 7077892
  154.6 2.5 %copy-start.12 = (bf16[1,1,1024,768]{3,2,1,0:T(8,128)(2,1)S(1)}, bf16[1,1,1024,768]{3,2,1,0:T(8,128)(2,1)}, u32[]{:S(2)}) copy-start(bf16[1,1,1024,768]{3,2,1,0:T(8,128)(2,1)} %param.12) | copy-start | bytes 4718596
  155.7 9.6 %collective-permute-start.15 = (bf16[384,384]{1,0:T(8,128)(2,1)S(1)}, bf16[384,384]{1,0:T(8,128)(2,1)S(1)}, u32[]{:S(2)}, u32[]{:S(2)}) collective-permute-start(bf16[384,384]{1,0:T(8,128)(2,1)S(1)} %constant_dynamic-slice_fusion.2), channel_id=1, source_target_pairs={{0,4},{1,5},{2,6},{3,7},{4,0},{5,1},{6,2},{7,3},{8,12},{9,13},{10,... | collective-permute-start | bytes 884744 | tf_op jit(solution)/shard_map/ppermute | solution.py:745
  157.1 3.9 %copy-start.3 = (f32[1536,128]{1,0:T(8,128)S(1)}, f32[1536,128]{1,0:T(8,128)}, u32[]{:S(2)}) copy-start(f32[1536,128]{1,0:T(8,128)} %get-tuple-element.127) | copy-start | bytes 2359300
  157.1 5.5 %copy-start.7 = (f32[24,1024]{1,0:T(8,128)S(1)}, f32[24,1024]{1,0:T(8,128)}, u32[]{:S(2)}) copy-start(f32[24,1024]{1,0:T(8,128)} %get-tuple-element.132) | copy-start | bytes 294916
  157.1 5.7 %copy-start.8 = (f32[16,1024]{1,0:T(8,128)S(1)}, f32[16,1024]{1,0:T(8,128)}, u32[]{:S(2)}) copy-start(f32[16,1024]{1,0:T(8,128)} %get-tuple-element.113.refs_14_) | copy-start | bytes 196612
  164.8 17.2 %collective-permute-start.17 = (bf16[928,384]{1,0:T(8,128)(2,1)}, bf16[928,384]{1,0:T(8,128)(2,1)}, u32[]{:S(2)}, u32[]{:S(2)}) collective-permute-start(bf16[928,384]{1,0:T(8,128)(2,1)} %constant_dynamic-slice_fusion.3), channel_id=1, source_target_pairs={{0,16},{16,0},{1,17},{17,1},{2,18},{18,2},{3,19},{19,3},{4,20},{20... | collective-permute-start | bytes 2138120 | tf_op jit(solution)/shard_map/ppermute | solution.py:745
  165.4 15.6 %collective-permute-start.16 = (bf16[384,384]{1,0:T(8,128)(2,1)S(1)}, bf16[384,384]{1,0:T(8,128)(2,1)S(1)}, u32[]{:S(2)}, u32[]{:S(2)}) collective-permute-start(bf16[384,384]{1,0:T(8,128)(2,1)S(1)} %add_convert_fusion.8), channel_id=1, source_target_pairs={{0,8},{1,9},{2,10},{3,11},{4,12},{5,13},{6,14},{7,15},{8,0},{9,1},... | collective-permute-start | bytes 884744 | tf_op jit(solution)/shard_map/ppermute | solution.py:745
  183.3 8.4 %collective-permute-start.18 = (bf16[464,384]{1,0:T(8,128)(2,1)S(1)}, bf16[464,384]{1,0:T(8,128)(2,1)S(1)}, u32[]{:S(2)}, u32[]{:S(2)}) collective-permute-start(bf16[464,384]{1,0:T(8,128)(2,1)S(1)} %constant_dynamic-slice_fusion.1), channel_id=1, source_target_pairs={{0,2},{1,3},{2,0},{3,1},{4,6},{5,7},{6,4},{7,5},{8,10},{9,11},{10,... | collective-permute-start | bytes 1069064 | tf_op jit(solution)/shard_map/ppermute | solution.py:745
  183.7 6.8 %collective-permute-start.19 = (bf16[384,384]{1,0:T(8,128)(2,1)S(1)}, bf16[384,384]{1,0:T(8,128)(2,1)S(1)}, u32[]{:S(2)}, u32[]{:S(2)}) collective-permute-start(bf16[384,384]{1,0:T(8,128)(2,1)S(1)} %add_convert_fusion.7), channel_id=1, source_target_pairs={{0,4},{1,5},{2,6},{3,7},{4,0},{5,1},{6,2},{7,3},{8,12},{9,13},{10,... | collective-permute-start | bytes 884744 | tf_op jit(solution)/shard_map/ppermute | solution.py:745
  184.9 2.7 %collective-permute-start.20 = (f32[2,48,128]{2,1,0:T(8,128)S(1)}, f32[2,48,128]{2,1,0:T(8,128)S(1)}, u32[]{:S(2)}, u32[]{:S(2)}) collective-permute-start(f32[2,48,128]{2,1,0:T(8,128)S(1)} %bitcast.72), channel_id=1, source_target_pairs={{0,1},{1,0},{2,3},{3,2},{4,5},{5,4},{6,7},{7,6},{8,9},{9,8},{10,11... | collective-permute-start | bytes 147464 | tf_op jit(solution)/shard_map/ppermute | solution.py:745
  191.8 4.5 %collective-permute-start.21 = (bf16[232,384]{1,0:T(8,128)(2,1)S(1)}, bf16[232,384]{1,0:T(8,128)(2,1)S(1)}, u32[]{:S(2)}, u32[]{:S(2)}) collective-permute-start(bf16[232,384]{1,0:T(8,128)(2,1)S(1)} %constant_dynamic-slice_fusion), channel_id=1, source_target_pairs={{0,4},{1,5},{2,6},{3,7},{4,0},{5,1},{6,2},{7,3},{8,12},{9,13},{10,... | collective-permute-start | bytes 534536 | tf_op jit(solution)/shard_map/ppermute | solution.py:745
  193.4 2.9 %collective-permute-start.22 = (f32[2,48,128]{2,1,0:T(8,128)S(1)}, f32[2,48,128]{2,1,0:T(8,128)S(1)}, u32[]{:S(2)}, u32[]{:S(2)}) collective-permute-start(f32[2,48,128]{2,1,0:T(8,128)S(1)} %add.217), channel_id=1, source_target_pairs={{0,2},{1,3},{2,0},{3,1},{4,6},{5,7},{6,4},{7,5},{8,10},{9,11},{10,... | collective-permute-start | bytes 147464 | tf_op jit(solution)/shard_map/ppermute | solution.py:745
  196.4 10.8 %collective-permute-start.23 = (bf16[232,384]{1,0:T(8,128)(2,1)S(1)}, bf16[232,384]{1,0:T(8,128)(2,1)S(1)}, u32[]{:S(2)}, u32[]{:S(2)}) collective-permute-start(bf16[232,384]{1,0:T(8,128)(2,1)S(1)} %add_convert_fusion.10), channel_id=1, source_target_pairs={{0,8},{1,9},{2,10},{3,11},{4,12},{5,13},{6,14},{7,15},{8,0},{9,1},... | collective-permute-start | bytes 534536 | tf_op jit(solution)/shard_map/ppermute | solution.py:745
  199.0 13.5 %collective-permute-start.27 = (bf16[768,384]{1,0:T(8,128)(2,1)S(1)}, bf16[768,384]{1,0:T(8,128)(2,1)S(1)}, u32[]{:S(2)}, u32[]{:S(2)}) collective-permute-start(bf16[768,384]{1,0:T(8,128)(2,1)S(1)} %maximum_select_fusion.4), channel_id=1, source_target_pairs={{0,2},{1,3},{2,0},{3,1},{4,6},{5,7},{6,4},{7,5},{8,10},{9,11},{10,... | collective-permute-start | bytes 1769480 | tf_op jit(solution)/shard_map/ppermute | solution.py:745
  199.3 7.9 %collective-permute-start.24 = (f32[2,48,128]{2,1,0:T(8,128)S(1)}, f32[2,48,128]{2,1,0:T(8,128)S(1)}, u32[]{:S(2)}, u32[]{:S(2)}) collective-permute-start(f32[2,48,128]{2,1,0:T(8,128)S(1)} %add.219), channel_id=1, source_target_pairs={{0,8},{1,9},{2,10},{3,11},{4,12},{5,13},{6,14},{7,15},{8,0},{9,1},... | collective-permute-start | bytes 147464 | tf_op jit(solution)/shard_map/ppermute | solution.py:745
  207.2 5.2 %collective-permute-start.25 = (bf16[232,384]{1,0:T(8,128)(2,1)S(1)}, bf16[232,384]{1,0:T(8,128)(2,1)S(1)}, u32[]{:S(2)}, u32[]{:S(2)}) collective-permute-start(bf16[232,384]{1,0:T(8,128)(2,1)S(1)} %add_convert_fusion.9), channel_id=1, source_target_pairs={{0,4},{1,5},{2,6},{3,7},{4,0},{5,1},{6,2},{7,3},{8,12},{9,13},{10,... | collective-permute-start | bytes 534536 | tf_op jit(solution)/shard_map/ppermute | solution.py:745
  208.8 3.7 %collective-permute-start.26 = (f32[2,48,128]{2,1,0:T(8,128)S(1)}, f32[2,48,128]{2,1,0:T(8,128)S(1)}, u32[]{:S(2)}, u32[]{:S(2)}) collective-permute-start(f32[2,48,128]{2,1,0:T(8,128)S(1)} %add.221), channel_id=1, source_target_pairs={{0,4},{1,5},{2,6},{3,7},{4,0},{5,1},{6,2},{7,3},{8,12},{9,13},{10,... | collective-permute-start | bytes 147464 | tf_op jit(solution)/shard_map/ppermute | solution.py:745
  212.5 5.5 %collective-permute-start.30 = (f32[48,128]{1,0:T(8,128)S(1)}, f32[48,128]{1,0:T(8,128)S(1)}, u32[]{:S(2)}, u32[]{:S(2)}) collective-permute-start(f32[48,128]{1,0:T(8,128)S(1)} %dynamic-slice_bitcast_fusion.2), channel_id=1, source_target_pairs={{0,16},{16,0},{1,17},{17,1},{2,18},{18,2},{3,19},{19,3},{4,20},{20... | collective-permute-start | bytes 73736 | tf_op jit(solution)/shard_map/ppermute | solution.py:745
  213.2 6.6 %collective-permute-start.29 = (bf16[464,384]{1,0:T(8,128)(2,1)S(1)}, bf16[464,384]{1,0:T(8,128)(2,1)S(1)}, u32[]{:S(2)}, u32[]{:S(2)}) collective-permute-start(bf16[464,384]{1,0:T(8,128)(2,1)S(1)} %maximum_select_fusion.5), channel_id=1, source_target_pairs={{0,2},{1,3},{2,0},{3,1},{4,6},{5,7},{6,4},{7,5},{8,10},{9,11},{10,... | collective-permute-start | bytes 1069064 | tf_op jit(solution)/shard_map/ppermute | solution.py:745
  213.8 14.4 %collective-permute-start.28 = (bf16[1536,384]{1,0:T(8,128)(2,1)S(1)}, bf16[1536,384]{1,0:T(8,128)(2,1)}, u32[]{:S(2)}, u32[]{:S(2)}) collective-permute-start(bf16[1536,384]{1,0:T(8,128)(2,1)S(1)} %maximum_select_fusion), channel_id=1, source_target_pairs={{0,1},{1,0},{2,3},{3,2},{4,5},{5,4},{6,7},{7,6},{8,9},{9,8},{10,11... | collective-permute-start | bytes 3538952 | tf_op jit(solution)/shard_map/ppermute | solution.py:745
  220.1 8.1 %collective-permute-start.31 = (bf16[928,384]{1,0:T(8,128)(2,1)S(1)}, bf16[928,384]{1,0:T(8,128)(2,1)}, u32[]{:S(2)}, u32[]{:S(2)}) collective-permute-start(bf16[928,384]{1,0:T(8,128)(2,1)S(1)} %maximum_select_fusion.3), channel_id=1, source_target_pairs={{0,1},{1,0},{2,3},{3,2},{4,5},{5,4},{6,7},{7,6},{8,9},{9,8},{10,11... | collective-permute-start | bytes 2138120 | tf_op jit(solution)/shard_map/ppermute | solution.py:745
where the time goes:
time: 237 us; the launch traced here: 236 us
  Pallas kernels  91.9 us (39%)
  waiting for transfers between devices  42.2 us (18%)
  starting transfers between devices  36.6 us (15%)
  local copies, waits for them, and re-layouts  23.4 us (10%)
  other arithmetic  20.7 us (9%)
  matrix products  19.4 us (8%)
    ppermute x32, waiting for transfers between devices, swap(): return lax.ppermute(block, axis, pairs)  42.2 us
    ppermute x32, starting transfers between devices, swap(): return lax.ppermute(block, axis, pairs)  36.6 us
    pallas_call x2, Pallas kernels, backward(): pl.pallas_call(functools.partial(backward_body, sizes, first_head, last),...  36 us
    pallas_call x1, Pallas kernels, forward(): pl.pallas_call(functools.partial(forward_body, sizes, tuple(lengths)), gr...  24 us
    pallas_call x1, Pallas kernels, gated(): pl.pallas_call(functools.partial(gated_body, sizes, tuple(lengths)), grid...  19.9 us
    dot_general x3, matrix products, mul_tn(): lax.dot_general(a, b, (((0,), (0,)), ((), ())), preferred_element_type=F32)  14.9 us
    pallas_call x1, Pallas kernels, input_backward(): pl.pallas_call(input_body, grid=(length // span,), in_specs=[SCALARS, dow...  11.9 us
    convert_element_type x11, other arithmetic, added(): return (keep.astype(F32) + got.astype(F32)).astype(BF16)  7.52 us
  transfers between devices with their start and end apart: 32, of which 16 were waited for; matrix products, arithmetic and copies ran while one was open for 13% of the time, Pallas kernels for 31%

commit v1 on v0

--- a/solution.py
+++ b/solution.py
@@ -11,7 +11,7 @@
 EPSILON = 1e-05
 LOG2E = math.log2(math.e)
 SPAN = 256
-STRETCH = 128
+STRETCH = 256
 GROUP = 8
 TILE = 256
 LANES = 128
@@ -73,6 +73,10 @@
 
 def sigmoid(v):
     return 0.5 * jnp.tanh(0.5 * v) + 0.5
+
+
+def decay_between(later, earlier):
+    return jnp.exp2(jnp.minimum(later - earlier, 0.0))
 
 
 def decays(step, rate2):
@@ -124,6 +128,7 @@
     width = inner // heads
     span = tokens_ref.shape[0]
     stretch = min(STRETCH, span)
+    half = stretch // 2
     copies = piece_copies(places_ref, lengths, pieces, weight, sems)
     kept = pltpu.make_async_copy(weight, weight_ref, sems.at[n_pieces])
 
@@ -201,9 +206,13 @@
                 row = slice(j, j + 1)
                 values = active_ref[rows, lanes].astype(F32)
                 stepped = (values * step_g[row]).astype(BF16)
-                decay = jnp.exp2(jnp.minimum(cum_g[row] - cum_c[:, row], 0.0))
-                weights = (scores * decay).astype(BF16)
-                scanned_ref[rows, lanes] = mul_nn(stepped, weights) + ec_g[row] * carried[rows, :]
+                early = (scores[:half] * decay_between(cum_g[row], cum_c[:half, row])).astype(BF16)
+                late = (scores[half:, half:] * decay_between(cum_g[row, half:], cum_c[half:, row])).astype(BF16)
+                inside = mul_nn(stepped[:, :half], early)
+                inside = jnp.concatenate(
+                    [inside[:, :half], inside[:, half:] + mul_nn(stepped[:, half:], late)], axis=1
+                )
+                scanned_ref[rows, lanes] = inside + ec_g[row] * carried[rows, :]
                 scaled[rows, :] = (values * factor_g[row]).astype(BF16)
 
         update[...] = mul_nt(scaled[...], b_in)
@@ -332,6 +341,7 @@
         d_active,
         sums,
         from_state,
+        push,
         scaled,
         d_scaled,
         d_scores,
@@ -352,6 +362,7 @@
     tiles = [(ref, before, t) for ref, before in zip(mixed_refs, before_refs) for t in range(ref.shape[1] // LANES)]
     first_tiles = [first_head * width // LANES, all_inner // LANES]
     stretch = min(STRETCH, span)
+    half = stretch // 2
     first_block = pl.program_id(0) == pl.num_programs(0) - 1
 
     @pl.when(pl.program_id(0) == 0)
@@ -390,7 +401,7 @@
             cum_g, step_g, factor_g, ec_g = cum_s[eight, :], step_s[eight, :], factor_s[eight, :], ec_s[eight, :]
             cum_c = as_columns(cum_g)
             pairs, directs, endings, dots = [], [], [], []
-            d_scores_g = d_scores[...]
+            d_early, d_late = d_scores[:half, :], d_scores[half:, half:]
             for j in range(GROUP):
                 h = group * GROUP + j
                 rows = pl.ds(pl.multiple_of(h * width, width), width)
@@ -399,10 +410,17 @@
                 stepped = (values * step_g[row]).astype(BF16)
                 low_d = d_scan_ref[rows, lanes]
                 d_scan = low_d.astype(F32)
-                decay = jnp.exp2(jnp.minimum(cum_g[row] - cum_c[:, row], 0.0))
-                weights = (scores * decay).astype(BF16)
-                inside = mul_nt(low_d, weights)
-                d_scores_g = d_scores_g + mul_tn(stepped, low_d) * decay
+                early = decay_between(cum_g[row], cum_c[:half, row])
+                late = decay_between(cum_g[row, half:], cum_c[half:, row])
+                inside = jnp.concatenate(
+                    [
+                        mul_nt(low_d, (scores[:half] * early).astype(BF16)),
+                        mul_nt(low_d[:, half:], (scores[half:, half:] * late).astype(BF16)),
+                    ],
+                    axis=1,
+                )
+                d_early = d_early + mul_tn(stepped[:, :half], low_d) * early
+                d_late = d_late + mul_tn(stepped[:, half:], low_d[:, half:]) * late
                 across = from_state[rows, :] * factor_g[row]
                 both = inside + across
                 d_active[rows, lanes] = step_g[row] * both + skip_ref[first_head + h] * d_scan
@@ -412,7 +430,8 @@
                 scaled[rows, :] = (values * (step_g[row] * factor_g[row])).astype(BF16)
                 d_scaled[rows, :] = (d_scan * ec_g[row]).astype(BF16)
                 dots.append(jnp.sum(d_state[rows, :] * states_ref[part, rows, :].astype(F32), axis=0, keepdims=True))
-            d_scores[...] = d_scores_g
+            d_scores[:half, :] = d_early
+            d_scores[half:, half:] = d_late
             pair_s[eight, :] = jnp.concatenate(pairs, axis=0)
             direct_s[eight, :] = jnp.concatenate(directs, axis=0)
             ending_s[eight, :] = jnp.concatenate(endings, axis=0)
@@ -428,7 +447,7 @@
         else:
             bc_out_ref[:state_dim, lanes] = d_b
             bc_out_ref[state_dim:, lanes] = d_c
-        from_state[...] = mul_nt(d_scaled[...], c_in)
+        push[...] = mul_nt(d_scaled[...], c_in)
 
         @pl.loop(0, heads // GROUP, unroll=HEADS_ABREAST)
         def _(group):
@@ -436,7 +455,7 @@
             total_g = total_s[eight, :]
             for j in range(GROUP):
                 rows = pl.ds(pl.multiple_of((group * GROUP + j) * width, width), width)
-                d_state[rows, :] = total_g[j : j + 1] * d_state[rows, :] + from_state[rows, :]
+                d_state[rows, :] = total_g[j : j + 1] * d_state[rows, :] + push[rows, :]
 
         d_log = (
             lane_sums(row_part_ref[:, lanes] - pair_s[...], ending)
@@ -700,6 +719,7 @@
             pltpu.VMEM((tiles * LANES, span), F32),
             pltpu.VMEM((5, tiles, 8, LANES), F32),
             pltpu.VMEM((inner, stretch), F32),
+            pltpu.VMEM((inner, state_dim), F32),
             pltpu.VMEM((inner, stretch), BF16),
             pltpu.VMEM((inner, stretch), BF16),
             pltpu.VMEM((stretch, stretch), F32),

time: 237 us -> 236 us (level)
  starting transfers between devices: 36.6 us -> 42.7 us
  Pallas kernels: 91.9 us -> 88 us
    ppermute x32, starting transfers between devices: 36.6 us -> 42.7 us  [swap(): return lax.ppermute(block, axis, pairs)]
    pallas_call x2, Pallas kernels: 36 us -> 32.7 us  [backward(): pl.pallas_call(functools.partial(backward_body, sizes, first_head, last),...]
    unnamed x39 -> x49, local copies, waits for them, and re-layouts: 4.69 us -> 4.88 us
  transfers between devices with their start and end apart: 32 -> 32, of which waited for: 16 -> 17; matrix products, arithmetic and copies ran while one was open for 13% -> 12% of each run, Pallas kernels for 31% -> 29%
where the time goes in v1:
time: 236 us
  Pallas kernels  88 us (37%)
  starting transfers between devices  42.7 us (18%)
  waiting for transfers between devices  40.4 us (17%)
  local copies, waits for them, and re-layouts  22.2 us (9%)
  matrix products  21.2 us (9%)
  other arithmetic  19.3 us (8%)
    ppermute x32, starting transfers between devices, swap(): return lax.ppermute(block, axis, pairs)  42.7 us
    ppermute x32, waiting for transfers between devices, swap(): return lax.ppermute(block, axis, pairs)  40.4 us
    pallas_call x2, Pallas kernels, backward(): pl.pallas_call(functools.partial(backward_body, sizes, first_head, last),...  32.7 us
    pallas_call x1, Pallas kernels, forward(): pl.pallas_call(functools.partial(forward_body, sizes, tuple(lengths)), gr...  23.6 us
    pallas_call x1, Pallas kernels, gated(): pl.pallas_call(functools.partial(gated_body, sizes, tuple(lengths)), grid...  19.8 us
    dot_general x3, matrix products, mul_tn(): lax.dot_general(a, b, (((0,), (0,)), ((), ())), preferred_element_type=F32)  16.6 us
    pallas_call x1, Pallas kernels, input_backward(): pl.pallas_call(input_body, grid=(length // span,), in_specs=[SCALARS, dow...  11.9 us
    convert_element_type x11, other arithmetic, added(): return (keep.astype(F32) + got.astype(F32)).astype(BF16)  7.51 us
  transfers between devices with their start and end apart: 32, of which 17 were waited for; matrix products, arithmetic and copies ran while one was open for 12% of the time, Pallas kernels for 29%

profile of v1, /device:TPU:1, one launch (start us, length us, event | category | flops | bytes accessed | tf_op | source)
XLA Modules:
  0.0 235.7 jit_solution(13435595796593186114)
XLA Ops:
  0.8 1.1 dynamic-slice_bitcast_fusion.1
  1.9 0.7 slice.102
  2.7 2.1 collective-permute-start
  5.1 1.1 dynamic-slice_bitcast_fusion
  6.2 8.8 %collective-permute-done.1 = bf16[7,896]{1,0:T(8,128)(2,1)S(1)} collective-permute-done((bf16[7,896]{1,0:T(8,128)(2,1)S(1)}, bf16[7,896]{1,0:T(8,128)(2,1)S(1)}, u32[]{:S(2)}, u32[]{:S(2)}) %collective-permute-start.1) | collective-permute-done | bytes 12576 | tf_op jit(solution)/shard_map/ppermute | solution.py:765
  15.6 1.1 collective-permute-start.2
  16.8 1.2 collective-permute-start.3
  20.1 5.9 %collective-permute-done.2.refs_3_ = bf16[576,384]{1,0:T(8,128)(2,1)S(1)} collective-permute-done((bf16[576,384]{1,0:T(8,128)(2,1)S(1)}, bf16[576,384]{1,0:T(8,128)(2,1)S(1)}, u32[]{:S(2)}, u32[]{:S(2)}) %collective-permute-start.2) | collective-permute-done | bytes 442400 | tf_op jit(solution)/shard_map/ppermute | solution.py:765
  26.6 2.7 %collective-permute-start.6 = (bf16[576,384]{1,0:T(8,128)(2,1)S(1)}, bf16[576,384]{1,0:T(8,128)(2,1)}, u32[]{:S(2)}, u32[]{:S(2)}) collective-permute-start(bf16[576,384]{1,0:T(8,128)(2,1)S(1)} %collective-permute-done.3.refs_5_), channel_id=1, source_target_pairs={{0,1},{1,0},{2,3},{3,2},{4,5},{5,4},{6,7},{7,6},{8,9},{9,8},{10,11... | collective-permute-start | bytes 1327112 | tf_op jit(solution)/shard_map/ppermute | solution.py:765
  30.6 0.7 copy.29.heads_ref.refs_10_.refs_12_
  32.2 23.6 %block_forward.1 = (bf16[1024,768]{1,0:T(8,128)(2,1)}, bf16[1024,1792]{1,0:T(8,128)(2,1)}, bf16[1792,1024]{1,0:T(8,128)(2,1)}, f32[24,1024]{1,0:T(8,128)}, bf16[...) custom-call(s32[14]{0:T(128)} %stack.60.places_ref, ...), custom_call_target="tpu_custom_call" | custom-call | flops 30000001024 | bytes 30000000 | tf_op jit(solution)/shard_map/block_forward/pallas_call | solution.py:531
  57.5 1.2 copy.30.inner_gain_ref
  58.7 0.8 copy-done.20
  59.6 19.8 %block_gated.1 = (bf16[1536,1024]{1,0:T(8,128)(2,1)}, bf16[1024,1536]{1,0:T(8,128)(2,1)}, bf16[1536,1024]{1,0:T(8,128)(2,1)}, f32[24,1024]{1,0:T(8,128)}, f32[24...) custom-call(s32[6]{0:T(128)} %stack.50.places_ref, f32[24]{0:T(128)} %reshape_squeeze.3.skip_ref.refs_0_, ...), custom_call_target="tpu_custom_call" | custom-call | flops 15000000512 | bytes 15000000 | tf_op jit(solution)/shard_map/block_gated/pallas_call | solution.py:588
  79.4 4.5 %convolution_convert_fusion.1 = bf16[1536,768]{1,0:T(8,128)(2,1)S(1)} fusion(bf16[1536,1024]{1,0:T(8,128)(2,1)} %get-tuple-element.98, f32[]{:T(128)} %bitcast.26, bf16[1,1,1024,768]{3,2,1,0:T(8,128)(2,1)S(1)} %copy-done.17), kind=kOutput, calls=%fused_computation.4 | convolution fusion | flops 2419458048 | bytes 7077892 | tf_op jit(solution)/shard_map/dot_general | solution.py:29
  83.9 1.4 copy-done.1
  85.7 5.2 %convolution_convert_fusion = bf16[1536,768]{1,0:T(8,128)(2,1)S(1)} fusion(bf16[1024,1536]{1,0:T(8,128)(2,1)} %get-tuple-element.99.d_gate_ref, bf16[1024,768]{1,0:T(8,128)(2,1)} %get-tuple-element.96), kind=kOutput, calls=%fused_computation.3 | convolution fusion | flops 2417098752 | bytes 7077888 | tf_op jit(solution)/shard_map/dot_general | solution.py:37
  90.9 1.6 add_convert_fusion.3
  92.5 1.0 constant_dynamic-slice_fusion.10
  93.4 1.1 constant_dynamic-slice_fusion.8
  95.4 2.3 collective-permute-done.10
  97.7 1.6 add_convert_fusion.2
  100.0 19.3 %block_backward.2 = (bf16[1024,2048]{1,0:T(8,128)(2,1)}, f32[16,1024]{1,0:T(8,128)}, f32[16,1024]{1,0:T(8,128)}, f32[5,8,128]{2,1,0:T(8,128)}, f32[256,1024]{1,0:T(8,128)}) custom-call(f32[24]{0:T(128)} %reshape_squeeze.3.skip_ref.refs_0_, bf16[1792,1024]{1,0:T(8,128)(2,1)} %get-tuple-element.94.refs_2_.refs_1_, ...), custom_call_target="tpu_custom_call" | custom-call | flops 20000000000 | bytes 20000000 | tf_op jit(solution)/shard_map/block_backward/pallas_call | solution.py:693
  119.3 3.2 %collective-permute-done.12 = bf16[768,384]{1,0:T(8,128)(2,1)S(1)} collective-permute-done((bf16[768,384]{1,0:T(8,128)(2,1)S(1)}, bf16[768,384]{1,0:T(8,128)(2,1)S(1)}, u32[]{:S(2)}, u32[]{:S(2)}) %collective-permute-start.12) | collective-permute-done | bytes 589856 | tf_op jit(solution)/shard_map/ppermute | solution.py:765
  122.9 1.3 collective-permute-start.13
  124.2 13.4 %block_backward.3 = (bf16[1024,2048]{1,0:T(8,128)(2,1)}, f32[8,1024]{1,0:T(8,128)}, f32[8,1024]{1,0:T(8,128)}, f32[5,6,128]{2,1,0:T(8,128)}) custom-call(f32[24]{0:T(128)} %reshape_squeeze.3.skip_ref.refs_0_, bf16[1792,1024]{1,0:T(8,128)(2,1)} %get-tuple-element.94.refs_2_.refs_1_, ...), custom_call_target="tpu_custom_call", output_to_operand_aliasing={{0}: (15, {})} | custom-call | flops 12000000000 | bytes 12000000 | tf_op jit(solution)/shard_map/block_backward/pallas_call | solution.py:693
  137.6 0.8 copy-done.4
  138.4 5.8 %fusion.2 = bf16[1856,768]{1,0:T(8,128)(2,1)S(1)} fusion(bf16[1024,768]{1,0:T(8,128)(2,1)} %get-tuple-element.96, bf16[1024,2048]{1,0:T(8,128)(2,1)} %get-tuple-element.122.d_rest_ref), kind=kOutput, calls=%fused_computation.5 | convolution fusion | flops 2920660992 | bytes 8355840 | tf_op jit(solution)/shard_map/dot_general | solution.py:37
  144.2 1.5 copy-done
  145.9 1.3 collective-permute-start.14
  147.2 3.0 %collective-permute-done.14 = bf16[928,768]{1,0:T(8,128)(2,1)} collective-permute-done((bf16[928,768]{1,0:T(8,128)(2,1)S(1)}, bf16[928,768]{1,0:T(8,128)(2,1)}, u32[]{:S(2)}, u32[]{:S(2)}) %collective-permute-start.14) | collective-permute-done | bytes 1425440 | tf_op jit(solution)/shard_map/ppermute | solution.py:765
  150.1 2.3 add_convert_fusion
  152.4 1.0 constant_dynamic-slice_fusion.3
  153.8 1.4 collective-permute-start.15
  155.2 5.7 %multiply_convert_fusion = bf16[1024,768]{1,0:T(8,128)(2,1)} fusion(bf16[1536,1024]{1,0:T(8,128)(2,1)S(1)} %copy-done.23, bf16[1536,768]{1,0:T(8,128)(2,1)} %get-tuple-element.119, f32[]{:T(128)} %bitcast.26, bf16[1,1,1024,768]{3,2,1,0:T(8,128)(2,1)S(1)} %copy-done.18), kind=kOutput, calls=%fused_computation.6 | convolution fusion | flops 2419064832 | bytes 8650756 | tf_op jit(solution)/shard_map/dot_general | solution.py:37
  160.9 0.9 reduce_sum.45
  161.8 0.7 reshape_transpose_reshape_broadcast_in_dim.15
  162.7 1.0 maximum_reduce_fusion
  163.8 0.8 pad_maximum_fusion.3
  165.3 2.4 %collective-permute-start.16 = (bf16[384,384]{1,0:T(8,128)(2,1)S(1)}, bf16[384,384]{1,0:T(8,128)(2,1)S(1)}, u32[]{:S(2)}, u32[]{:S(2)}) collective-permute-start(bf16[384,384]{1,0:T(8,128)(2,1)S(1)} %add_convert_fusion.8), channel_id=1, source_target_pairs={{0,8},{1,9},{2,10},{3,11},{4,12},{5,13},{6,14},{7,15},{8,0},{9,1},... | collective-permute-start | bytes 884744 | tf_op jit(solution)/shard_map/ppermute | solution.py:765
  167.7 11.9 %input_backward.1 = (f32[1024,768]{1,0:T(8,128)}, f32[8,768]{1,0:T(8,128)}) custom-call(f32[1]{0:T(128)} %bitcast.15.alive_ref, bf16[1024,768]{1,0:T(8,128)(2,1)} %bitcast.86, bf16[1024,768]{1,0:T(8,128)(2,1)} %bitcast.84, f32[1,768]{1,0:T(1,128)} %bitcast.82, bf16[1024,1536]{1,0:T(8,128)(2,1)} %get-tuple-element.99.d_gate_ref, ...), custom_call_target="tpu_custom_call" | custom-call | flops 8000000000 | bytes 8000000 | tf_op jit(solution)/shard_map/input_backward/pallas_call | solution.py:652
  179.6 0.7 reduce_sum.46
  180.5 0.8 collective-permute-done.16
  181.9 1.3 add_convert_fusion.4
  183.2 1.2 collective-permute-start.18
  184.4 0.8 collective-permute-start.19
  185.3 1.8 collective-permute-start.20
  187.1 0.9 collective-permute-done.20
  187.9 3.3 %collective-permute-done.19 = bf16[384,384]{1,0:T(8,128)(2,1)S(1)} collective-permute-done((bf16[384,384]{1,0:T(8,128)(2,1)S(1)}, bf16[384,384]{1,0:T(8,128)(2,1)S(1)}, u32[]{:S(2)}, u32[]{:S(2)}) %collective-permute-start.19) | collective-permute-done | bytes 294944 | tf_op jit(solution)/shard_map/ppermute | solution.py:765
  191.7 1.2 collective-permute-start.21
  192.9 1.1 collective-permute-start.22
  194.0 1.8 collective-permute-done.22
  196.1 2.4 %collective-permute-start.23 = (bf16[232,384]{1,0:T(8,128)(2,1)S(1)}, bf16[232,384]{1,0:T(8,128)(2,1)S(1)}, u32[]{:S(2)}, u32[]{:S(2)}) collective-permute-start(bf16[232,384]{1,0:T(8,128)(2,1)S(1)} %add_convert_fusion.10), channel_id=1, source_target_pairs={{0,8},{1,9},{2,10},{3,11},{4,12},{5,13},{6,14},{7,15},{8,0},{9,1},... | collective-permute-start | bytes 534536 | tf_op jit(solution)/shard_map/ppermute | solution.py:765
  198.7 1.2 collective-permute-start.27
  199.9 3.9 %collective-permute-done.24 = f32[2,48,128]{2,1,0:T(8,128)S(1)} collective-permute-done((f32[2,48,128]{2,1,0:T(8,128)S(1)}, f32[2,48,128]{2,1,0:T(8,128)S(1)}, u32[]{:S(2)}, u32[]{:S(2)}) %collective-permute-start.24) | collective-permute-done | bytes 49184 | tf_op jit(solution)/shard_map/ppermute | solution.py:765
  203.9 4.7 %collective-permute-start.25 = (bf16[232,384]{1,0:T(8,128)(2,1)S(1)}, bf16[232,384]{1,0:T(8,128)(2,1)S(1)}, u32[]{:S(2)}, u32[]{:S(2)}) collective-permute-start(bf16[232,384]{1,0:T(8,128)(2,1)S(1)} %add_convert_fusion.9), channel_id=1, source_target_pairs={{0,4},{1,5},{2,6},{3,7},{4,0},{5,1},{6,2},{7,3},{8,12},{9,13},{10,... | collective-permute-start | bytes 534536 | tf_op jit(solution)/shard_map/ppermute | solution.py:765
  208.7 3.6 %collective-permute-done.26 = f32[2,48,128]{2,1,0:T(8,128)S(1)} collective-permute-done((f32[2,48,128]{2,1,0:T(8,128)S(1)}, f32[2,48,128]{2,1,0:T(8,128)S(1)}, u32[]{:S(2)}, u32[]{:S(2)}) %collective-permute-start.26) | collective-permute-done | bytes 49184 | tf_op jit(solution)/shard_map/ppermute | solution.py:765
  213.0 1.2 collective-permute-start.29
  214.6 4.4 %collective-permute-start.28 = (bf16[1536,384]{1,0:T(8,128)(2,1)S(1)}, bf16[1536,384]{1,0:T(8,128)(2,1)}, u32[]{:S(2)}, u32[]{:S(2)}) collective-permute-start(bf16[1536,384]{1,0:T(8,128)(2,1)S(1)} %maximum_select_fusion), channel_id=1, source_target_pairs={{0,1},{1,0},{2,3},{3,2},{4,5},{5,4},{6,7},{7,6},{8,9},{9,8},{10,11... | collective-permute-start | bytes 3538952 | tf_op jit(solution)/shard_map/ppermute | solution.py:765
  219.9 5.0 %collective-permute-start.31 = (bf16[928,384]{1,0:T(8,128)(2,1)S(1)}, bf16[928,384]{1,0:T(8,128)(2,1)}, u32[]{:S(2)}, u32[]{:S(2)}) collective-permute-start(bf16[928,384]{1,0:T(8,128)(2,1)S(1)} %maximum_select_fusion.3), channel_id=1, source_target_pairs={{0,1},{1,0},{2,3},{3,2},{4,5},{5,4},{6,7},{7,6},{8,9},{9,8},{10,11... | collective-permute-start | bytes 2138120 | tf_op jit(solution)/shard_map/ppermute | solution.py:765
  227.9 1.4 fusion.16
  229.2 1.6 fusion.6
  230.9 1.7 fusion.7
  233.0 2.7 %convert_bitcast_fusion = f32[384,3352]{0,1:T(8,128)} fusion(bf16[1816,384]{1,0:T(8,128)(2,1)S(1)} %fusion.6, bf16[1536,384]{1,0:T(8,128)(2,1)S(1)} %maximum_select_fusion.1), kind=kLoop, calls=%fused_computation | loop fusion | flops 5148672 | bytes 7723008 | tf_op jit(solution)/shard_map/transpose | solution.py:1148
  (141 shorter events, 18.1 us)
Async XLA Ops:
  0.6 4.2 %copy-start.11 = (bf16[896]{0:T(1024)(128)(2,1)S(1)}, bf16[896]{0:T(1024)(128)(2,1)}, u32[]{:S(2)}) copy-start(bf16[896]{0:T(1024)(128)(2,1)} %param.17) | copy-start | bytes 5380
  0.7 4.2 %copy-start.10 = (bf16[768]{0:T(1024)(128)(2,1)S(1)}, bf16[768]{0:T(1024)(128)(2,1)}, u32[]{:S(2)}) copy-start(bf16[768]{0:T(1024)(128)(2,1)} %param.21) | copy-start | bytes 4612
  0.7 4.2 %copy-start.13 = (bf16[384]{0:T(512)(128)(2,1)S(1)}, bf16[384]{0:T(512)(128)(2,1)}, u32[]{:S(2)}) copy-start(bf16[384]{0:T(512)(128)(2,1)} %param.14) | copy-start | bytes 2308
  0.7 4.2 %copy-start.16 = (bf16[12]{0:T(256)(128)(2,1)S(1)}, bf16[12]{0:T(256)(128)(2,1)}, u32[]{:S(2)}) copy-start(bf16[12]{0:T(256)(128)(2,1)} %param.18) | copy-start | bytes 76
  0.7 4.2 %copy-start.15 = (bf16[12]{0:T(256)(128)(2,1)S(1)}, bf16[12]{0:T(256)(128)(2,1)}, u32[]{:S(2)}) copy-start(bf16[12]{0:T(256)(128)(2,1)} %param.19) | copy-start | bytes 76
  0.7 4.2 %copy-start.14 = (bf16[12]{0:T(256)(128)(2,1)S(1)}, bf16[12]{0:T(256)(128)(2,1)}, u32[]{:S(2)}) copy-start(bf16[12]{0:T(256)(128)(2,1)} %param.20) | copy-start | bytes 76
  0.7 4.3 %copy-start.9 = (bf16[896,4]{0,1:T(4,128)(2,1)S(1)}, bf16[896,4]{0,1:T(4,128)(2,1)}, u32[]{:S(2)}) copy-start(bf16[896,4]{0,1:T(4,128)(2,1)} %param.16) | copy-start | bytes 21508
  0.8 29.8 %copy-start.6 = (bf16[768,768]{1,0:T(8,128)(2,1)S(1)}, bf16[768,768]{1,0:T(8,128)(2,1)}, u32[]{:S(2)}) copy-start(bf16[768,768]{1,0:T(8,128)(2,1)} %refs_3_.1) | copy-start | bytes 3538948
  2.7 12.9 %collective-permute-start = (bf16[576,384]{1,0:T(8,128)(2,1)S(1)}, bf16[576,384]{1,0:T(8,128)(2,1)S(1)}, u32[]{:S(2)}, u32[]{:S(2)}) collective-permute-start(bf16[576,384]{1,0:T(8,128)(2,1)S(1)} %pad_maximum_fusion.2), channel_id=1, source_target_pairs={{0,16},{16,0},{1,17},{17,1},{2,18},{18,2},{3,19},{19,3},{4,20},{20... | collective-permute-start | bytes 1327112 | tf_op jit(solution)/shard_map/ppermute | solution.py:765
  5.0 10.0 %collective-permute-start.1 = (bf16[7,896]{1,0:T(8,128)(2,1)S(1)}, bf16[7,896]{1,0:T(8,128)(2,1)S(1)}, u32[]{:S(2)}, u32[]{:S(2)}) collective-permute-start(bf16[7,896]{1,0:T(8,128)(2,1)S(1)} %fusion.13), channel_id=1, source_target_pairs={{0,16},{16,0},{1,17},{17,1},{2,18},{18,2},{3,19},{19,3},{4,20},{20... | collective-permute-start | bytes 37640 | tf_op jit(solution)/shard_map/ppermute | solution.py:765
  15.6 16.6 %copy-start.12 = (bf16[576,384]{1,0:T(8,128)(2,1)}, bf16[576,384]{1,0:T(8,128)(2,1)S(1)}, u32[]{:S(2)}) copy-start(bf16[576,384]{1,0:T(8,128)(2,1)S(1)} %collective-permute-done.refs_1_) | copy-start | bytes 1327108
  15.6 10.4 %collective-permute-start.2 = (bf16[576,384]{1,0:T(8,128)(2,1)S(1)}, bf16[576,384]{1,0:T(8,128)(2,1)S(1)}, u32[]{:S(2)}, u32[]{:S(2)}) collective-permute-start(bf16[576,384]{1,0:T(8,128)(2,1)S(1)} %dynamic-slice_bitcast_fusion), channel_id=1, source_target_pairs={{0,16},{16,0},{1,17},{17,1},{2,18},{18,2},{3,19},{19,3},{4,20},{20... | collective-permute-start | bytes 1327112 | tf_op jit(solution)/shard_map/ppermute | solution.py:765
  16.8 9.8 %collective-permute-start.3 = (bf16[576,384]{1,0:T(8,128)(2,1)S(1)}, bf16[576,384]{1,0:T(8,128)(2,1)S(1)}, u32[]{:S(2)}, u32[]{:S(2)}) collective-permute-start(bf16[576,384]{1,0:T(8,128)(2,1)S(1)} %collective-permute-done.refs_1_), channel_id=1, source_target_pairs={{0,2},{1,3},{2,0},{3,1},{4,6},{5,7},{6,4},{7,5},{8,10},{9,11},{10,... | collective-permute-start | bytes 1327112 | tf_op jit(solution)/shard_map/ppermute | solution.py:765
  26.1 6.1 %copy-start.21 = (bf16[576,384]{1,0:T(8,128)(2,1)}, bf16[576,384]{1,0:T(8,128)(2,1)S(1)}, u32[]{:S(2)}) copy-start(bf16[576,384]{1,0:T(8,128)(2,1)S(1)} %collective-permute-done.2.refs_3_) | copy-start | bytes 1327108
  26.6 5.6 %copy-start.22 = (bf16[576,384]{1,0:T(8,128)(2,1)}, bf16[576,384]{1,0:T(8,128)(2,1)S(1)}, u32[]{:S(2)}) copy-start(bf16[576,384]{1,0:T(8,128)(2,1)S(1)} %collective-permute-done.3.refs_5_) | copy-start | bytes 1327108
  26.6 4.7 %collective-permute-start.6 = (bf16[576,384]{1,0:T(8,128)(2,1)S(1)}, bf16[576,384]{1,0:T(8,128)(2,1)}, u32[]{:S(2)}, u32[]{:S(2)}) collective-permute-start(bf16[576,384]{1,0:T(8,128)(2,1)S(1)} %collective-permute-done.3.refs_5_), channel_id=1, source_target_pairs={{0,1},{1,0},{2,3},{3,2},{4,5},{5,4},{6,7},{7,6},{8,9},{9,8},{10,11... | collective-permute-start | bytes 1327112 | tf_op jit(solution)/shard_map/ppermute | solution.py:765
  29.4 2.2 collective-permute-start.4
  29.4 2.8 %collective-permute-start.5 = (bf16[576,384]{1,0:T(8,128)(2,1)S(1)}, bf16[576,384]{1,0:T(8,128)(2,1)}, u32[]{:S(2)}, u32[]{:S(2)}) collective-permute-start(bf16[576,384]{1,0:T(8,128)(2,1)S(1)} %collective-permute-done.2.refs_3_), channel_id=1, source_target_pairs={{0,1},{1,0},{2,3},{3,2},{4,5},{5,4},{6,7},{7,6},{8,9},{9,8},{10,11... | collective-permute-start | bytes 1327112 | tf_op jit(solution)/shard_map/ppermute | solution.py:765
  31.3 24.5 %collective-permute-start.7 = (bf16[384,768]{1,0:T(8,128)(2,1)S(1)}, bf16[384,768]{1,0:T(8,128)(2,1)S(1)}, u32[]{:S(2)}, u32[]{:S(2)}) collective-permute-start(bf16[384,768]{1,0:T(8,128)(2,1)S(1)} %constant_dynamic-slice_fusion.12), channel_id=1, source_target_pairs={{0,16},{16,0},{1,17},{17,1},{2,18},{18,2},{3,19},{19,3},{4,20},{20... | collective-permute-start | bytes 1769480 | tf_op jit(solution)/shard_map/ppermute | solution.py:765
  55.8 2.9 %copy-start.19 = (bf16[384,768]{1,0:T(8,128)(2,1)}, bf16[384,768]{1,0:T(8,128)(2,1)S(1)}, u32[]{:S(2)}) copy-start(bf16[384,768]{1,0:T(8,128)(2,1)S(1)} %collective-permute-done.7.refs_4_) | copy-start | bytes 1769476
  55.8 2.9 %collective-permute-start.8 = (bf16[384,768]{1,0:T(8,128)(2,1)S(1)}, bf16[384,768]{1,0:T(8,128)(2,1)S(1)}, u32[]{:S(2)}, u32[]{:S(2)}) collective-permute-start(bf16[384,768]{1,0:T(8,128)(2,1)S(1)} %collective-permute-done.7.refs_4_), channel_id=1, source_target_pairs={{0,1},{1,0},{2,3},{3,2},{4,5},{5,4},{6,7},{7,6},{8,9},{9,8},{10,11... | collective-permute-start | bytes 1769480 | tf_op jit(solution)/shard_map/ppermute | solution.py:765
  58.7 0.8 copy-start.20
  59.6 19.8 %copy-start.17 = (bf16[1,1,1024,768]{3,2,1,0:T(8,128)(2,1)S(1)}, bf16[1,1,1024,768]{3,2,1,0:T(8,128)(2,1)}, u32[]{:S(2)}) copy-start(bf16[1,1,1024,768]{3,2,1,0:T(8,128)(2,1)} %param.23) | copy-start | bytes 4718596
  83.9 1.4 copy-start.1
  85.5 5.4 %collective-permute-start.9 = (bf16[1536,384]{1,0:T(8,128)(2,1)S(1)}, bf16[1536,384]{1,0:T(8,128)(2,1)}, u32[]{:S(2)}, u32[]{:S(2)}) collective-permute-start(bf16[1536,384]{1,0:T(8,128)(2,1)S(1)} %constant_dynamic-slice_fusion.11), channel_id=1, source_target_pairs={{0,1},{1,0},{2,3},{3,2},{4,5},{5,4},{6,7},{7,6},{8,9},{9,8},{10,11... | collective-permute-start | bytes 3538952 | tf_op jit(solution)/shard_map/ppermute | solution.py:765
  85.7 5.2 %copy-start.2 = (bf16[1536,768]{1,0:T(8,128)(2,1)S(1)}, bf16[1536,768]{1,0:T(8,128)(2,1)}, u32[]{:S(2)}) copy-start(bf16[1536,768]{1,0:T(8,128)(2,1)} %copy-done.1) | copy-start | bytes 7077892
  94.5 3.2 %collective-permute-start.10 = (bf16[768,768]{1,0:T(8,128)(2,1)}, bf16[768,768]{1,0:T(8,128)(2,1)}, u32[]{:S(2)}, u32[]{:S(2)}) collective-permute-start(bf16[768,768]{1,0:T(8,128)(2,1)} %constant_dynamic-slice_fusion.8), channel_id=1, source_target_pairs={{0,1},{1,0},{2,3},{3,2},{4,5},{5,4},{6,7},{7,6},{8,9},{9,8},{10,11... | collective-permute-start | bytes 3538952 | tf_op jit(solution)/shard_map/ppermute | solution.py:765
  94.9 24.4 %collective-permute-start.11 = (bf16[768,384]{1,0:T(8,128)(2,1)}, bf16[768,384]{1,0:T(8,128)(2,1)S(1)}, u32[]{:S(2)}, u32[]{:S(2)}) collective-permute-start(bf16[768,384]{1,0:T(8,128)(2,1)} %get-tuple-element.167), channel_id=1, source_target_pairs={{0,16},{16,0},{1,17},{17,1},{2,18},{18,2},{3,19},{19,3},{4,20},{20... | collective-permute-start | bytes 1769480 | tf_op jit(solution)/shard_map/ppermute | solution.py:765
  99.4 23.1 %collective-permute-start.12 = (bf16[768,384]{1,0:T(8,128)(2,1)S(1)}, bf16[768,384]{1,0:T(8,128)(2,1)S(1)}, u32[]{:S(2)}, u32[]{:S(2)}) collective-permute-start(bf16[768,384]{1,0:T(8,128)(2,1)S(1)} %get-tuple-element.164), channel_id=1, source_target_pairs={{0,16},{16,0},{1,17},{17,1},{2,18},{18,2},{3,19},{19,3},{4,20},{20... | collective-permute-start | bytes 1769480 | tf_op jit(solution)/shard_map/ppermute | solution.py:765
  122.9 14.7 %collective-permute-start.13 = (bf16[768,384]{1,0:T(8,128)(2,1)S(1)}, bf16[768,384]{1,0:T(8,128)(2,1)S(1)}, u32[]{:S(2)}, u32[]{:S(2)}) collective-permute-start(bf16[768,384]{1,0:T(8,128)(2,1)S(1)} %constant_dynamic-slice_fusion.5), channel_id=1, source_target_pairs={{0,2},{1,3},{2,0},{3,1},{4,6},{5,7},{6,4},{7,5},{8,10},{9,11},{10,... | collective-permute-start | bytes 1769480 | tf_op jit(solution)/shard_map/ppermute | solution.py:765
  137.6 0.8 copy-start.4
  144.2 1.6 copy-start
  145.9 4.3 %collective-permute-start.14 = (bf16[928,768]{1,0:T(8,128)(2,1)S(1)}, bf16[928,768]{1,0:T(8,128)(2,1)}, u32[]{:S(2)}, u32[]{:S(2)}) collective-permute-start(bf16[928,768]{1,0:T(8,128)(2,1)S(1)} %constant_dynamic-slice_fusion.4), channel_id=1, source_target_pairs={{0,1},{1,0},{2,3},{3,2},{4,5},{5,4},{6,7},{7,6},{8,9},{9,8},{10,11... | collective-permute-start | bytes 4276232 | tf_op jit(solution)/shard_map/ppermute | solution.py:765
  150.1 5.1 %copy-start.23 = (bf16[1536,1024]{1,0:T(8,128)(2,1)S(1)}, bf16[1536,1024]{1,0:T(8,128)(2,1)}, u32[]{:S(2)}) copy-start(bf16[1536,1024]{1,0:T(8,128)(2,1)} %get-tuple-element.98) | copy-start | bytes 9437188
  152.4 1.2 copy-start.5
  152.4 2.8 %copy-start.18 = (bf16[1,1,1024,768]{3,2,1,0:T(8,128)(2,1)S(1)}, bf16[1,1,1024,768]{3,2,1,0:T(8,128)(2,1)}, u32[]{:S(2)}) copy-start(bf16[1,1,1024,768]{3,2,1,0:T(8,128)(2,1)} %param.12) | copy-start | bytes 4718596
  153.8 11.4 %collective-permute-start.15 = (bf16[384,384]{1,0:T(8,128)(2,1)S(1)}, bf16[384,384]{1,0:T(8,128)(2,1)S(1)}, u32[]{:S(2)}, u32[]{:S(2)}) collective-permute-start(bf16[384,384]{1,0:T(8,128)(2,1)S(1)} %constant_dynamic-slice_fusion.2), channel_id=1, source_target_pairs={{0,4},{1,5},{2,6},{3,7},{4,0},{5,1},{6,2},{7,3},{8,12},{9,13},{10,... | collective-permute-start | bytes 884744 | tf_op jit(solution)/shard_map/ppermute | solution.py:765
  155.2 5.7 %copy-start.3 = (f32[1536,128]{1,0:T(8,128)S(1)}, f32[1536,128]{1,0:T(8,128)}, u32[]{:S(2)}) copy-start(f32[1536,128]{1,0:T(8,128)} %get-tuple-element.127) | copy-start | bytes 2359300
  155.2 7.3 %copy-start.7 = (f32[24,1024]{1,0:T(8,128)S(1)}, f32[24,1024]{1,0:T(8,128)}, u32[]{:S(2)}) copy-start(f32[24,1024]{1,0:T(8,128)} %get-tuple-element.132) | copy-start | bytes 294916
  155.2 7.5 %copy-start.8 = (f32[16,1024]{1,0:T(8,128)S(1)}, f32[16,1024]{1,0:T(8,128)}, u32[]{:S(2)}) copy-start(f32[16,1024]{1,0:T(8,128)} %get-tuple-element.113.refs_14_) | copy-start | bytes 196612
  164.6 17.2 %collective-permute-start.17 = (bf16[928,384]{1,0:T(8,128)(2,1)}, bf16[928,384]{1,0:T(8,128)(2,1)}, u32[]{:S(2)}, u32[]{:S(2)}) collective-permute-start(bf16[928,384]{1,0:T(8,128)(2,1)} %constant_dynamic-slice_fusion.3), channel_id=1, source_target_pairs={{0,16},{16,0},{1,17},{17,1},{2,18},{18,2},{3,19},{19,3},{4,20},{20... | collective-permute-start | bytes 2138120 | tf_op jit(solution)/shard_map/ppermute | solution.py:765
  165.3 16.0 %collective-permute-start.16 = (bf16[384,384]{1,0:T(8,128)(2,1)S(1)}, bf16[384,384]{1,0:T(8,128)(2,1)S(1)}, u32[]{:S(2)}, u32[]{:S(2)}) collective-permute-start(bf16[384,384]{1,0:T(8,128)(2,1)S(1)} %add_convert_fusion.8), channel_id=1, source_target_pairs={{0,8},{1,9},{2,10},{3,11},{4,12},{5,13},{6,14},{7,15},{8,0},{9,1},... | collective-permute-start | bytes 884744 | tf_op jit(solution)/shard_map/ppermute | solution.py:765
  183.2 8.4 %collective-permute-start.18 = (bf16[464,384]{1,0:T(8,128)(2,1)S(1)}, bf16[464,384]{1,0:T(8,128)(2,1)S(1)}, u32[]{:S(2)}, u32[]{:S(2)}) collective-permute-start(bf16[464,384]{1,0:T(8,128)(2,1)S(1)} %constant_dynamic-slice_fusion.1), channel_id=1, source_target_pairs={{0,2},{1,3},{2,0},{3,1},{4,6},{5,7},{6,4},{7,5},{8,10},{9,11},{10,... | collective-permute-start | bytes 1069064 | tf_op jit(solution)/shard_map/ppermute | solution.py:765
  184.4 6.8 %collective-permute-start.19 = (bf16[384,384]{1,0:T(8,128)(2,1)S(1)}, bf16[384,384]{1,0:T(8,128)(2,1)S(1)}, u32[]{:S(2)}, u32[]{:S(2)}) collective-permute-start(bf16[384,384]{1,0:T(8,128)(2,1)S(1)} %add_convert_fusion.7), channel_id=1, source_target_pairs={{0,4},{1,5},{2,6},{3,7},{4,0},{5,1},{6,2},{7,3},{8,12},{9,13},{10,... | collective-permute-start | bytes 884744 | tf_op jit(solution)/shard_map/ppermute | solution.py:765
  185.3 2.6 %collective-permute-start.20 = (f32[2,48,128]{2,1,0:T(8,128)S(1)}, f32[2,48,128]{2,1,0:T(8,128)S(1)}, u32[]{:S(2)}, u32[]{:S(2)}) collective-permute-start(f32[2,48,128]{2,1,0:T(8,128)S(1)} %bitcast.72), channel_id=1, source_target_pairs={{0,1},{1,0},{2,3},{3,2},{4,5},{5,4},{6,7},{7,6},{8,9},{9,8},{10,11... | collective-permute-start | bytes 147464 | tf_op jit(solution)/shard_map/ppermute | solution.py:765
  191.7 4.4 %collective-permute-start.21 = (bf16[232,384]{1,0:T(8,128)(2,1)S(1)}, bf16[232,384]{1,0:T(8,128)(2,1)S(1)}, u32[]{:S(2)}, u32[]{:S(2)}) collective-permute-start(bf16[232,384]{1,0:T(8,128)(2,1)S(1)} %constant_dynamic-slice_fusion), channel_id=1, source_target_pairs={{0,4},{1,5},{2,6},{3,7},{4,0},{5,1},{6,2},{7,3},{8,12},{9,13},{10,... | collective-permute-start | bytes 534536 | tf_op jit(solution)/shard_map/ppermute | solution.py:765
  192.9 2.9 %collective-permute-start.22 = (f32[2,48,128]{2,1,0:T(8,128)S(1)}, f32[2,48,128]{2,1,0:T(8,128)S(1)}, u32[]{:S(2)}, u32[]{:S(2)}) collective-permute-start(f32[2,48,128]{2,1,0:T(8,128)S(1)} %add.217), channel_id=1, source_target_pairs={{0,2},{1,3},{2,0},{3,1},{4,6},{5,7},{6,4},{7,5},{8,10},{9,11},{10,... | collective-permute-start | bytes 147464 | tf_op jit(solution)/shard_map/ppermute | solution.py:765
  196.1 7.7 %collective-permute-start.23 = (bf16[232,384]{1,0:T(8,128)(2,1)S(1)}, bf16[232,384]{1,0:T(8,128)(2,1)S(1)}, u32[]{:S(2)}, u32[]{:S(2)}) collective-permute-start(bf16[232,384]{1,0:T(8,128)(2,1)S(1)} %add_convert_fusion.10), channel_id=1, source_target_pairs={{0,8},{1,9},{2,10},{3,11},{4,12},{5,13},{6,14},{7,15},{8,0},{9,1},... | collective-permute-start | bytes 534536 | tf_op jit(solution)/shard_map/ppermute | solution.py:765
  198.7 13.6 %collective-permute-start.27 = (bf16[768,384]{1,0:T(8,128)(2,1)S(1)}, bf16[768,384]{1,0:T(8,128)(2,1)S(1)}, u32[]{:S(2)}, u32[]{:S(2)}) collective-permute-start(bf16[768,384]{1,0:T(8,128)(2,1)S(1)} %maximum_select_fusion.4), channel_id=1, source_target_pairs={{0,2},{1,3},{2,0},{3,1},{4,6},{5,7},{6,4},{7,5},{8,10},{9,11},{10,... | collective-permute-start | bytes 1769480 | tf_op jit(solution)/shard_map/ppermute | solution.py:765
  199.9 4.0 %collective-permute-start.24 = (f32[2,48,128]{2,1,0:T(8,128)S(1)}, f32[2,48,128]{2,1,0:T(8,128)S(1)}, u32[]{:S(2)}, u32[]{:S(2)}) collective-permute-start(f32[2,48,128]{2,1,0:T(8,128)S(1)} %add.219), channel_id=1, source_target_pairs={{0,8},{1,9},{2,10},{3,11},{4,12},{5,13},{6,14},{7,15},{8,0},{9,1},... | collective-permute-start | bytes 147464 | tf_op jit(solution)/shard_map/ppermute | solution.py:765
  203.9 8.4 %collective-permute-start.25 = (bf16[232,384]{1,0:T(8,128)(2,1)S(1)}, bf16[232,384]{1,0:T(8,128)(2,1)S(1)}, u32[]{:S(2)}, u32[]{:S(2)}) collective-permute-start(bf16[232,384]{1,0:T(8,128)(2,1)S(1)} %add_convert_fusion.9), channel_id=1, source_target_pairs={{0,4},{1,5},{2,6},{3,7},{4,0},{5,1},{6,2},{7,3},{8,12},{9,13},{10,... | collective-permute-start | bytes 534536 | tf_op jit(solution)/shard_map/ppermute | solution.py:765
  208.6 3.7 %collective-permute-start.26 = (f32[2,48,128]{2,1,0:T(8,128)S(1)}, f32[2,48,128]{2,1,0:T(8,128)S(1)}, u32[]{:S(2)}, u32[]{:S(2)}) collective-permute-start(f32[2,48,128]{2,1,0:T(8,128)S(1)} %add.221), channel_id=1, source_target_pairs={{0,4},{1,5},{2,6},{3,7},{4,0},{5,1},{6,2},{7,3},{8,12},{9,13},{10,... | collective-permute-start | bytes 147464 | tf_op jit(solution)/shard_map/ppermute | solution.py:765
  212.3 6.7 %collective-permute-start.30 = (f32[48,128]{1,0:T(8,128)S(1)}, f32[48,128]{1,0:T(8,128)S(1)}, u32[]{:S(2)}, u32[]{:S(2)}) collective-permute-start(f32[48,128]{1,0:T(8,128)S(1)} %dynamic-slice_bitcast_fusion.2), channel_id=1, source_target_pairs={{0,16},{16,0},{1,17},{17,1},{2,18},{18,2},{3,19},{19,3},{4,20},{20... | collective-permute-start | bytes 73736 | tf_op jit(solution)/shard_map/ppermute | solution.py:765
  213.0 6.6 %collective-permute-start.29 = (bf16[464,384]{1,0:T(8,128)(2,1)S(1)}, bf16[464,384]{1,0:T(8,128)(2,1)S(1)}, u32[]{:S(2)}, u32[]{:S(2)}) collective-permute-start(bf16[464,384]{1,0:T(8,128)(2,1)S(1)} %maximum_select_fusion.5), channel_id=1, source_target_pairs={{0,2},{1,3},{2,0},{3,1},{4,6},{5,7},{6,4},{7,5},{8,10},{9,11},{10,... | collective-permute-start | bytes 1069064 | tf_op jit(solution)/shard_map/ppermute | solution.py:765
  214.6 13.3 %collective-permute-start.28 = (bf16[1536,384]{1,0:T(8,128)(2,1)S(1)}, bf16[1536,384]{1,0:T(8,128)(2,1)}, u32[]{:S(2)}, u32[]{:S(2)}) collective-permute-start(bf16[1536,384]{1,0:T(8,128)(2,1)S(1)} %maximum_select_fusion), channel_id=1, source_target_pairs={{0,1},{1,0},{2,3},{3,2},{4,5},{5,4},{6,7},{7,6},{8,9},{9,8},{10,11... | collective-permute-start | bytes 3538952 | tf_op jit(solution)/shard_map/ppermute | solution.py:765
  219.9 8.0 %collective-permute-start.31 = (bf16[928,384]{1,0:T(8,128)(2,1)S(1)}, bf16[928,384]{1,0:T(8,128)(2,1)}, u32[]{:S(2)}, u32[]{:S(2)}) collective-permute-start(bf16[928,384]{1,0:T(8,128)(2,1)S(1)} %maximum_select_fusion.3), channel_id=1, source_target_pairs={{0,1},{1,0},{2,3},{3,2},{4,5},{5,4},{6,7},{7,6},{8,9},{9,8},{10,11... | collective-permute-start | bytes 2138120 | tf_op jit(solution)/shard_map/ppermute | solution.py:765

commit v2 on v1

--- a/solution.py
+++ b/solution.py
@@ -955,13 +955,15 @@
             return cut(term, core, 2, axis), swap(cut(term, 1 - core, 2, axis), "dp", 1)
 
         out_keep, out_got = by_cores(mul_nn(low_mixed, incoming).astype(BF16), 1)
-        gate_term = mul_tn(d_gate, normed).astype(BF16)
-        out_got, gate_term = together(out_got, gate_term)
+        gate_part = lambda c, left: mul_tn(cut(left, c, 2, 1), normed)
+        gate_sent = gate_part(1 - core, d_gate).astype(BF16)
+        out_got, gate_sent = together(out_got, gate_sent)
         out_block = added(out_keep, out_got)
         out_give = cut(out_block, 1 - mine, 2)
         got_out = across(out_give)
-        gate_keep, gate_got = by_cores(after(gate_term, out_give), 0)
-        gate_keep, gate_give = owned(added(gate_keep, gate_got))
+        gate_got = swap(gate_sent, "dp", 1)
+        gate_block = added(gate_part(core, after(d_gate, gate_sent, out_give)), gate_got)
+        gate_keep, gate_give = owned(gate_block)
         got_gate = across(gate_give)
         first = kernels[0]([], gate_give)
         got_out, got_gate, _ = together(got_out, got_gate, first[-1])

time: 236 us -> 233 us (0.987)
  starting transfers between devices: 42.7 us -> 38.4 us
  waiting for transfers between devices: 40.4 us -> 43.7 us
  local copies, waits for them, and re-layouts: 22.2 us -> 19.5 us
    ppermute x32, starting transfers between devices: 42.7 us -> 38.4 us  [swap(): return lax.ppermute(block, axis, pairs)]
    ppermute x32, waiting for transfers between devices: 40.4 us -> 43.7 us  [swap(): return lax.ppermute(block, axis, pairs)]
    dot_general x3 -> x4, matrix products: 16.6 us -> 17.3 us  [mul_tn(): lax.dot_general(a, b, (((0,), (0,)), ((), ())), preferred_element_type=F32)]
    convert_element_type x11 -> x10, other arithmetic: 7.51 us -> 7.08 us  [added(): return (keep.astype(F32) + got.astype(F32)).astype(BF16)]
  transfers between devices with their start and end apart: 32 -> 32, of which waited for: 17 -> 16; matrix products, arithmetic and copies ran while one was open for 12% -> 13% of each run, Pallas kernels for 29% -> 29%
where the time goes in v2:
time: 233 us
  Pallas kernels  87.9 us (38%)
  waiting for transfers between devices  43.7 us (19%)
  starting transfers between devices  38.4 us (16%)
  matrix products  22.3 us (10%)
  local copies, waits for them, and re-layouts  19.5 us (8%)
  other arithmetic  18.8 us (8%)
    ppermute x32, waiting for transfers between devices, swap(): return lax.ppermute(block, axis, pairs)  43.7 us
    ppermute x32, starting transfers between devices, swap(): return lax.ppermute(block, axis, pairs)  38.4 us
    pallas_call x2, Pallas kernels, backward(): pl.pallas_call(functools.partial(backward_body, sizes, first_head, last),...  32.7 us
    pallas_call x1, Pallas kernels, forward(): pl.pallas_call(functools.partial(forward_body, sizes, tuple(lengths)), gr...  23.6 us
    pallas_call x1, Pallas kernels, gated(): pl.pallas_call(functools.partial(gated_body, sizes, tuple(lengths)), grid...  19.7 us
    dot_general x4, matrix products, mul_tn(): lax.dot_general(a, b, (((0,), (0,)), ((), ())), preferred_element_type=F32)  17.3 us
    pallas_call x1, Pallas kernels, input_backward(): pl.pallas_call(input_body, grid=(length // span,), in_specs=[SCALARS, dow...  11.9 us
    convert_element_type x10, other arithmetic, added(): return (keep.astype(F32) + got.astype(F32)).astype(BF16)  7.08 us
  transfers between devices with their start and end apart: 32, of which 16 were waited for; matrix products, arithmetic and copies ran while one was open for 13% of the time, Pallas kernels for 29%

profile of v2, /device:TPU:1, one launch (start us, length us, event | category | flops | bytes accessed | tf_op | source)
XLA Modules:
  0.0 232.6 jit_solution(7533382923897950340)
XLA Ops:
  0.8 1.1 dynamic-slice_bitcast_fusion.1
  1.9 0.7 slice.102
  2.7 2.1 collective-permute-start
  5.1 1.1 dynamic-slice_bitcast_fusion
  6.2 8.8 %collective-permute-done.1 = bf16[7,896]{1,0:T(8,128)(2,1)S(1)} collective-permute-done((bf16[7,896]{1,0:T(8,128)(2,1)S(1)}, bf16[7,896]{1,0:T(8,128)(2,1)S(1)}, u32[]{:S(2)}, u32[]{:S(2)}) %collective-permute-start.1) | collective-permute-done | bytes 12576 | tf_op jit(solution)/shard_map/ppermute | solution.py:765
  15.6 1.1 collective-permute-start.2
  16.8 1.2 collective-permute-start.3
  18.9 0.6 pad_bitcast_fusion.taps_ref.refs_9_.refs_11_
  19.5 0.6 maximum_select_fusion.6.raw_weight_ref
  20.1 5.9 %collective-permute-done.2.refs_3_ = bf16[576,384]{1,0:T(8,128)(2,1)S(1)} collective-permute-done((bf16[576,384]{1,0:T(8,128)(2,1)S(1)}, bf16[576,384]{1,0:T(8,128)(2,1)S(1)}, u32[]{:S(2)}, u32[]{:S(2)}) %collective-permute-start.2) | collective-permute-done | bytes 442400 | tf_op jit(solution)/shard_map/ppermute | solution.py:765
  26.6 2.7 %collective-permute-start.6 = (bf16[576,384]{1,0:T(8,128)(2,1)S(1)}, bf16[576,384]{1,0:T(8,128)(2,1)}, u32[]{:S(2)}, u32[]{:S(2)}) collective-permute-start(bf16[576,384]{1,0:T(8,128)(2,1)S(1)} %collective-permute-done.3.refs_5_), channel_id=1, source_target_pairs={{0,1},{1,0},{2,3},{3,2},{4,5},{5,4},{6,7},{7,6},{8,9},{9,8},{10,11... | collective-permute-start | bytes 1327112 | tf_op jit(solution)/shard_map/ppermute | solution.py:765
  29.9 0.7 stack.60.places_ref
  30.6 0.7 copy.29.heads_ref.refs_10_.refs_12_
  32.2 23.6 %block_forward.1 = (bf16[1024,768]{1,0:T(8,128)(2,1)}, bf16[1024,1792]{1,0:T(8,128)(2,1)}, bf16[1792,1024]{1,0:T(8,128)(2,1)}, f32[24,1024]{1,0:T(8,128)}, bf16[...) custom-call(s32[14]{0:T(128)} %stack.60.places_ref, ...), custom_call_target="tpu_custom_call" | custom-call | flops 30000001024 | bytes 30000000 | tf_op jit(solution)/shard_map/block_forward/pallas_call | solution.py:531
  57.5 1.2 copy.30.inner_gain_ref
  58.7 0.8 copy-done.18
  59.6 19.7 %block_gated.1 = (bf16[1536,1024]{1,0:T(8,128)(2,1)}, bf16[1024,1536]{1,0:T(8,128)(2,1)}, bf16[1536,1024]{1,0:T(8,128)(2,1)}, f32[24,1024]{1,0:T(8,128)}, f32[24...) custom-call(s32[6]{0:T(128)} %stack.50.places_ref, f32[24]{0:T(128)} %reshape_squeeze.3.skip_ref.refs_0_, ...), custom_call_target="tpu_custom_call" | custom-call | flops 15000000512 | bytes 15000000 | tf_op jit(solution)/shard_map/block_gated/pallas_call | solution.py:588
  79.3 5.0 %convolution_convert_fusion = bf16[1536,768]{1,0:T(8,128)(2,1)S(1)} fusion(bf16[1536,1024]{1,0:T(8,128)(2,1)} %get-tuple-element.98, f32[]{:T(128)} %bitcast.26, bf16[1,1,1024,768]{3,2,1,0:T(8,128)(2,1)} %param.23), kind=kOutput, calls=%fused_computation.3 | convolution fusion | flops 2419458048 | bytes 7077892 | tf_op jit(solution)/shard_map/dot_general | solution.py:29
  84.6 4.3 %fusion.10 = bf16[768,768]{1,0:T(8,128)(2,1)} fusion(bf16[1024,768]{1,0:T(8,128)(2,1)} %get-tuple-element.96, bf16[1024,1536]{1,0:T(8,128)(2,1)} %get-tuple-element.102.d_gate_ref, s32[]{:T(128)S(6)} %select_n.203), kind=kOutput, calls=%fused_computation.16 | convolution fusion | flops 1208549376 | bytes 4325380 | tf_op jit(solution)/shard_map/dot_general | solution.py:37
  89.3 1.7 add_convert_fusion.3
  92.6 1.5 add_convert_fusion.2
  94.8 19.3 %block_backward.2 = (bf16[1024,2048]{1,0:T(8,128)(2,1)}, f32[16,1024]{1,0:T(8,128)}, f32[16,1024]{1,0:T(8,128)}, f32[5,8,128]{2,1,0:T(8,128)}, f32[256,1024]{1,0:T(8,128)}) custom-call(f32[24]{0:T(128)} %reshape_squeeze.3.skip_ref.refs_0_, bf16[1792,1024]{1,0:T(8,128)(2,1)} %get-tuple-element.94.refs_2_.refs_1_, ...), custom_call_target="tpu_custom_call" | custom-call | flops 20000000000 | bytes 20000000 | tf_op jit(solution)/shard_map/block_backward/pallas_call | solution.py:693
  114.1 4.6 %collective-permute-done.12 = bf16[768,384]{1,0:T(8,128)(2,1)S(1)} collective-permute-done((bf16[768,384]{1,0:T(8,128)(2,1)S(1)}, bf16[768,384]{1,0:T(8,128)(2,1)S(1)}, u32[]{:S(2)}, u32[]{:S(2)}) %collective-permute-start.12) | collective-permute-done | bytes 589856 | tf_op jit(solution)/shard_map/ppermute | solution.py:765
  119.1 1.3 collective-permute-start.13
  120.4 13.4 %block_backward.3 = (bf16[1024,2048]{1,0:T(8,128)(2,1)}, f32[8,1024]{1,0:T(8,128)}, f32[8,1024]{1,0:T(8,128)}, f32[5,6,128]{2,1,0:T(8,128)}) custom-call(f32[24]{0:T(128)} %reshape_squeeze.3.skip_ref.refs_0_, bf16[1792,1024]{1,0:T(8,128)(2,1)} %get-tuple-element.94.refs_2_.refs_1_, ...), custom_call_target="tpu_custom_call", output_to_operand_aliasing={{0}: (15, {})} | custom-call | flops 12000000000 | bytes 12000000 | tf_op jit(solution)/shard_map/block_backward/pallas_call | solution.py:693
  133.8 0.8 copy-done.2
  134.6 5.8 %fusion.2 = bf16[1856,768]{1,0:T(8,128)(2,1)S(1)} fusion(bf16[1024,768]{1,0:T(8,128)(2,1)} %get-tuple-element.96, bf16[1024,2048]{1,0:T(8,128)(2,1)} %get-tuple-element.122.d_rest_ref), kind=kOutput, calls=%fused_computation.4 | convolution fusion | flops 2920660992 | bytes 8355840 | tf_op jit(solution)/shard_map/dot_general | solution.py:37
  140.4 1.5 copy-done
  142.1 1.3 collective-permute-start.14
  143.4 3.0 %collective-permute-done.14 = bf16[928,768]{1,0:T(8,128)(2,1)} collective-permute-done((bf16[928,768]{1,0:T(8,128)(2,1)S(1)}, bf16[928,768]{1,0:T(8,128)(2,1)}, u32[]{:S(2)}, u32[]{:S(2)}) %collective-permute-start.14) | collective-permute-done | bytes 1425440 | tf_op jit(solution)/shard_map/ppermute | solution.py:765
  146.3 2.3 add_convert_fusion
  148.6 1.0 constant_dynamic-slice_fusion.3
  150.0 1.4 collective-permute-start.15
  151.4 5.7 %multiply_convert_fusion = bf16[1024,768]{1,0:T(8,128)(2,1)} fusion(bf16[1536,1024]{1,0:T(8,128)(2,1)S(1)} %copy-done.23, bf16[1536,768]{1,0:T(8,128)(2,1)} %get-tuple-element.119, f32[]{:T(128)} %bitcast.26, bf16[1,1,1024,768]{3,2,1,0:T(8,128)(2,1)S(1)} %copy-done.16), kind=kOutput, calls=%fused_computation.5 | convolution fusion | flops 2419064832 | bytes 8650756 | tf_op jit(solution)/shard_map/dot_general | solution.py:37
  157.1 0.9 reduce_sum.45
  158.0 0.7 reshape_transpose_reshape_broadcast_in_dim.15
  158.9 1.0 maximum_reduce_fusion
  160.0 0.8 pad_maximum_fusion.3
  161.5 2.4 %collective-permute-start.16 = (bf16[384,384]{1,0:T(8,128)(2,1)S(1)}, bf16[384,384]{1,0:T(8,128)(2,1)S(1)}, u32[]{:S(2)}, u32[]{:S(2)}) collective-permute-start(bf16[384,384]{1,0:T(8,128)(2,1)S(1)} %add_convert_fusion.8), channel_id=1, source_target_pairs={{0,8},{1,9},{2,10},{3,11},{4,12},{5,13},{6,14},{7,15},{8,0},{9,1},... | collective-permute-start | bytes 884744 | tf_op jit(solution)/shard_map/ppermute | solution.py:765
  163.8 11.9 %input_backward.1 = (f32[1024,768]{1,0:T(8,128)}, f32[8,768]{1,0:T(8,128)}) custom-call(f32[1]{0:T(128)} %bitcast.15.alive_ref, bf16[1024,768]{1,0:T(8,128)(2,1)} %bitcast.86, bf16[1024,768]{1,0:T(8,128)(2,1)} %bitcast.84, f32[1,768]{1,0:T(1,128)} %bitcast.82, bf16[1024,1536]{1,0:T(8,128)(2,1)} %get-tuple-element.102.d_gate_ref, ...), custom_call_target="tpu_custom_call" | custom-call | flops 8000000000 | bytes 8000000 | tf_op jit(solution)/shard_map/input_backward/pallas_call | solution.py:652
  175.8 0.7 reduce_sum.46
  176.7 0.8 collective-permute-done.16
  178.1 1.3 add_convert_fusion.4
  179.4 1.2 collective-permute-start.18
  180.6 1.0 add_convert_fusion.7
  181.6 0.8 collective-permute-start.19
  182.5 1.8 collective-permute-start.20
  184.2 0.9 collective-permute-done.20
  185.1 3.3 %collective-permute-done.19 = bf16[384,384]{1,0:T(8,128)(2,1)S(1)} collective-permute-done((bf16[384,384]{1,0:T(8,128)(2,1)S(1)}, bf16[384,384]{1,0:T(8,128)(2,1)S(1)}, u32[]{:S(2)}, u32[]{:S(2)}) %collective-permute-start.19) | collective-permute-done | bytes 294944 | tf_op jit(solution)/shard_map/ppermute | solution.py:765
  188.5 1.2 collective-permute-start.21
  190.2 2.5 %collective-permute-done.22 = f32[2,48,128]{2,1,0:T(8,128)S(1)} collective-permute-done((f32[2,48,128]{2,1,0:T(8,128)S(1)}, f32[2,48,128]{2,1,0:T(8,128)S(1)}, u32[]{:S(2)}, u32[]{:S(2)}) %collective-permute-start.22) | collective-permute-done | bytes 49184 | tf_op jit(solution)/shard_map/ppermute | solution.py:765
  193.0 2.4 %collective-permute-start.23 = (bf16[232,384]{1,0:T(8,128)(2,1)S(1)}, bf16[232,384]{1,0:T(8,128)(2,1)S(1)}, u32[]{:S(2)}, u32[]{:S(2)}) collective-permute-start(bf16[232,384]{1,0:T(8,128)(2,1)S(1)} %add_convert_fusion.10), channel_id=1, source_target_pairs={{0,8},{1,9},{2,10},{3,11},{4,12},{5,13},{6,14},{7,15},{8,0},{9,1},... | collective-permute-start | bytes 534536 | tf_op jit(solution)/shard_map/ppermute | solution.py:765
  196.1 7.0 %collective-permute-done.24 = f32[2,48,128]{2,1,0:T(8,128)S(1)} collective-permute-done((f32[2,48,128]{2,1,0:T(8,128)S(1)}, f32[2,48,128]{2,1,0:T(8,128)S(1)}, u32[]{:S(2)}, u32[]{:S(2)}) %collective-permute-start.24) | collective-permute-done | bytes 49184 | tf_op jit(solution)/shard_map/ppermute | solution.py:765
  203.3 1.4 collective-permute-start.26
  204.7 4.1 %collective-permute-done.26 = f32[2,48,128]{2,1,0:T(8,128)S(1)} collective-permute-done((f32[2,48,128]{2,1,0:T(8,128)S(1)}, f32[2,48,128]{2,1,0:T(8,128)S(1)}, u32[]{:S(2)}, u32[]{:S(2)}) %collective-permute-start.26) | collective-permute-done | bytes 49184 | tf_op jit(solution)/shard_map/ppermute | solution.py:765
  208.8 0.7 collective-permute-start.30
  210.7 4.7 %collective-permute-start.28 = (bf16[1536,384]{1,0:T(8,128)(2,1)S(1)}, bf16[1536,384]{1,0:T(8,128)(2,1)}, u32[]{:S(2)}, u32[]{:S(2)}) collective-permute-start(bf16[1536,384]{1,0:T(8,128)(2,1)S(1)} %maximum_select_fusion), channel_id=1, source_target_pairs={{0,1},{1,0},{2,3},{3,2},{4,5},{5,4},{6,7},{7,6},{8,9},{9,8},{10,11... | collective-permute-start | bytes 3538952 | tf_op jit(solution)/shard_map/ppermute | solution.py:765
  215.5 0.7 collective-permute-done.29
  216.5 5.3 %collective-permute-start.31 = (bf16[928,384]{1,0:T(8,128)(2,1)S(1)}, bf16[928,384]{1,0:T(8,128)(2,1)}, u32[]{:S(2)}, u32[]{:S(2)}) collective-permute-start(bf16[928,384]{1,0:T(8,128)(2,1)S(1)} %maximum_select_fusion.3), channel_id=1, source_target_pairs={{0,1},{1,0},{2,3},{3,2},{4,5},{5,4},{6,7},{7,6},{8,9},{9,8},{10,11... | collective-permute-start | bytes 2138120 | tf_op jit(solution)/shard_map/ppermute | solution.py:765
  222.4 0.6 slice.90
  224.8 1.4 fusion.27
  226.2 1.6 fusion.15
  227.8 1.7 fusion.16
  229.9 2.7 %convert_bitcast_fusion = f32[384,3352]{0,1:T(8,128)} fusion(bf16[1816,384]{1,0:T(8,128)(2,1)S(1)} %fusion.15, bf16[1536,384]{1,0:T(8,128)(2,1)S(1)} %maximum_select_fusion.1), kind=kLoop, calls=%fused_computation | loop fusion | flops 5148672 | bytes 7723008 | tf_op jit(solution)/shard_map/transpose | solution.py:1150
  (140 shorter events, 16.7 us)
Async XLA Ops:
  0.6 4.2 %copy-start.10 = (bf16[896]{0:T(1024)(128)(2,1)S(1)}, bf16[896]{0:T(1024)(128)(2,1)}, u32[]{:S(2)}) copy-start(bf16[896]{0:T(1024)(128)(2,1)} %param.17) | copy-start | bytes 5380
  0.7 4.2 %copy-start.9 = (bf16[768]{0:T(1024)(128)(2,1)S(1)}, bf16[768]{0:T(1024)(128)(2,1)}, u32[]{:S(2)}) copy-start(bf16[768]{0:T(1024)(128)(2,1)} %param.21) | copy-start | bytes 4612
  0.7 4.2 %copy-start.12 = (bf16[384]{0:T(512)(128)(2,1)S(1)}, bf16[384]{0:T(512)(128)(2,1)}, u32[]{:S(2)}) copy-start(bf16[384]{0:T(512)(128)(2,1)} %param.14) | copy-start | bytes 2308
  0.7 4.2 %copy-start.15 = (bf16[12]{0:T(256)(128)(2,1)S(1)}, bf16[12]{0:T(256)(128)(2,1)}, u32[]{:S(2)}) copy-start(bf16[12]{0:T(256)(128)(2,1)} %param.18) | copy-start | bytes 76
  0.7 4.2 %copy-start.14 = (bf16[12]{0:T(256)(128)(2,1)S(1)}, bf16[12]{0:T(256)(128)(2,1)}, u32[]{:S(2)}) copy-start(bf16[12]{0:T(256)(128)(2,1)} %param.19) | copy-start | bytes 76
  0.7 4.2 %copy-start.13 = (bf16[12]{0:T(256)(128)(2,1)S(1)}, bf16[12]{0:T(256)(128)(2,1)}, u32[]{:S(2)}) copy-start(bf16[12]{0:T(256)(128)(2,1)} %param.20) | copy-start | bytes 76
  0.7 4.3 %copy-start.8 = (bf16[896,4]{0,1:T(4,128)(2,1)S(1)}, bf16[896,4]{0,1:T(4,128)(2,1)}, u32[]{:S(2)}) copy-start(bf16[896,4]{0,1:T(4,128)(2,1)} %param.16) | copy-start | bytes 21508
  0.8 29.8 %copy-start.5 = (bf16[768,768]{1,0:T(8,128)(2,1)S(1)}, bf16[768,768]{1,0:T(8,128)(2,1)}, u32[]{:S(2)}) copy-start(bf16[768,768]{1,0:T(8,128)(2,1)} %refs_3_.1) | copy-start | bytes 3538948
  2.7 12.9 %collective-permute-start = (bf16[576,384]{1,0:T(8,128)(2,1)S(1)}, bf16[576,384]{1,0:T(8,128)(2,1)S(1)}, u32[]{:S(2)}, u32[]{:S(2)}) collective-permute-start(bf16[576,384]{1,0:T(8,128)(2,1)S(1)} %pad_maximum_fusion.2), channel_id=1, source_target_pairs={{0,16},{16,0},{1,17},{17,1},{2,18},{18,2},{3,19},{19,3},{4,20},{20... | collective-permute-start | bytes 1327112 | tf_op jit(solution)/shard_map/ppermute | solution.py:765
  5.0 10.0 %collective-permute-start.1 = (bf16[7,896]{1,0:T(8,128)(2,1)S(1)}, bf16[7,896]{1,0:T(8,128)(2,1)S(1)}, u32[]{:S(2)}, u32[]{:S(2)}) collective-permute-start(bf16[7,896]{1,0:T(8,128)(2,1)S(1)} %fusion.22), channel_id=1, source_target_pairs={{0,16},{16,0},{1,17},{17,1},{2,18},{18,2},{3,19},{19,3},{4,20},{20... | collective-permute-start | bytes 37640 | tf_op jit(solution)/shard_map/ppermute | solution.py:765
  15.6 16.6 %copy-start.11 = (bf16[576,384]{1,0:T(8,128)(2,1)}, bf16[576,384]{1,0:T(8,128)(2,1)S(1)}, u32[]{:S(2)}) copy-start(bf16[576,384]{1,0:T(8,128)(2,1)S(1)} %collective-permute-done.refs_1_) | copy-start | bytes 1327108
  15.6 10.4 %collective-permute-start.2 = (bf16[576,384]{1,0:T(8,128)(2,1)S(1)}, bf16[576,384]{1,0:T(8,128)(2,1)S(1)}, u32[]{:S(2)}, u32[]{:S(2)}) collective-permute-start(bf16[576,384]{1,0:T(8,128)(2,1)S(1)} %dynamic-slice_bitcast_fusion), channel_id=1, source_target_pairs={{0,16},{16,0},{1,17},{17,1},{2,18},{18,2},{3,19},{19,3},{4,20},{20... | collective-permute-start | bytes 1327112 | tf_op jit(solution)/shard_map/ppermute | solution.py:765
  16.8 9.8 %collective-permute-start.3 = (bf16[576,384]{1,0:T(8,128)(2,1)S(1)}, bf16[576,384]{1,0:T(8,128)(2,1)S(1)}, u32[]{:S(2)}, u32[]{:S(2)}) collective-permute-start(bf16[576,384]{1,0:T(8,128)(2,1)S(1)} %collective-permute-done.refs_1_), channel_id=1, source_target_pairs={{0,2},{1,3},{2,0},{3,1},{4,6},{5,7},{6,4},{7,5},{8,10},{9,11},{10,... | collective-permute-start | bytes 1327112 | tf_op jit(solution)/shard_map/ppermute | solution.py:765
  26.1 6.1 %copy-start.19 = (bf16[576,384]{1,0:T(8,128)(2,1)}, bf16[576,384]{1,0:T(8,128)(2,1)S(1)}, u32[]{:S(2)}) copy-start(bf16[576,384]{1,0:T(8,128)(2,1)S(1)} %collective-permute-done.2.refs_3_) | copy-start | bytes 1327108
  26.6 5.6 %copy-start.20 = (bf16[576,384]{1,0:T(8,128)(2,1)}, bf16[576,384]{1,0:T(8,128)(2,1)S(1)}, u32[]{:S(2)}) copy-start(bf16[576,384]{1,0:T(8,128)(2,1)S(1)} %collective-permute-done.3.refs_5_) | copy-start | bytes 1327108
  26.6 4.7 %collective-permute-start.6 = (bf16[576,384]{1,0:T(8,128)(2,1)S(1)}, bf16[576,384]{1,0:T(8,128)(2,1)}, u32[]{:S(2)}, u32[]{:S(2)}) collective-permute-start(bf16[576,384]{1,0:T(8,128)(2,1)S(1)} %collective-permute-done.3.refs_5_), channel_id=1, source_target_pairs={{0,1},{1,0},{2,3},{3,2},{4,5},{5,4},{6,7},{7,6},{8,9},{9,8},{10,11... | collective-permute-start | bytes 1327112 | tf_op jit(solution)/shard_map/ppermute | solution.py:765
  29.4 2.2 collective-permute-start.4
  29.4 2.8 %collective-permute-start.5 = (bf16[576,384]{1,0:T(8,128)(2,1)S(1)}, bf16[576,384]{1,0:T(8,128)(2,1)}, u32[]{:S(2)}, u32[]{:S(2)}) collective-permute-start(bf16[576,384]{1,0:T(8,128)(2,1)S(1)} %collective-permute-done.2.refs_3_), channel_id=1, source_target_pairs={{0,1},{1,0},{2,3},{3,2},{4,5},{5,4},{6,7},{7,6},{8,9},{9,8},{10,11... | collective-permute-start | bytes 1327112 | tf_op jit(solution)/shard_map/ppermute | solution.py:765
  31.3 24.5 %collective-permute-start.7 = (bf16[384,768]{1,0:T(8,128)(2,1)S(1)}, bf16[384,768]{1,0:T(8,128)(2,1)S(1)}, u32[]{:S(2)}, u32[]{:S(2)}) collective-permute-start(bf16[384,768]{1,0:T(8,128)(2,1)S(1)} %constant_dynamic-slice_fusion.11), channel_id=1, source_target_pairs={{0,16},{16,0},{1,17},{17,1},{2,18},{18,2},{3,19},{19,3},{4,20},{20... | collective-permute-start | bytes 1769480 | tf_op jit(solution)/shard_map/ppermute | solution.py:765
  55.8 2.9 %copy-start.17 = (bf16[384,768]{1,0:T(8,128)(2,1)}, bf16[384,768]{1,0:T(8,128)(2,1)S(1)}, u32[]{:S(2)}) copy-start(bf16[384,768]{1,0:T(8,128)(2,1)S(1)} %collective-permute-done.7.refs_4_) | copy-start | bytes 1769476
  55.8 2.9 %collective-permute-start.8 = (bf16[384,768]{1,0:T(8,128)(2,1)S(1)}, bf16[384,768]{1,0:T(8,128)(2,1)S(1)}, u32[]{:S(2)}, u32[]{:S(2)}) collective-permute-start(bf16[384,768]{1,0:T(8,128)(2,1)S(1)} %collective-permute-done.7.refs_4_), channel_id=1, source_target_pairs={{0,1},{1,0},{2,3},{3,2},{4,5},{5,4},{6,7},{7,6},{8,9},{9,8},{10,11... | collective-permute-start | bytes 1769480 | tf_op jit(solution)/shard_map/ppermute | solution.py:765
  58.7 0.8 copy-start.18
  84.4 4.5 %collective-permute-start.9 = (bf16[1536,384]{1,0:T(8,128)(2,1)S(1)}, bf16[1536,384]{1,0:T(8,128)(2,1)}, u32[]{:S(2)}, u32[]{:S(2)}) collective-permute-start(bf16[1536,384]{1,0:T(8,128)(2,1)S(1)} %constant_dynamic-slice_fusion.10), channel_id=1, source_target_pairs={{0,1},{1,0},{2,3},{3,2},{4,5},{5,4},{6,7},{7,6},{8,9},{9,8},{10,11... | collective-permute-start | bytes 3538952 | tf_op jit(solution)/shard_map/ppermute | solution.py:765
  88.9 3.1 %collective-permute-start.10 = (bf16[768,768]{1,0:T(8,128)(2,1)}, bf16[768,768]{1,0:T(8,128)(2,1)S(1)}, u32[]{:S(2)}, u32[]{:S(2)}) collective-permute-start(bf16[768,768]{1,0:T(8,128)(2,1)} %fusion.10), channel_id=1, source_target_pairs={{0,1},{1,0},{2,3},{3,2},{4,5},{5,4},{6,7},{7,6},{8,9},{9,8},{10,11... | collective-permute-start | bytes 3538952 | tf_op jit(solution)/shard_map/ppermute | solution.py:765
  89.3 2.7 %copy-start.21 = (bf16[1024,1536]{1,0:T(8,128)(2,1)S(1)}, bf16[1024,1536]{1,0:T(8,128)(2,1)}, u32[]{:S(2)}) copy-start(bf16[1024,1536]{1,0:T(8,128)(2,1)} %get-tuple-element.102.d_gate_ref) | copy-start | bytes 9437188
  91.1 1.5 copy-start.22
  91.2 22.9 %collective-permute-start.11 = (bf16[768,384]{1,0:T(8,128)(2,1)S(1)}, bf16[768,384]{1,0:T(8,128)(2,1)S(1)}, u32[]{:S(2)}, u32[]{:S(2)}) collective-permute-start(bf16[768,384]{1,0:T(8,128)(2,1)S(1)} %get-tuple-element.167), channel_id=1, source_target_pairs={{0,16},{16,0},{1,17},{17,1},{2,18},{18,2},{3,19},{19,3},{4,20},{20... | collective-permute-start | bytes 1769480 | tf_op jit(solution)/shard_map/ppermute | solution.py:765
  94.3 24.4 %collective-permute-start.12 = (bf16[768,384]{1,0:T(8,128)(2,1)S(1)}, bf16[768,384]{1,0:T(8,128)(2,1)S(1)}, u32[]{:S(2)}, u32[]{:S(2)}) collective-permute-start(bf16[768,384]{1,0:T(8,128)(2,1)S(1)} %get-tuple-element.164), channel_id=1, source_target_pairs={{0,16},{16,0},{1,17},{17,1},{2,18},{18,2},{3,19},{19,3},{4,20},{20... | collective-permute-start | bytes 1769480 | tf_op jit(solution)/shard_map/ppermute | solution.py:765
  119.1 14.7 %collective-permute-start.13 = (bf16[768,384]{1,0:T(8,128)(2,1)S(1)}, bf16[768,384]{1,0:T(8,128)(2,1)S(1)}, u32[]{:S(2)}, u32[]{:S(2)}) collective-permute-start(bf16[768,384]{1,0:T(8,128)(2,1)S(1)} %constant_dynamic-slice_fusion.5), channel_id=1, source_target_pairs={{0,2},{1,3},{2,0},{3,1},{4,6},{5,7},{6,4},{7,5},{8,10},{9,11},{10,... | collective-permute-start | bytes 1769480 | tf_op jit(solution)/shard_map/ppermute | solution.py:765
  133.8 0.8 copy-start.2
  140.4 1.6 copy-start
  142.1 4.3 %collective-permute-start.14 = (bf16[928,768]{1,0:T(8,128)(2,1)S(1)}, bf16[928,768]{1,0:T(8,128)(2,1)}, u32[]{:S(2)}, u32[]{:S(2)}) collective-permute-start(bf16[928,768]{1,0:T(8,128)(2,1)S(1)} %constant_dynamic-slice_fusion.4), channel_id=1, source_target_pairs={{0,1},{1,0},{2,3},{3,2},{4,5},{5,4},{6,7},{7,6},{8,9},{9,8},{10,11... | collective-permute-start | bytes 4276232 | tf_op jit(solution)/shard_map/ppermute | solution.py:765
  146.3 5.1 %copy-start.23 = (bf16[1536,1024]{1,0:T(8,128)(2,1)S(1)}, bf16[1536,1024]{1,0:T(8,128)(2,1)}, u32[]{:S(2)}) copy-start(bf16[1536,1024]{1,0:T(8,128)(2,1)} %get-tuple-element.98) | copy-start | bytes 9437188
  148.6 1.2 copy-start.3
  148.6 2.8 %copy-start.16 = (bf16[1,1,1024,768]{3,2,1,0:T(8,128)(2,1)S(1)}, bf16[1,1,1024,768]{3,2,1,0:T(8,128)(2,1)}, u32[]{:S(2)}) copy-start(bf16[1,1,1024,768]{3,2,1,0:T(8,128)(2,1)} %param.12) | copy-start | bytes 4718596
  150.0 11.4 %collective-permute-start.15 = (bf16[384,384]{1,0:T(8,128)(2,1)S(1)}, bf16[384,384]{1,0:T(8,128)(2,1)S(1)}, u32[]{:S(2)}, u32[]{:S(2)}) collective-permute-start(bf16[384,384]{1,0:T(8,128)(2,1)S(1)} %constant_dynamic-slice_fusion.2), channel_id=1, source_target_pairs={{0,4},{1,5},{2,6},{3,7},{4,0},{5,1},{6,2},{7,3},{8,12},{9,13},{10,... | collective-permute-start | bytes 884744 | tf_op jit(solution)/shard_map/ppermute | solution.py:765
  151.4 5.7 %copy-start.1 = (f32[1536,128]{1,0:T(8,128)S(1)}, f32[1536,128]{1,0:T(8,128)}, u32[]{:S(2)}) copy-start(f32[1536,128]{1,0:T(8,128)} %get-tuple-element.127) | copy-start | bytes 2359300
  151.4 7.3 %copy-start.6 = (f32[24,1024]{1,0:T(8,128)S(1)}, f32[24,1024]{1,0:T(8,128)}, u32[]{:S(2)}) copy-start(f32[24,1024]{1,0:T(8,128)} %get-tuple-element.132) | copy-start | bytes 294916
  151.4 7.5 %copy-start.7 = (f32[16,1024]{1,0:T(8,128)S(1)}, f32[16,1024]{1,0:T(8,128)}, u32[]{:S(2)}) copy-start(f32[16,1024]{1,0:T(8,128)} %get-tuple-element.113.refs_14_) | copy-start | bytes 196612
  160.8 17.2 %collective-permute-start.17 = (bf16[928,384]{1,0:T(8,128)(2,1)}, bf16[928,384]{1,0:T(8,128)(2,1)}, u32[]{:S(2)}, u32[]{:S(2)}) collective-permute-start(bf16[928,384]{1,0:T(8,128)(2,1)} %constant_dynamic-slice_fusion.3), channel_id=1, source_target_pairs={{0,16},{16,0},{1,17},{17,1},{2,18},{18,2},{3,19},{19,3},{4,20},{20... | collective-permute-start | bytes 2138120 | tf_op jit(solution)/shard_map/ppermute | solution.py:765
  161.5 16.0 %collective-permute-start.16 = (bf16[384,384]{1,0:T(8,128)(2,1)S(1)}, bf16[384,384]{1,0:T(8,128)(2,1)S(1)}, u32[]{:S(2)}, u32[]{:S(2)}) collective-permute-start(bf16[384,384]{1,0:T(8,128)(2,1)S(1)} %add_convert_fusion.8), channel_id=1, source_target_pairs={{0,8},{1,9},{2,10},{3,11},{4,12},{5,13},{6,14},{7,15},{8,0},{9,1},... | collective-permute-start | bytes 884744 | tf_op jit(solution)/shard_map/ppermute | solution.py:765
  177.5 1.9 copy-start.4
  179.4 9.0 %collective-permute-start.18 = (bf16[464,384]{1,0:T(8,128)(2,1)S(1)}, bf16[464,384]{1,0:T(8,128)(2,1)S(1)}, u32[]{:S(2)}, u32[]{:S(2)}) collective-permute-start(bf16[464,384]{1,0:T(8,128)(2,1)S(1)} %constant_dynamic-slice_fusion.1), channel_id=1, source_target_pairs={{0,2},{1,3},{2,0},{3,1},{4,6},{5,7},{6,4},{7,5},{8,10},{9,11},{10,... | collective-permute-start | bytes 1069064 | tf_op jit(solution)/shard_map/ppermute | solution.py:765
  181.6 6.8 %collective-permute-start.19 = (bf16[384,384]{1,0:T(8,128)(2,1)S(1)}, bf16[384,384]{1,0:T(8,128)(2,1)S(1)}, u32[]{:S(2)}, u32[]{:S(2)}) collective-permute-start(bf16[384,384]{1,0:T(8,128)(2,1)S(1)} %add_convert_fusion.7), channel_id=1, source_target_pairs={{0,4},{1,5},{2,6},{3,7},{4,0},{5,1},{6,2},{7,3},{8,12},{9,13},{10,... | collective-permute-start | bytes 884744 | tf_op jit(solution)/shard_map/ppermute | solution.py:765
  182.5 2.6 %collective-permute-start.20 = (f32[2,48,128]{2,1,0:T(8,128)S(1)}, f32[2,48,128]{2,1,0:T(8,128)S(1)}, u32[]{:S(2)}, u32[]{:S(2)}) collective-permute-start(f32[2,48,128]{2,1,0:T(8,128)S(1)} %bitcast.72), channel_id=1, source_target_pairs={{0,1},{1,0},{2,3},{3,2},{4,5},{5,4},{6,7},{7,6},{8,9},{9,8},{10,11... | collective-permute-start | bytes 147464 | tf_op jit(solution)/shard_map/ppermute | solution.py:765
  188.5 4.4 %collective-permute-start.21 = (bf16[232,384]{1,0:T(8,128)(2,1)S(1)}, bf16[232,384]{1,0:T(8,128)(2,1)S(1)}, u32[]{:S(2)}, u32[]{:S(2)}) collective-permute-start(bf16[232,384]{1,0:T(8,128)(2,1)S(1)} %constant_dynamic-slice_fusion), channel_id=1, source_target_pairs={{0,4},{1,5},{2,6},{3,7},{4,0},{5,1},{6,2},{7,3},{8,12},{9,13},{10,... | collective-permute-start | bytes 534536 | tf_op jit(solution)/shard_map/ppermute | solution.py:765
  189.7 2.9 %collective-permute-start.22 = (f32[2,48,128]{2,1,0:T(8,128)S(1)}, f32[2,48,128]{2,1,0:T(8,128)S(1)}, u32[]{:S(2)}, u32[]{:S(2)}) collective-permute-start(f32[2,48,128]{2,1,0:T(8,128)S(1)} %add.217), channel_id=1, source_target_pairs={{0,2},{1,3},{2,0},{3,1},{4,6},{5,7},{6,4},{7,5},{8,10},{9,11},{10,... | collective-permute-start | bytes 147464 | tf_op jit(solution)/shard_map/ppermute | solution.py:765
  193.0 10.2 %collective-permute-start.23 = (bf16[232,384]{1,0:T(8,128)(2,1)S(1)}, bf16[232,384]{1,0:T(8,128)(2,1)S(1)}, u32[]{:S(2)}, u32[]{:S(2)}) collective-permute-start(bf16[232,384]{1,0:T(8,128)(2,1)S(1)} %add_convert_fusion.10), channel_id=1, source_target_pairs={{0,8},{1,9},{2,10},{3,11},{4,12},{5,13},{6,14},{7,15},{8,0},{9,1},... | collective-permute-start | bytes 534536 | tf_op jit(solution)/shard_map/ppermute | solution.py:765
  195.5 13.3 %collective-permute-start.27 = (bf16[768,384]{1,0:T(8,128)(2,1)S(1)}, bf16[768,384]{1,0:T(8,128)(2,1)S(1)}, u32[]{:S(2)}, u32[]{:S(2)}) collective-permute-start(bf16[768,384]{1,0:T(8,128)(2,1)S(1)} %maximum_select_fusion.4), channel_id=1, source_target_pairs={{0,2},{1,3},{2,0},{3,1},{4,6},{5,7},{6,4},{7,5},{8,10},{9,11},{10,... | collective-permute-start | bytes 1769480 | tf_op jit(solution)/shard_map/ppermute | solution.py:765
  196.1 7.0 %collective-permute-start.24 = (f32[2,48,128]{2,1,0:T(8,128)S(1)}, f32[2,48,128]{2,1,0:T(8,128)S(1)}, u32[]{:S(2)}, u32[]{:S(2)}) collective-permute-start(f32[2,48,128]{2,1,0:T(8,128)S(1)} %add.219), channel_id=1, source_target_pairs={{0,8},{1,9},{2,10},{3,11},{4,12},{5,13},{6,14},{7,15},{8,0},{9,1},... | collective-permute-start | bytes 147464 | tf_op jit(solution)/shard_map/ppermute | solution.py:765
  203.2 5.6 %collective-permute-start.25 = (bf16[232,384]{1,0:T(8,128)(2,1)S(1)}, bf16[232,384]{1,0:T(8,128)(2,1)S(1)}, u32[]{:S(2)}, u32[]{:S(2)}) collective-permute-start(bf16[232,384]{1,0:T(8,128)(2,1)S(1)} %add_convert_fusion.9), channel_id=1, source_target_pairs={{0,4},{1,5},{2,6},{3,7},{4,0},{5,1},{6,2},{7,3},{8,12},{9,13},{10,... | collective-permute-start | bytes 534536 | tf_op jit(solution)/shard_map/ppermute | solution.py:765
  203.3 5.5 %collective-permute-start.26 = (f32[2,48,128]{2,1,0:T(8,128)S(1)}, f32[2,48,128]{2,1,0:T(8,128)S(1)}, u32[]{:S(2)}, u32[]{:S(2)}) collective-permute-start(f32[2,48,128]{2,1,0:T(8,128)S(1)} %add.221), channel_id=1, source_target_pairs={{0,4},{1,5},{2,6},{3,7},{4,0},{5,1},{6,2},{7,3},{8,12},{9,13},{10,... | collective-permute-start | bytes 147464 | tf_op jit(solution)/shard_map/ppermute | solution.py:765
  208.8 6.7 %collective-permute-start.30 = (f32[48,128]{1,0:T(8,128)S(1)}, f32[48,128]{1,0:T(8,128)S(1)}, u32[]{:S(2)}, u32[]{:S(2)}) collective-permute-start(f32[48,128]{1,0:T(8,128)S(1)} %dynamic-slice_bitcast_fusion.2), channel_id=1, source_target_pairs={{0,16},{16,0},{1,17},{17,1},{2,18},{18,2},{3,19},{19,3},{4,20},{20... | collective-permute-start | bytes 73736 | tf_op jit(solution)/shard_map/ppermute | solution.py:765
  209.7 6.6 %collective-permute-start.29 = (bf16[464,384]{1,0:T(8,128)(2,1)S(1)}, bf16[464,384]{1,0:T(8,128)(2,1)S(1)}, u32[]{:S(2)}, u32[]{:S(2)}) collective-permute-start(bf16[464,384]{1,0:T(8,128)(2,1)S(1)} %maximum_select_fusion.5), channel_id=1, source_target_pairs={{0,2},{1,3},{2,0},{3,1},{4,6},{5,7},{6,4},{7,5},{8,10},{9,11},{10,... | collective-permute-start | bytes 1069064 | tf_op jit(solution)/shard_map/ppermute | solution.py:765
  210.7 14.1 %collective-permute-start.28 = (bf16[1536,384]{1,0:T(8,128)(2,1)S(1)}, bf16[1536,384]{1,0:T(8,128)(2,1)}, u32[]{:S(2)}, u32[]{:S(2)}) collective-permute-start(bf16[1536,384]{1,0:T(8,128)(2,1)S(1)} %maximum_select_fusion), channel_id=1, source_target_pairs={{0,1},{1,0},{2,3},{3,2},{4,5},{5,4},{6,7},{7,6},{8,9},{9,8},{10,11... | collective-permute-start | bytes 3538952 | tf_op jit(solution)/shard_map/ppermute | solution.py:765
  216.5 8.3 %collective-permute-start.31 = (bf16[928,384]{1,0:T(8,128)(2,1)S(1)}, bf16[928,384]{1,0:T(8,128)(2,1)}, u32[]{:S(2)}, u32[]{:S(2)}) collective-permute-start(bf16[928,384]{1,0:T(8,128)(2,1)S(1)} %maximum_select_fusion.3), channel_id=1, source_target_pairs={{0,1},{1,0},{2,3},{3,2},{4,5},{5,4},{6,7},{7,6},{8,9},{9,8},{10,11... | collective-permute-start | bytes 2138120 | tf_op jit(solution)/shard_map/ppermute | solution.py:765

commit v3 on v2

--- a/solution.py
+++ b/solution.py
@@ -983,8 +983,7 @@
 
         keep_a, give_a = sides(added(keep_a, after(got_a, give_b)), "dp", turn)
         got_a = over(give_a, turn)
-        block_out = fillers[0](after(give_b, give_a))
-        got_a, block_out = together(got_a, block_out)
+        got_a, give_b = together(got_a, give_b)
         block_a = added(keep_a, got_a)
         sent_a = [over(block_a, bit) for bit in wide[:1]]
         input_grad, small = fillers[1](results, rest, block_a)
@@ -997,7 +996,9 @@
         block_b = added(keep_b, got_b)
 
         keep_b, give_b = sides(block_b, "dp", near)
-        got_b, got_a, got_s = together(over(give_b, near), over(block_a, turn), over(small, 1))
+        moved = over(give_b, near), over(block_a, turn), over(small, 1)
+        block_out = fillers[0](together(give_b, block_a, small)[0])
+        got_b, got_a, got_s, block_out = together(*moved, block_out)
         block_a, small = joined(block_a, got_a, side(turn)), small + got_s
         spread_a = over(block_a, near)
         keep_b, give_b = sides(added(keep_b, got_b), "dp", turn)

time: 233 us -> 232 us (level)
  waiting for transfers between devices: 43.7 us -> 47 us
  starting transfers between devices: 38.4 us -> 36 us
    ppermute x32, waiting for transfers between devices: 43.7 us -> 47 us  [swap(): return lax.ppermute(block, axis, pairs)]
    ppermute x32, starting transfers between devices: 38.4 us -> 36 us  [swap(): return lax.ppermute(block, axis, pairs)]
  transfers between devices with their start and end apart: 32 -> 32, of which waited for: 16 -> 13; matrix products, arithmetic and copies ran while one was open for 13% -> 13% of each run, Pallas kernels for 29% -> 29%
where the time goes in v3:
time: 232 us; the launch traced here: 231 us
  Pallas kernels  87.9 us (38%)
  waiting for transfers between devices  47 us (20%)
  starting transfers between devices  36 us (16%)
  matrix products  23.1 us (10%)
  local copies, waits for them, and re-layouts  18.8 us (8%)
  other arithmetic  16.6 us (7%)
    ppermute x32, waiting for transfers between devices, swap(): return lax.ppermute(block, axis, pairs)  47 us
    ppermute x32, starting transfers between devices, swap(): return lax.ppermute(block, axis, pairs)  36 us
    pallas_call x2, Pallas kernels, backward(): pl.pallas_call(functools.partial(backward_body, sizes, first_head, last),...  32.7 us
    pallas_call x1, Pallas kernels, forward(): pl.pallas_call(functools.partial(forward_body, sizes, tuple(lengths)), gr...  23.6 us
    pallas_call x1, Pallas kernels, gated(): pl.pallas_call(functools.partial(gated_body, sizes, tuple(lengths)), grid...  19.7 us
    dot_general x4, matrix products, mul_tn(): lax.dot_general(a, b, (((0,), (0,)), ((), ())), preferred_element_type=F32)  18.1 us
    pallas_call x1, Pallas kernels, input_backward(): pl.pallas_call(input_body, grid=(length // span,), in_specs=[SCALARS, dow...  11.9 us
    convert_element_type x10, other arithmetic, added(): return (keep.astype(F32) + got.astype(F32)).astype(BF16)  5.98 us
  transfers between devices with their start and end apart: 32, of which 13 were waited for; matrix products, arithmetic and copies ran while one was open for 13% of the time, Pallas kernels for 29%

profile of v3, /device:TPU:1, one launch (start us, length us, event | category | flops | bytes accessed | tf_op | source)
XLA Modules:
  0.0 231.4 jit_solution(15369260834028168433)
XLA Ops:
  0.8 1.1 dynamic-slice_bitcast_fusion.1
  1.9 0.7 slice.102
  2.7 2.1 collective-permute-start
  5.1 1.1 dynamic-slice_bitcast_fusion
  6.2 8.8 %collective-permute-done.1 = bf16[7,896]{1,0:T(8,128)(2,1)S(1)} collective-permute-done((bf16[7,896]{1,0:T(8,128)(2,1)S(1)}, bf16[7,896]{1,0:T(8,128)(2,1)S(1)}, u32[]{:S(2)}, u32[]{:S(2)}) %collective-permute-start.1) | collective-permute-done | bytes 12576 | tf_op jit(solution)/shard_map/ppermute | solution.py:765
  15.6 1.1 collective-permute-start.2
  16.8 1.2 collective-permute-start.3
  18.9 0.6 pad_bitcast_fusion.taps_ref.refs_9_.refs_11_
  19.5 0.6 maximum_select_fusion.6.raw_weight_ref
  20.1 5.9 %collective-permute-done.2.refs_3_ = bf16[576,384]{1,0:T(8,128)(2,1)S(1)} collective-permute-done((bf16[576,384]{1,0:T(8,128)(2,1)S(1)}, bf16[576,384]{1,0:T(8,128)(2,1)S(1)}, u32[]{:S(2)}, u32[]{:S(2)}) %collective-permute-start.2) | collective-permute-done | bytes 442400 | tf_op jit(solution)/shard_map/ppermute | solution.py:765
  26.6 2.7 %collective-permute-start.6 = (bf16[576,384]{1,0:T(8,128)(2,1)S(1)}, bf16[576,384]{1,0:T(8,128)(2,1)}, u32[]{:S(2)}, u32[]{:S(2)}) collective-permute-start(bf16[576,384]{1,0:T(8,128)(2,1)S(1)} %collective-permute-done.3.refs_5_), channel_id=1, source_target_pairs={{0,1},{1,0},{2,3},{3,2},{4,5},{5,4},{6,7},{7,6},{8,9},{9,8},{10,11... | collective-permute-start | bytes 1327112 | tf_op jit(solution)/shard_map/ppermute | solution.py:765
  29.9 0.6 stack.60.places_ref
  30.5 0.7 copy.29.heads_ref.refs_10_.refs_12_
  31.6 0.6 collective-permute-done.5.refs_4_
  32.2 23.6 %block_forward.1 = (bf16[1024,768]{1,0:T(8,128)(2,1)}, bf16[1024,1792]{1,0:T(8,128)(2,1)}, bf16[1792,1024]{1,0:T(8,128)(2,1)}, f32[24,1024]{1,0:T(8,128)}, bf16[...) custom-call(s32[14]{0:T(128)} %stack.60.places_ref, ...), custom_call_target="tpu_custom_call" | custom-call | flops 30000001024 | bytes 30000000 | tf_op jit(solution)/shard_map/block_forward/pallas_call | solution.py:531
  56.9 0.6 stack.50.places_ref
  57.5 1.2 copy.30.inner_gain_ref
  58.7 0.8 copy-done.21
  59.6 19.7 %block_gated.1 = (bf16[1536,1024]{1,0:T(8,128)(2,1)}, bf16[1024,1536]{1,0:T(8,128)(2,1)}, bf16[1536,1024]{1,0:T(8,128)(2,1)}, f32[24,1024]{1,0:T(8,128)}, f32[24...) custom-call(s32[6]{0:T(128)} %stack.50.places_ref, f32[24]{0:T(128)} %reshape_squeeze.3.skip_ref.refs_0_, ...), custom_call_target="tpu_custom_call" | custom-call | flops 15000000512 | bytes 15000000 | tf_op jit(solution)/shard_map/block_gated/pallas_call | solution.py:588
  79.2 5.0 %convolution_convert_fusion = bf16[1536,768]{1,0:T(8,128)(2,1)S(1)} fusion(bf16[1536,1024]{1,0:T(8,128)(2,1)} %get-tuple-element.98, f32[]{:T(128)} %bitcast.26, bf16[1,1,1024,768]{3,2,1,0:T(8,128)(2,1)} %param.23), kind=kOutput, calls=%fused_computation.3 | convolution fusion | flops 2419458048 | bytes 7077892 | tf_op jit(solution)/shard_map/dot_general | solution.py:29
  84.6 4.3 %fusion.10 = bf16[768,768]{1,0:T(8,128)(2,1)} fusion(bf16[1024,768]{1,0:T(8,128)(2,1)} %get-tuple-element.96, bf16[1024,1536]{1,0:T(8,128)(2,1)} %get-tuple-element.102.d_gate_ref, s32[]{:T(128)S(6)} %select_n.203), kind=kOutput, calls=%fused_computation.16 | convolution fusion | flops 1208549376 | bytes 4325380 | tf_op jit(solution)/shard_map/dot_general | solution.py:37
  89.3 1.7 add_convert_fusion.3
  92.6 1.5 add_convert_fusion.2
  94.8 19.3 %block_backward.2 = (bf16[1024,2048]{1,0:T(8,128)(2,1)}, f32[16,1024]{1,0:T(8,128)}, f32[16,1024]{1,0:T(8,128)}, f32[5,8,128]{2,1,0:T(8,128)}, f32[256,1024]{1,0:T(8,128)}) custom-call(f32[24]{0:T(128)} %reshape_squeeze.3.skip_ref.refs_0_, bf16[1792,1024]{1,0:T(8,128)(2,1)} %get-tuple-element.94.refs_2_.refs_1_, ...), custom_call_target="tpu_custom_call" | custom-call | flops 20000000000 | bytes 20000000 | tf_op jit(solution)/shard_map/block_backward/pallas_call | solution.py:693
  114.1 4.6 %collective-permute-done.12 = bf16[768,384]{1,0:T(8,128)(2,1)S(1)} collective-permute-done((bf16[768,384]{1,0:T(8,128)(2,1)S(1)}, bf16[768,384]{1,0:T(8,128)(2,1)S(1)}, u32[]{:S(2)}, u32[]{:S(2)}) %collective-permute-start.12) | collective-permute-done | bytes 589856 | tf_op jit(solution)/shard_map/ppermute | solution.py:765
  119.1 1.4 collective-permute-start.13
  120.5 13.4 %block_backward.3 = (bf16[1024,2048]{1,0:T(8,128)(2,1)}, f32[8,1024]{1,0:T(8,128)}, f32[8,1024]{1,0:T(8,128)}, f32[5,6,128]{2,1,0:T(8,128)}) custom-call(f32[24]{0:T(128)} %reshape_squeeze.3.skip_ref.refs_0_, bf16[1792,1024]{1,0:T(8,128)(2,1)} %get-tuple-element.94.refs_2_.refs_1_, ...), custom_call_target="tpu_custom_call", output_to_operand_aliasing={{0}: (15, {})} | custom-call | flops 12000000000 | bytes 12000000 | tf_op jit(solution)/shard_map/block_backward/pallas_call | solution.py:693
  133.9 0.8 copy-done.1
  134.7 5.8 %fusion.2 = bf16[1856,768]{1,0:T(8,128)(2,1)S(1)} fusion(bf16[1024,768]{1,0:T(8,128)(2,1)} %get-tuple-element.96, bf16[1024,2048]{1,0:T(8,128)(2,1)} %get-tuple-element.123.d_rest_ref), kind=kOutput, calls=%fused_computation.4 | convolution fusion | flops 2920660992 | bytes 8355840 | tf_op jit(solution)/shard_map/dot_general | solution.py:37
  140.5 1.6 copy-done
  142.2 1.2 collective-permute-start.14
  143.4 3.0 %collective-permute-done.14 = bf16[928,768]{1,0:T(8,128)(2,1)} collective-permute-done((bf16[928,768]{1,0:T(8,128)(2,1)S(1)}, bf16[928,768]{1,0:T(8,128)(2,1)}, u32[]{:S(2)}, u32[]{:S(2)}) %collective-permute-start.14) | collective-permute-done | bytes 1425440 | tf_op jit(solution)/shard_map/ppermute | solution.py:765
  146.3 2.1 add_convert_fusion
  148.5 0.9 constant_dynamic-slice_fusion.3
  149.9 1.3 collective-permute-start.15
  151.3 1.4 reduce_sum.45
  153.8 4.5 %collective-permute-done.15 = bf16[384,384]{1,0:T(8,128)(2,1)S(1)} collective-permute-done((bf16[384,384]{1,0:T(8,128)(2,1)S(1)}, bf16[384,384]{1,0:T(8,128)(2,1)S(1)}, u32[]{:S(2)}, u32[]{:S(2)}) %collective-permute-start.15) | collective-permute-done | bytes 294944 | tf_op jit(solution)/shard_map/ppermute | solution.py:765
  158.4 2.3 %collective-permute-start.16 = (bf16[384,384]{1,0:T(8,128)(2,1)S(1)}, bf16[384,384]{1,0:T(8,128)(2,1)S(1)}, u32[]{:S(2)}, u32[]{:S(2)}) collective-permute-start(bf16[384,384]{1,0:T(8,128)(2,1)S(1)} %add_convert_fusion.8), channel_id=1, source_target_pairs={{0,8},{1,9},{2,10},{3,11},{4,12},{5,13},{6,14},{7,15},{8,0},{9,1},... | collective-permute-start | bytes 884744 | tf_op jit(solution)/shard_map/ppermute | solution.py:765
  160.8 11.9 %input_backward.1 = (f32[1024,768]{1,0:T(8,128)}, f32[8,768]{1,0:T(8,128)}) custom-call(f32[1]{0:T(128)} %bitcast.15.alive_ref, bf16[1024,768]{1,0:T(8,128)(2,1)} %bitcast.86, bf16[1024,768]{1,0:T(8,128)(2,1)} %bitcast.84, f32[1,768]{1,0:T(1,128)} %bitcast.82, bf16[1024,1536]{1,0:T(8,128)(2,1)} %get-tuple-element.102.d_gate_ref, ...), custom_call_target="tpu_custom_call" | custom-call | flops 8000000000 | bytes 8000000 | tf_op jit(solution)/shard_map/input_backward/pallas_call | solution.py:652
  172.7 0.7 reduce_sum.46
  173.7 1.5 collective-permute-start.19
  175.2 1.3 add_convert_fusion.4
  176.5 1.2 collective-permute-start.18
  177.7 1.8 collective-permute-start.20
  179.5 6.5 %multiply_convert_fusion = bf16[1024,768]{1,0:T(8,128)(2,1)} fusion(bf16[1536,1024]{1,0:T(8,128)(2,1)} %get-tuple-element.98, bf16[1536,768]{1,0:T(8,128)(2,1)} %get-tuple-element.133, f32[]{:T(128)} %bitcast.26, bf16[1,1,1024,768]{3,2,1,0:T(8,128)(2,1)S(1)} %copy-done.19), kind=kOutput, calls=%fused_computation.5 | convolution fusion | flops 2419064832 | bytes 8650756 | tf_op jit(solution)/shard_map/dot_general | solution.py:37
  187.0 2.7 %collective-permute-done.22 = f32[2,48,128]{2,1,0:T(8,128)S(1)} collective-permute-done((f32[2,48,128]{2,1,0:T(8,128)S(1)}, f32[2,48,128]{2,1,0:T(8,128)S(1)}, u32[]{:S(2)}, u32[]{:S(2)}) %collective-permute-start.22) | collective-permute-done | bytes 49184 | tf_op jit(solution)/shard_map/ppermute | solution.py:765
  189.6 1.4 collective-permute-done.21
  191.0 2.4 %collective-permute-start.23 = (bf16[232,384]{1,0:T(8,128)(2,1)S(1)}, bf16[232,384]{1,0:T(8,128)(2,1)S(1)}, u32[]{:S(2)}, u32[]{:S(2)}) collective-permute-start(bf16[232,384]{1,0:T(8,128)(2,1)S(1)} %add_convert_fusion.10), channel_id=1, source_target_pairs={{0,8},{1,9},{2,10},{3,11},{4,12},{5,13},{6,14},{7,15},{8,0},{9,1},... | collective-permute-start | bytes 534536 | tf_op jit(solution)/shard_map/ppermute | solution.py:765
  193.6 1.2 collective-permute-start.27
  194.8 8.5 %collective-permute-done.24 = f32[2,48,128]{2,1,0:T(8,128)S(1)} collective-permute-done((f32[2,48,128]{2,1,0:T(8,128)S(1)}, f32[2,48,128]{2,1,0:T(8,128)S(1)}, u32[]{:S(2)}, u32[]{:S(2)}) %collective-permute-start.24) | collective-permute-done | bytes 49184 | tf_op jit(solution)/shard_map/ppermute | solution.py:765
  203.3 0.6 collective-permute-start.25
  204.0 0.9 collective-permute-start.26
  204.9 4.0 %collective-permute-done.26 = f32[2,48,128]{2,1,0:T(8,128)S(1)} collective-permute-done((f32[2,48,128]{2,1,0:T(8,128)S(1)}, f32[2,48,128]{2,1,0:T(8,128)S(1)}, u32[]{:S(2)}, u32[]{:S(2)}) %collective-permute-start.26) | collective-permute-done | bytes 49184 | tf_op jit(solution)/shard_map/ppermute | solution.py:765
  209.5 1.1 collective-permute-start.29
  211.0 3.2 %collective-permute-start.28 = (bf16[1536,384]{1,0:T(8,128)(2,1)S(1)}, bf16[1536,384]{1,0:T(8,128)(2,1)}, u32[]{:S(2)}, u32[]{:S(2)}) collective-permute-start(bf16[1536,384]{1,0:T(8,128)(2,1)S(1)} %maximum_select_fusion), channel_id=1, source_target_pairs={{0,1},{1,0},{2,3},{3,2},{4,5},{5,4},{6,7},{7,6},{8,9},{9,8},{10,11... | collective-permute-start | bytes 3538952 | tf_op jit(solution)/shard_map/ppermute | solution.py:765
  214.3 2.2 collective-permute-done.29
  216.8 3.8 %collective-permute-start.31 = (bf16[928,384]{1,0:T(8,128)(2,1)S(1)}, bf16[928,384]{1,0:T(8,128)(2,1)}, u32[]{:S(2)}, u32[]{:S(2)}) collective-permute-start(bf16[928,384]{1,0:T(8,128)(2,1)S(1)} %maximum_select_fusion.3), channel_id=1, source_target_pairs={{0,1},{1,0},{2,3},{3,2},{4,5},{5,4},{6,7},{7,6},{8,9},{9,8},{10,11... | collective-permute-start | bytes 2138120 | tf_op jit(solution)/shard_map/ppermute | solution.py:765
  221.2 0.6 slice.90
  222.4 0.6 slice_bitcast_fusion
  223.0 0.6 slice_bitcast_fusion.1
  223.6 1.4 fusion.27
  225.0 1.6 fusion.15
  226.6 1.7 fusion.16
  228.7 2.7 %convert_bitcast_fusion = f32[384,3352]{0,1:T(8,128)} fusion(bf16[1816,384]{1,0:T(8,128)(2,1)S(1)} %fusion.15, bf16[1536,384]{1,0:T(8,128)(2,1)S(1)} %maximum_select_fusion.1), kind=kLoop, calls=%fused_computation | loop fusion | flops 5148672 | bytes 7723008 | tf_op jit(solution)/shard_map/transpose | solution.py:1151
  (144 shorter events, 13.3 us)
Async XLA Ops:
  0.6 4.2 %copy-start.13 = (bf16[896]{0:T(1024)(128)(2,1)S(1)}, bf16[896]{0:T(1024)(128)(2,1)}, u32[]{:S(2)}) copy-start(bf16[896]{0:T(1024)(128)(2,1)} %param.17) | copy-start | bytes 5380
  0.7 4.2 %copy-start.12 = (bf16[768]{0:T(1024)(128)(2,1)S(1)}, bf16[768]{0:T(1024)(128)(2,1)}, u32[]{:S(2)}) copy-start(bf16[768]{0:T(1024)(128)(2,1)} %param.21) | copy-start | bytes 4612
  0.7 4.2 %copy-start.15 = (bf16[384]{0:T(512)(128)(2,1)S(1)}, bf16[384]{0:T(512)(128)(2,1)}, u32[]{:S(2)}) copy-start(bf16[384]{0:T(512)(128)(2,1)} %param.14) | copy-start | bytes 2308
  0.7 4.2 %copy-start.18 = (bf16[12]{0:T(256)(128)(2,1)S(1)}, bf16[12]{0:T(256)(128)(2,1)}, u32[]{:S(2)}) copy-start(bf16[12]{0:T(256)(128)(2,1)} %param.18) | copy-start | bytes 76
  0.7 4.2 %copy-start.17 = (bf16[12]{0:T(256)(128)(2,1)S(1)}, bf16[12]{0:T(256)(128)(2,1)}, u32[]{:S(2)}) copy-start(bf16[12]{0:T(256)(128)(2,1)} %param.19) | copy-start | bytes 76
  0.7 4.2 %copy-start.16 = (bf16[12]{0:T(256)(128)(2,1)S(1)}, bf16[12]{0:T(256)(128)(2,1)}, u32[]{:S(2)}) copy-start(bf16[12]{0:T(256)(128)(2,1)} %param.20) | copy-start | bytes 76
  0.7 4.3 %copy-start.9 = (bf16[896,4]{0,1:T(4,128)(2,1)S(1)}, bf16[896,4]{0,1:T(4,128)(2,1)}, u32[]{:S(2)}) copy-start(bf16[896,4]{0,1:T(4,128)(2,1)} %param.16) | copy-start | bytes 21508
  0.8 29.7 %copy-start.3 = (bf16[768,768]{1,0:T(8,128)(2,1)S(1)}, bf16[768,768]{1,0:T(8,128)(2,1)}, u32[]{:S(2)}) copy-start(bf16[768,768]{1,0:T(8,128)(2,1)} %refs_3_.1) | copy-start | bytes 3538948
  2.7 12.9 %collective-permute-start = (bf16[576,384]{1,0:T(8,128)(2,1)S(1)}, bf16[576,384]{1,0:T(8,128)(2,1)S(1)}, u32[]{:S(2)}, u32[]{:S(2)}) collective-permute-start(bf16[576,384]{1,0:T(8,128)(2,1)S(1)} %pad_maximum_fusion.2), channel_id=1, source_target_pairs={{0,16},{16,0},{1,17},{17,1},{2,18},{18,2},{3,19},{19,3},{4,20},{20... | collective-permute-start | bytes 1327112 | tf_op jit(solution)/shard_map/ppermute | solution.py:765
  5.0 10.0 %collective-permute-start.1 = (bf16[7,896]{1,0:T(8,128)(2,1)S(1)}, bf16[7,896]{1,0:T(8,128)(2,1)S(1)}, u32[]{:S(2)}, u32[]{:S(2)}) collective-permute-start(bf16[7,896]{1,0:T(8,128)(2,1)S(1)} %fusion.22), channel_id=1, source_target_pairs={{0,16},{16,0},{1,17},{17,1},{2,18},{18,2},{3,19},{19,3},{4,20},{20... | collective-permute-start | bytes 37640 | tf_op jit(solution)/shard_map/ppermute | solution.py:765
  15.6 16.6 %copy-start.14 = (bf16[576,384]{1,0:T(8,128)(2,1)}, bf16[576,384]{1,0:T(8,128)(2,1)S(1)}, u32[]{:S(2)}) copy-start(bf16[576,384]{1,0:T(8,128)(2,1)S(1)} %collective-permute-done.refs_1_) | copy-start | bytes 1327108
  15.6 10.4 %collective-permute-start.2 = (bf16[576,384]{1,0:T(8,128)(2,1)S(1)}, bf16[576,384]{1,0:T(8,128)(2,1)S(1)}, u32[]{:S(2)}, u32[]{:S(2)}) collective-permute-start(bf16[576,384]{1,0:T(8,128)(2,1)S(1)} %dynamic-slice_bitcast_fusion), channel_id=1, source_target_pairs={{0,16},{16,0},{1,17},{17,1},{2,18},{18,2},{3,19},{19,3},{4,20},{20... | collective-permute-start | bytes 1327112 | tf_op jit(solution)/shard_map/ppermute | solution.py:765
  16.8 9.8 %collective-permute-start.3 = (bf16[576,384]{1,0:T(8,128)(2,1)S(1)}, bf16[576,384]{1,0:T(8,128)(2,1)S(1)}, u32[]{:S(2)}, u32[]{:S(2)}) collective-permute-start(bf16[576,384]{1,0:T(8,128)(2,1)S(1)} %collective-permute-done.refs_1_), channel_id=1, source_target_pairs={{0,2},{1,3},{2,0},{3,1},{4,6},{5,7},{6,4},{7,5},{8,10},{9,11},{10,... | collective-permute-start | bytes 1327112 | tf_op jit(solution)/shard_map/ppermute | solution.py:765
  26.1 6.1 %copy-start.22 = (bf16[576,384]{1,0:T(8,128)(2,1)}, bf16[576,384]{1,0:T(8,128)(2,1)S(1)}, u32[]{:S(2)}) copy-start(bf16[576,384]{1,0:T(8,128)(2,1)S(1)} %collective-permute-done.2.refs_3_) | copy-start | bytes 1327108
  26.6 5.6 %copy-start.23 = (bf16[576,384]{1,0:T(8,128)(2,1)}, bf16[576,384]{1,0:T(8,128)(2,1)S(1)}, u32[]{:S(2)}) copy-start(bf16[576,384]{1,0:T(8,128)(2,1)S(1)} %collective-permute-done.3.refs_5_) | copy-start | bytes 1327108
  26.6 4.6 %collective-permute-start.6 = (bf16[576,384]{1,0:T(8,128)(2,1)S(1)}, bf16[576,384]{1,0:T(8,128)(2,1)}, u32[]{:S(2)}, u32[]{:S(2)}) collective-permute-start(bf16[576,384]{1,0:T(8,128)(2,1)S(1)} %collective-permute-done.3.refs_5_), channel_id=1, source_target_pairs={{0,1},{1,0},{2,3},{3,2},{4,5},{5,4},{6,7},{7,6},{8,9},{9,8},{10,11... | collective-permute-start | bytes 1327112 | tf_op jit(solution)/shard_map/ppermute | solution.py:765
  29.4 2.2 collective-permute-start.4
  29.4 2.8 %collective-permute-start.5 = (bf16[576,384]{1,0:T(8,128)(2,1)S(1)}, bf16[576,384]{1,0:T(8,128)(2,1)}, u32[]{:S(2)}, u32[]{:S(2)}) collective-permute-start(bf16[576,384]{1,0:T(8,128)(2,1)S(1)} %collective-permute-done.2.refs_3_), channel_id=1, source_target_pairs={{0,1},{1,0},{2,3},{3,2},{4,5},{5,4},{6,7},{7,6},{8,9},{9,8},{10,11... | collective-permute-start | bytes 1327112 | tf_op jit(solution)/shard_map/ppermute | solution.py:765
  31.2 24.6 %collective-permute-start.7 = (bf16[384,768]{1,0:T(8,128)(2,1)S(1)}, bf16[384,768]{1,0:T(8,128)(2,1)S(1)}, u32[]{:S(2)}, u32[]{:S(2)}) collective-permute-start(bf16[384,768]{1,0:T(8,128)(2,1)S(1)} %constant_dynamic-slice_fusion.11), channel_id=1, source_target_pairs={{0,16},{16,0},{1,17},{17,1},{2,18},{18,2},{3,19},{19,3},{4,20},{20... | collective-permute-start | bytes 1769480 | tf_op jit(solution)/shard_map/ppermute | solution.py:765
  55.8 2.9 %copy-start.20 = (bf16[384,768]{1,0:T(8,128)(2,1)}, bf16[384,768]{1,0:T(8,128)(2,1)S(1)}, u32[]{:S(2)}) copy-start(bf16[384,768]{1,0:T(8,128)(2,1)S(1)} %collective-permute-done.7.refs_4_) | copy-start | bytes 1769476
  55.8 2.9 %collective-permute-start.8 = (bf16[384,768]{1,0:T(8,128)(2,1)S(1)}, bf16[384,768]{1,0:T(8,128)(2,1)S(1)}, u32[]{:S(2)}, u32[]{:S(2)}) collective-permute-start(bf16[384,768]{1,0:T(8,128)(2,1)S(1)} %collective-permute-done.7.refs_4_), channel_id=1, source_target_pairs={{0,1},{1,0},{2,3},{3,2},{4,5},{5,4},{6,7},{7,6},{8,9},{9,8},{10,11... | collective-permute-start | bytes 1769480 | tf_op jit(solution)/shard_map/ppermute | solution.py:765
  58.7 0.8 copy-start.21
  84.4 4.5 %collective-permute-start.9 = (bf16[1536,384]{1,0:T(8,128)(2,1)S(1)}, bf16[1536,384]{1,0:T(8,128)(2,1)}, u32[]{:S(2)}, u32[]{:S(2)}) collective-permute-start(bf16[1536,384]{1,0:T(8,128)(2,1)S(1)} %constant_dynamic-slice_fusion.10), channel_id=1, source_target_pairs={{0,1},{1,0},{2,3},{3,2},{4,5},{5,4},{6,7},{7,6},{8,9},{9,8},{10,11... | collective-permute-start | bytes 3538952 | tf_op jit(solution)/shard_map/ppermute | solution.py:765
  88.9 3.1 %collective-permute-start.10 = (bf16[768,768]{1,0:T(8,128)(2,1)}, bf16[768,768]{1,0:T(8,128)(2,1)S(1)}, u32[]{:S(2)}, u32[]{:S(2)}) collective-permute-start(bf16[768,768]{1,0:T(8,128)(2,1)} %fusion.10), channel_id=1, source_target_pairs={{0,1},{1,0},{2,3},{3,2},{4,5},{5,4},{6,7},{7,6},{8,9},{9,8},{10,11... | collective-permute-start | bytes 3538952 | tf_op jit(solution)/shard_map/ppermute | solution.py:765
  89.3 2.7 %copy-start.24 = (bf16[1024,1536]{1,0:T(8,128)(2,1)S(1)}, bf16[1024,1536]{1,0:T(8,128)(2,1)}, u32[]{:S(2)}) copy-start(bf16[1024,1536]{1,0:T(8,128)(2,1)} %get-tuple-element.102.d_gate_ref) | copy-start | bytes 9437188
  91.0 1.5 copy-start.25
  91.2 22.9 %collective-permute-start.11 = (bf16[768,384]{1,0:T(8,128)(2,1)S(1)}, bf16[768,384]{1,0:T(8,128)(2,1)S(1)}, u32[]{:S(2)}, u32[]{:S(2)}) collective-permute-start(bf16[768,384]{1,0:T(8,128)(2,1)S(1)} %get-tuple-element.167), channel_id=1, source_target_pairs={{0,16},{16,0},{1,17},{17,1},{2,18},{18,2},{3,19},{19,3},{4,20},{20... | collective-permute-start | bytes 1769480 | tf_op jit(solution)/shard_map/ppermute | solution.py:765
  94.3 24.4 %collective-permute-start.12 = (bf16[768,384]{1,0:T(8,128)(2,1)S(1)}, bf16[768,384]{1,0:T(8,128)(2,1)S(1)}, u32[]{:S(2)}, u32[]{:S(2)}) collective-permute-start(bf16[768,384]{1,0:T(8,128)(2,1)S(1)} %get-tuple-element.164), channel_id=1, source_target_pairs={{0,16},{16,0},{1,17},{17,1},{2,18},{18,2},{3,19},{19,3},{4,20},{20... | collective-permute-start | bytes 1769480 | tf_op jit(solution)/shard_map/ppermute | solution.py:765
  119.1 14.8 %collective-permute-start.13 = (bf16[768,384]{1,0:T(8,128)(2,1)S(1)}, bf16[768,384]{1,0:T(8,128)(2,1)S(1)}, u32[]{:S(2)}, u32[]{:S(2)}) collective-permute-start(bf16[768,384]{1,0:T(8,128)(2,1)S(1)} %constant_dynamic-slice_fusion.5), channel_id=1, source_target_pairs={{0,2},{1,3},{2,0},{3,1},{4,6},{5,7},{6,4},{7,5},{8,10},{9,11},{10,... | collective-permute-start | bytes 1769480 | tf_op jit(solution)/shard_map/ppermute | solution.py:765
  133.9 0.8 copy-start.1
  140.5 1.6 copy-start
  142.2 4.2 %collective-permute-start.14 = (bf16[928,768]{1,0:T(8,128)(2,1)S(1)}, bf16[928,768]{1,0:T(8,128)(2,1)}, u32[]{:S(2)}, u32[]{:S(2)}) collective-permute-start(bf16[928,768]{1,0:T(8,128)(2,1)S(1)} %constant_dynamic-slice_fusion.4), channel_id=1, source_target_pairs={{0,1},{1,0},{2,3},{3,2},{4,5},{5,4},{6,7},{7,6},{8,9},{9,8},{10,11... | collective-permute-start | bytes 4276232 | tf_op jit(solution)/shard_map/ppermute | solution.py:765
  148.5 1.2 copy-start.2
  149.7 3.0 %copy-start.4 = (f32[24,1024]{1,0:T(8,128)S(1)}, f32[24,1024]{1,0:T(8,128)}, u32[]{:S(2)}) copy-start(f32[24,1024]{1,0:T(8,128)} %get-tuple-element.129) | copy-start | bytes 294916
  149.7 3.2 %copy-start.5 = (f32[16,1024]{1,0:T(8,128)S(1)}, f32[16,1024]{1,0:T(8,128)}, u32[]{:S(2)}) copy-start(f32[16,1024]{1,0:T(8,128)} %get-tuple-element.113.refs_14_) | copy-start | bytes 196612
  149.7 3.2 %copy-start.6 = (f32[16,1024]{1,0:T(8,128)S(1)}, f32[16,1024]{1,0:T(8,128)}, u32[]{:S(2)}) copy-start(f32[16,1024]{1,0:T(8,128)} %get-tuple-element.127) | copy-start | bytes 196612
  149.7 3.2 %copy-start.7 = (f32[8,1024]{1,0:T(8,128)S(1)}, f32[8,1024]{1,0:T(8,128)}, u32[]{:S(2)}) copy-start(f32[8,1024]{1,0:T(8,128)} %get-tuple-element.126) | copy-start | bytes 98308
  149.7 3.2 %copy-start.8 = (f32[8,1024]{1,0:T(8,128)S(1)}, f32[8,1024]{1,0:T(8,128)}, u32[]{:S(2)}) copy-start(f32[8,1024]{1,0:T(8,128)} %get-tuple-element.128) | copy-start | bytes 98308
  149.7 3.5 %copy-start.10 = (f32[5,8,128]{2,1,0:T(8,128)S(1)}, f32[5,8,128]{2,1,0:T(8,128)}, u32[]{:S(2)}) copy-start(f32[5,8,128]{2,1,0:T(8,128)} %get-tuple-element.120) | copy-start | bytes 61444
  149.7 3.5 %copy-start.11 = (f32[5,6,128]{2,1,0:T(8,128)S(1)}, f32[5,6,128]{2,1,0:T(8,128)}, u32[]{:S(2)}) copy-start(f32[5,6,128]{2,1,0:T(8,128)} %get-tuple-element.121) | copy-start | bytes 46084
  149.9 8.4 %collective-permute-start.15 = (bf16[384,384]{1,0:T(8,128)(2,1)S(1)}, bf16[384,384]{1,0:T(8,128)(2,1)S(1)}, u32[]{:S(2)}, u32[]{:S(2)}) collective-permute-start(bf16[384,384]{1,0:T(8,128)(2,1)S(1)} %constant_dynamic-slice_fusion.2), channel_id=1, source_target_pairs={{0,4},{1,5},{2,6},{3,7},{4,0},{5,1},{6,2},{7,3},{8,12},{9,13},{10,... | collective-permute-start | bytes 884744 | tf_op jit(solution)/shard_map/ppermute | solution.py:765
  153.3 20.3 %collective-permute-start.17 = (bf16[928,384]{1,0:T(8,128)(2,1)}, bf16[928,384]{1,0:T(8,128)(2,1)}, u32[]{:S(2)}, u32[]{:S(2)}) collective-permute-start(bf16[928,384]{1,0:T(8,128)(2,1)} %constant_dynamic-slice_fusion.3), channel_id=1, source_target_pairs={{0,16},{16,0},{1,17},{17,1},{2,18},{18,2},{3,19},{19,3},{4,20},{20... | collective-permute-start | bytes 2138120 | tf_op jit(solution)/shard_map/ppermute | solution.py:765
  158.4 15.2 %collective-permute-start.16 = (bf16[384,384]{1,0:T(8,128)(2,1)S(1)}, bf16[384,384]{1,0:T(8,128)(2,1)S(1)}, u32[]{:S(2)}, u32[]{:S(2)}) collective-permute-start(bf16[384,384]{1,0:T(8,128)(2,1)S(1)} %add_convert_fusion.8), channel_id=1, source_target_pairs={{0,8},{1,9},{2,10},{3,11},{4,12},{5,13},{6,14},{7,15},{8,0},{9,1},... | collective-permute-start | bytes 884744 | tf_op jit(solution)/shard_map/ppermute | solution.py:765
  173.7 5.8 %copy-start.19 = (bf16[1,1,1024,768]{3,2,1,0:T(8,128)(2,1)S(1)}, bf16[1,1,1024,768]{3,2,1,0:T(8,128)(2,1)}, u32[]{:S(2)}) copy-start(bf16[1,1,1024,768]{3,2,1,0:T(8,128)(2,1)} %param.12) | copy-start | bytes 4718596
  173.7 12.3 %collective-permute-start.19 = (bf16[384,384]{1,0:T(8,128)(2,1)S(1)}, bf16[384,384]{1,0:T(8,128)(2,1)S(1)}, u32[]{:S(2)}, u32[]{:S(2)}) collective-permute-start(bf16[384,384]{1,0:T(8,128)(2,1)S(1)} %add_convert_fusion.7), channel_id=1, source_target_pairs={{0,4},{1,5},{2,6},{3,7},{4,0},{5,1},{6,2},{7,3},{8,12},{9,13},{10,... | collective-permute-start | bytes 884744 | tf_op jit(solution)/shard_map/ppermute | solution.py:765
  176.5 9.5 %collective-permute-start.18 = (bf16[464,384]{1,0:T(8,128)(2,1)S(1)}, bf16[464,384]{1,0:T(8,128)(2,1)S(1)}, u32[]{:S(2)}, u32[]{:S(2)}) collective-permute-start(bf16[464,384]{1,0:T(8,128)(2,1)S(1)} %constant_dynamic-slice_fusion.1), channel_id=1, source_target_pairs={{0,2},{1,3},{2,0},{3,1},{4,6},{5,7},{6,4},{7,5},{8,10},{9,11},{10,... | collective-permute-start | bytes 1069064 | tf_op jit(solution)/shard_map/ppermute | solution.py:765
  177.7 8.4 %collective-permute-start.20 = (f32[2,48,128]{2,1,0:T(8,128)S(1)}, f32[2,48,128]{2,1,0:T(8,128)S(1)}, u32[]{:S(2)}, u32[]{:S(2)}) collective-permute-start(f32[2,48,128]{2,1,0:T(8,128)S(1)} %bitcast.72), channel_id=1, source_target_pairs={{0,1},{1,0},{2,3},{3,2},{4,5},{5,4},{6,7},{7,6},{8,9},{9,8},{10,11... | collective-permute-start | bytes 147464 | tf_op jit(solution)/shard_map/ppermute | solution.py:765
  186.2 4.8 %collective-permute-start.21 = (bf16[232,384]{1,0:T(8,128)(2,1)S(1)}, bf16[232,384]{1,0:T(8,128)(2,1)S(1)}, u32[]{:S(2)}, u32[]{:S(2)}) collective-permute-start(bf16[232,384]{1,0:T(8,128)(2,1)S(1)} %constant_dynamic-slice_fusion), channel_id=1, source_target_pairs={{0,4},{1,5},{2,6},{3,7},{4,0},{5,1},{6,2},{7,3},{8,12},{9,13},{10,... | collective-permute-start | bytes 534536 | tf_op jit(solution)/shard_map/ppermute | solution.py:765
  186.7 2.9 %collective-permute-start.22 = (f32[2,48,128]{2,1,0:T(8,128)S(1)}, f32[2,48,128]{2,1,0:T(8,128)S(1)}, u32[]{:S(2)}, u32[]{:S(2)}) collective-permute-start(f32[2,48,128]{2,1,0:T(8,128)S(1)} %add.217), channel_id=1, source_target_pairs={{0,2},{1,3},{2,0},{3,1},{4,6},{5,7},{6,4},{7,5},{8,10},{9,11},{10,... | collective-permute-start | bytes 147464 | tf_op jit(solution)/shard_map/ppermute | solution.py:765
  191.0 12.2 %collective-permute-start.23 = (bf16[232,384]{1,0:T(8,128)(2,1)S(1)}, bf16[232,384]{1,0:T(8,128)(2,1)S(1)}, u32[]{:S(2)}, u32[]{:S(2)}) collective-permute-start(bf16[232,384]{1,0:T(8,128)(2,1)S(1)} %add_convert_fusion.10), channel_id=1, source_target_pairs={{0,8},{1,9},{2,10},{3,11},{4,12},{5,13},{6,14},{7,15},{8,0},{9,1},... | collective-permute-start | bytes 534536 | tf_op jit(solution)/shard_map/ppermute | solution.py:765
  193.6 15.3 %collective-permute-start.27 = (bf16[768,384]{1,0:T(8,128)(2,1)S(1)}, bf16[768,384]{1,0:T(8,128)(2,1)S(1)}, u32[]{:S(2)}, u32[]{:S(2)}) collective-permute-start(bf16[768,384]{1,0:T(8,128)(2,1)S(1)} %maximum_select_fusion.4), channel_id=1, source_target_pairs={{0,2},{1,3},{2,0},{3,1},{4,6},{5,7},{6,4},{7,5},{8,10},{9,11},{10,... | collective-permute-start | bytes 1769480 | tf_op jit(solution)/shard_map/ppermute | solution.py:765
  194.8 8.5 %collective-permute-start.24 = (f32[2,48,128]{2,1,0:T(8,128)S(1)}, f32[2,48,128]{2,1,0:T(8,128)S(1)}, u32[]{:S(2)}, u32[]{:S(2)}) collective-permute-start(f32[2,48,128]{2,1,0:T(8,128)S(1)} %add.219), channel_id=1, source_target_pairs={{0,8},{1,9},{2,10},{3,11},{4,12},{5,13},{6,14},{7,15},{8,0},{9,1},... | collective-permute-start | bytes 147464 | tf_op jit(solution)/shard_map/ppermute | solution.py:765
  203.3 5.6 %collective-permute-start.25 = (bf16[232,384]{1,0:T(8,128)(2,1)S(1)}, bf16[232,384]{1,0:T(8,128)(2,1)S(1)}, u32[]{:S(2)}, u32[]{:S(2)}) collective-permute-start(bf16[232,384]{1,0:T(8,128)(2,1)S(1)} %add_convert_fusion.9), channel_id=1, source_target_pairs={{0,4},{1,5},{2,6},{3,7},{4,0},{5,1},{6,2},{7,3},{8,12},{9,13},{10,... | collective-permute-start | bytes 534536 | tf_op jit(solution)/shard_map/ppermute | solution.py:765
  204.0 4.9 %collective-permute-start.26 = (f32[2,48,128]{2,1,0:T(8,128)S(1)}, f32[2,48,128]{2,1,0:T(8,128)S(1)}, u32[]{:S(2)}, u32[]{:S(2)}) collective-permute-start(f32[2,48,128]{2,1,0:T(8,128)S(1)} %add.221), channel_id=1, source_target_pairs={{0,4},{1,5},{2,6},{3,7},{4,0},{5,1},{6,2},{7,3},{8,12},{9,13},{10,... | collective-permute-start | bytes 147464 | tf_op jit(solution)/shard_map/ppermute | solution.py:765
  208.9 5.4 %collective-permute-start.30 = (f32[48,128]{1,0:T(8,128)S(1)}, f32[48,128]{1,0:T(8,128)S(1)}, u32[]{:S(2)}, u32[]{:S(2)}) collective-permute-start(f32[48,128]{1,0:T(8,128)S(1)} %dynamic-slice_bitcast_fusion.2), channel_id=1, source_target_pairs={{0,16},{16,0},{1,17},{17,1},{2,18},{18,2},{3,19},{19,3},{4,20},{20... | collective-permute-start | bytes 73736 | tf_op jit(solution)/shard_map/ppermute | solution.py:765
  209.5 7.1 %collective-permute-start.29 = (bf16[464,384]{1,0:T(8,128)(2,1)S(1)}, bf16[464,384]{1,0:T(8,128)(2,1)S(1)}, u32[]{:S(2)}, u32[]{:S(2)}) collective-permute-start(bf16[464,384]{1,0:T(8,128)(2,1)S(1)} %maximum_select_fusion.5), channel_id=1, source_target_pairs={{0,2},{1,3},{2,0},{3,1},{4,6},{5,7},{6,4},{7,5},{8,10},{9,11},{10,... | collective-permute-start | bytes 1069064 | tf_op jit(solution)/shard_map/ppermute | solution.py:765
  211.0 12.6 %collective-permute-start.28 = (bf16[1536,384]{1,0:T(8,128)(2,1)S(1)}, bf16[1536,384]{1,0:T(8,128)(2,1)}, u32[]{:S(2)}, u32[]{:S(2)}) collective-permute-start(bf16[1536,384]{1,0:T(8,128)(2,1)S(1)} %maximum_select_fusion), channel_id=1, source_target_pairs={{0,1},{1,0},{2,3},{3,2},{4,5},{5,4},{6,7},{7,6},{8,9},{9,8},{10,11... | collective-permute-start | bytes 3538952 | tf_op jit(solution)/shard_map/ppermute | solution.py:765
  216.8 6.8 %collective-permute-start.31 = (bf16[928,384]{1,0:T(8,128)(2,1)S(1)}, bf16[928,384]{1,0:T(8,128)(2,1)}, u32[]{:S(2)}, u32[]{:S(2)}) collective-permute-start(bf16[928,384]{1,0:T(8,128)(2,1)S(1)} %maximum_select_fusion.3), channel_id=1, source_target_pairs={{0,1},{1,0},{2,3},{3,2},{4,5},{5,4},{6,7},{7,6},{8,9},{9,8},{10,11... | collective-permute-start | bytes 2138120 | tf_op jit(solution)/shard_map/ppermute | solution.py:765
